TPU v7x, 512 devices: a whole 4x4x16 slice. The times are simulated.
512 devices in a mesh: slab: 16 (over z), energy: 32 (over x, y, core).
Axes of the slice: x: 4, y: 4, z: 16, core: 2. Of those that a mesh axis runs over, the one named last changes fastest.
Arguments:
- green_left: bfloat16 [32, 32, 256, 512], P('energy', 'slab'), may hold values from -1.1 to 1.1
- sigma_lesser: bfloat16 [32, 32, 256, 512], P('energy', 'slab'), may hold values from -2.390625 to 2.390625
- coupling: float32 [32, 32], P('energy', 'slab'), may hold values from 0.56 to 0.99
- energy_weights: float32 [32], replicated, may hold values from 0.05 to 0.3
Outputs:
- lesser: float32 [32, 32, 256, 512], P(None, 'slab', 'energy')
- density: float32 [32, 256, 512], P('slab', 'energy')
All inputs are finite; a program needn't handle non-finite values.
Results may differ from a plain program's by a relative error of at most 0.0003.
Values sent between devices are 32-bit elements; how exact they have to be, the bound alone decides.
No kernel may reach another device: no remote copies, remote signals or barrier semaphores. Data moves between devices by JAX's collectives and lax.ppermute only.
A program may use at most 64 MiB of HBM per device.

v0:
```python
import jax
import jax.numpy as jnp
from jax import lax
from jax.sharding import PartitionSpec as P


def shifted(value, axis, steps):
    count = lax.axis_size(axis)
    initial, last = (max(0, -steps), min(count, count - steps))
    return lax.ppermute(value, axis, [(source, source + steps) for source in range(initial, last)])


def complex_product(first_factor, second_factor):
    orbitals = first_factor.shape[-2]
    real_rows = jnp.einsum(
        "...ij,...jk->...ik",
        first_factor[..., :orbitals],
        second_factor,
        precision=lax.Precision.HIGHEST,
    )
    imag_rows = jnp.einsum(
        "...ij,...jk->...ik",
        first_factor[..., orbitals:],
        second_factor,
        precision=lax.Precision.HIGHEST,
    )
    return jnp.concatenate(
        [
            real_rows[..., :orbitals] - imag_rows[..., orbitals:],
            real_rows[..., orbitals:] + imag_rows[..., :orbitals],
        ],
        axis=-1,
    )


def dagger(matrix):
    orbitals = matrix.shape[-2]
    return jnp.concatenate(
        [
            jnp.swapaxes(matrix[..., :orbitals], -1, -2),
            -jnp.swapaxes(matrix[..., orbitals:], -1, -2),
        ],
        axis=-1,
    )


def congruence(green, middle):
    return complex_product(complex_product(green, middle), dagger(green))


def per_device(green_left, sigma_lesser, coupling, energy_weights):
    green = green_left.astype(jnp.float32)
    sigma = sigma_lesser.astype(jnp.float32)
    squared = coupling * coupling
    local_energies = green.shape[0]
    orbitals = green.shape[2]
    sources = congruence(green, sigma)
    identity_block = jnp.eye(orbitals, dtype=jnp.float32)
    zero_block = jnp.zeros_like(identity_block)
    contact = jnp.broadcast_to(
        jnp.concatenate([zero_block, identity_block], axis=-1),
        (local_energies, orbitals, 2 * orbitals),
    )
    position = lax.axis_index("slab")

    def advance_slab(state_in):
        first_block = sources[:, 0] + squared[:, 0][:, None, None] * congruence(
            green[:, 0], state_in
        )
        second_block = sources[:, 1] + squared[:, 1][:, None, None] * congruence(
            green[:, 1], first_block
        )
        return (second_block, jnp.stack([first_block, second_block], axis=1))

    def retain_buffer(held):
        return (held[1], held[2])

    def pending_partial_labour(held):
        return advance_slab(held[0])

    def turn(turn_index, carry):
        outgoing, result = carry
        received = shifted(outgoing, "slab", 1)
        state_in = jnp.where(position == 0, contact, received)
        return lax.cond(
            turn_index == position,
            pending_partial_labour,
            retain_buffer,
            (state_in, outgoing, result),
        )

    start = (jnp.zeros_like(contact), jnp.zeros_like(sources))
    _, lesser_local = lax.fori_loop(0, lax.axis_size("slab"), turn, start)
    block_rows = lax.all_to_all(lesser_local, "energy", split_axis=2, concat_axis=0, tiled=True)
    summed = jnp.einsum("e,ebrc->brc", energy_weights, block_rows, precision=lax.Precision.HIGHEST)
    integrated = summed[None]
    return (block_rows, integrated[0])


def solution(mesh):
    in_specs = (
        P("energy", "slab", None, None),
        P("energy", "slab", None, None),
        P("energy", "slab"),
        P(),
    )
    out_specs = (P(None, "slab", "energy", None), P("slab", "energy", None))
    return jax.shard_map(
        per_device, mesh=mesh, in_specs=in_specs, out_specs=out_specs, check_vma=False
    )
```

profile of v0, /device:TPU:481, one launch (start us, length us, event | category | flops | bytes accessed | tf_op | source)
XLA Modules:
  0.0 429.5 jit_solution(8364739151299995572)
XLA Ops:
  0.7 1.3 copy.11
  3.9 2.0 convolution_bitcast_fusion.11
  9.3 361.7 %while.16 = (s32[]{:T(128)}, f32[1,256,512]{2,1,0:T(8,128)S(1)}, f32[1,2,256,512]{3,2,1,0:T(8,128)}, s32[]{:T(128)}, f32[1,2,256,512]{3,2,1,0:T(8,128)S(1)}, /*i...) while((s32[]{:T(128)}, f32[1,256,512]{2,1,0:T(8,128)S(1)}, ...), condition=%wide.region_3.4_spmd, body=%wide.region_0.3_spmd.sunk | while | flops 3224109056 | bytes 28836120 | solution.py:93
  10.6 13.4 %collective-permute-done = f32[1,256,512]{2,1,0:T(8,128)S(1)} collective-permute-done((f32[1,256,512]{2,1,0:T(8,128)S(1)}, f32[1,256,512]{2,1,0:T(8,128)S(1)}, u32[]{:S(2)}, u32[]{:S(2)}) %collective-permute-start) | collective-permute-done | bytes 524320 | tf_op jit(solution)/shard_map/while/body/eval_jaxpr/ppermute | solution.py:10
  24.0 1.3 collective-permute-start
  25.3 12.5 %collective-permute-done = f32[1,256,512]{2,1,0:T(8,128)S(1)} collective-permute-done((f32[1,256,512]{2,1,0:T(8,128)S(1)}, f32[1,256,512]{2,1,0:T(8,128)S(1)}, u32[]{:S(2)}, u32[]{:S(2)}) %collective-permute-start) | collective-permute-done | bytes 524320 | tf_op jit(solution)/shard_map/while/body/eval_jaxpr/ppermute | solution.py:10
  37.8 1.3 collective-permute-start
  39.1 11.5 %collective-permute-done = f32[1,256,512]{2,1,0:T(8,128)S(1)} collective-permute-done((f32[1,256,512]{2,1,0:T(8,128)S(1)}, f32[1,256,512]{2,1,0:T(8,128)S(1)}, u32[]{:S(2)}, u32[]{:S(2)}) %collective-permute-start) | collective-permute-done | bytes 524320 | tf_op jit(solution)/shard_map/while/body/eval_jaxpr/ppermute | solution.py:10
  50.6 1.3 collective-permute-start
  51.9 10.6 %collective-permute-done = f32[1,256,512]{2,1,0:T(8,128)S(1)} collective-permute-done((f32[1,256,512]{2,1,0:T(8,128)S(1)}, f32[1,256,512]{2,1,0:T(8,128)S(1)}, u32[]{:S(2)}, u32[]{:S(2)}) %collective-permute-start) | collective-permute-done | bytes 524320 | tf_op jit(solution)/shard_map/while/body/eval_jaxpr/ppermute | solution.py:10
  62.5 1.3 collective-permute-start
  63.8 11.6 %collective-permute-done = f32[1,256,512]{2,1,0:T(8,128)S(1)} collective-permute-done((f32[1,256,512]{2,1,0:T(8,128)S(1)}, f32[1,256,512]{2,1,0:T(8,128)S(1)}, u32[]{:S(2)}, u32[]{:S(2)}) %collective-permute-start) | collective-permute-done | bytes 524320 | tf_op jit(solution)/shard_map/while/body/eval_jaxpr/ppermute | solution.py:10
  75.4 1.3 collective-permute-start
  76.7 10.0 %collective-permute-done = f32[1,256,512]{2,1,0:T(8,128)S(1)} collective-permute-done((f32[1,256,512]{2,1,0:T(8,128)S(1)}, f32[1,256,512]{2,1,0:T(8,128)S(1)}, u32[]{:S(2)}, u32[]{:S(2)}) %collective-permute-start) | collective-permute-done | bytes 524320 | tf_op jit(solution)/shard_map/while/body/eval_jaxpr/ppermute | solution.py:10
  86.7 1.3 collective-permute-start
  88.0 9.0 %collective-permute-done = f32[1,256,512]{2,1,0:T(8,128)S(1)} collective-permute-done((f32[1,256,512]{2,1,0:T(8,128)S(1)}, f32[1,256,512]{2,1,0:T(8,128)S(1)}, u32[]{:S(2)}, u32[]{:S(2)}) %collective-permute-start) | collective-permute-done | bytes 524320 | tf_op jit(solution)/shard_map/while/body/eval_jaxpr/ppermute | solution.py:10
  97.0 1.3 collective-permute-start
  98.3 10.1 %collective-permute-done = f32[1,256,512]{2,1,0:T(8,128)S(1)} collective-permute-done((f32[1,256,512]{2,1,0:T(8,128)S(1)}, f32[1,256,512]{2,1,0:T(8,128)S(1)}, u32[]{:S(2)}, u32[]{:S(2)}) %collective-permute-start) | collective-permute-done | bytes 524320 | tf_op jit(solution)/shard_map/while/body/eval_jaxpr/ppermute | solution.py:10
  108.4 1.3 collective-permute-start
  109.7 11.3 %collective-permute-done = f32[1,256,512]{2,1,0:T(8,128)S(1)} collective-permute-done((f32[1,256,512]{2,1,0:T(8,128)S(1)}, f32[1,256,512]{2,1,0:T(8,128)S(1)}, u32[]{:S(2)}, u32[]{:S(2)}) %collective-permute-start) | collective-permute-done | bytes 524320 | tf_op jit(solution)/shard_map/while/body/eval_jaxpr/ppermute | solution.py:10
  121.0 1.3 collective-permute-start
  122.3 12.6 %collective-permute-done = f32[1,256,512]{2,1,0:T(8,128)S(1)} collective-permute-done((f32[1,256,512]{2,1,0:T(8,128)S(1)}, f32[1,256,512]{2,1,0:T(8,128)S(1)}, u32[]{:S(2)}, u32[]{:S(2)}) %collective-permute-start) | collective-permute-done | bytes 524320 | tf_op jit(solution)/shard_map/while/body/eval_jaxpr/ppermute | solution.py:10
  136.2 14.3 %collective-permute-done = f32[1,256,512]{2,1,0:T(8,128)S(1)} collective-permute-done((f32[1,256,512]{2,1,0:T(8,128)S(1)}, f32[1,256,512]{2,1,0:T(8,128)S(1)}, u32[]{:S(2)}, u32[]{:S(2)}) %collective-permute-start) | collective-permute-done | bytes 524320 | tf_op jit(solution)/shard_map/while/body/eval_jaxpr/ppermute | solution.py:10
  151.8 15.4 %collective-permute-done = f32[1,256,512]{2,1,0:T(8,128)S(1)} collective-permute-done((f32[1,256,512]{2,1,0:T(8,128)S(1)}, f32[1,256,512]{2,1,0:T(8,128)S(1)}, u32[]{:S(2)}, u32[]{:S(2)}) %collective-permute-start) | collective-permute-done | bytes 524320 | tf_op jit(solution)/shard_map/while/body/eval_jaxpr/ppermute | solution.py:10
  167.3 1.3 collective-permute-start
  168.5 16.3 %collective-permute-done = f32[1,256,512]{2,1,0:T(8,128)S(1)} collective-permute-done((f32[1,256,512]{2,1,0:T(8,128)S(1)}, f32[1,256,512]{2,1,0:T(8,128)S(1)}, u32[]{:S(2)}, u32[]{:S(2)}) %collective-permute-start) | collective-permute-done | bytes 524320 | tf_op jit(solution)/shard_map/while/body/eval_jaxpr/ppermute | solution.py:10
  186.2 15.0 %collective-permute-done = f32[1,256,512]{2,1,0:T(8,128)S(1)} collective-permute-done((f32[1,256,512]{2,1,0:T(8,128)S(1)}, f32[1,256,512]{2,1,0:T(8,128)S(1)}, u32[]{:S(2)}, u32[]{:S(2)}) %collective-permute-start) | collective-permute-done | bytes 524320 | tf_op jit(solution)/shard_map/while/body/eval_jaxpr/ppermute | solution.py:10
  202.5 14.4 %collective-permute-done = f32[1,256,512]{2,1,0:T(8,128)S(1)} collective-permute-done((f32[1,256,512]{2,1,0:T(8,128)S(1)}, f32[1,256,512]{2,1,0:T(8,128)S(1)}, u32[]{:S(2)}, u32[]{:S(2)}) %collective-permute-start) | collective-permute-done | bytes 524320 | tf_op jit(solution)/shard_map/while/body/eval_jaxpr/ppermute | solution.py:10
  218.2 139.3 %collective-permute-done = f32[1,256,512]{2,1,0:T(8,128)S(1)} collective-permute-done((f32[1,256,512]{2,1,0:T(8,128)S(1)}, f32[1,256,512]{2,1,0:T(8,128)S(1)}, u32[]{:S(2)}, u32[]{:S(2)}) %collective-permute-start) | collective-permute-done | bytes 524320 | tf_op jit(solution)/shard_map/while/body/eval_jaxpr/ppermute | solution.py:10
  357.5 13.6 %conditional.2 = ((f32[1,256,512]{2,1,0:T(8,128)S(1)}, f32[1,2,256,512]{3,2,1,0:T(8,128)})) conditional(s32[]{:T(128)} %convert_element_type.15, (f32[1,256,512]{2,1,0:T(8,128)S(1)}, f32[1,2,256,512]{3,2,1,0:T(8,128)}) %tuple.60, (f32[1,2,256,512]{3,2,1,0:T(8,128)S(1)}, f32[1,2]{1,0:T(1,128)S(1)}, pred[]{:T(512)}, f32[1,256,512]{2,1,0:T(8,128)S(1)}, ...), branch_computations={%region_1.1_spmd, %region_2.2_spmd} | conditional | flops 3224109056 | bytes 26738742 | solution.py:85
  371.1 2.0 copy.13
  373.1 53.2 %all_to_all.18 = f32[1,2,256,512]{3,1,0,2:T(2,128)S(1)} all-to-all(f32[1,2,256,512]{3,1,0,2:T(2,128)S(1)} %copy.13), channel_id=1, replica_groups=mesh['slab'=16,'energy'=32] {'energy'}, dimensions={2} | all-to-all | bytes 2097152 | tf_op jit(solution)/shard_map/all_to_all | solution.py:94
  (65 shorter events, 29.5 us)
Async XLA Ops:
  0.6 1.4 copy-start
  0.6 1.4 copy-start.2
  5.9 1.9 copy-start.1
  7.1 0.7 copy-start.4
  9.3 14.7 %collective-permute-start = (f32[1,256,512]{2,1,0:T(8,128)S(1)}, f32[1,256,512]{2,1,0:T(8,128)S(1)}, u32[]{:S(2)}, u32[]{:S(2)}) collective-permute-start(f32[1,256,512]{2,1,0:T(8,128)S(1)} %get-tuple-element.352), channel_id=1, source_target_pairs={{0,32},{32,64},{64,96},{96,128},{128,160},{160,192},{192,224},{224... | collective-permute-start | bytes 1572872 | tf_op jit(solution)/shard_map/while/body/eval_jaxpr/ppermute | solution.py:10
  24.0 13.8 %collective-permute-start = (f32[1,256,512]{2,1,0:T(8,128)S(1)}, f32[1,256,512]{2,1,0:T(8,128)S(1)}, u32[]{:S(2)}, u32[]{:S(2)}) collective-permute-start(f32[1,256,512]{2,1,0:T(8,128)S(1)} %get-tuple-element.352), channel_id=1, source_target_pairs={{0,32},{32,64},{64,96},{96,128},{128,160},{160,192},{192,224},{224... | collective-permute-start | bytes 1572872 | tf_op jit(solution)/shard_map/while/body/eval_jaxpr/ppermute | solution.py:10
  37.8 12.8 %collective-permute-start = (f32[1,256,512]{2,1,0:T(8,128)S(1)}, f32[1,256,512]{2,1,0:T(8,128)S(1)}, u32[]{:S(2)}, u32[]{:S(2)}) collective-permute-start(f32[1,256,512]{2,1,0:T(8,128)S(1)} %get-tuple-element.352), channel_id=1, source_target_pairs={{0,32},{32,64},{64,96},{96,128},{128,160},{160,192},{192,224},{224... | collective-permute-start | bytes 1572872 | tf_op jit(solution)/shard_map/while/body/eval_jaxpr/ppermute | solution.py:10
  50.6 11.9 %collective-permute-start = (f32[1,256,512]{2,1,0:T(8,128)S(1)}, f32[1,256,512]{2,1,0:T(8,128)S(1)}, u32[]{:S(2)}, u32[]{:S(2)}) collective-permute-start(f32[1,256,512]{2,1,0:T(8,128)S(1)} %get-tuple-element.352), channel_id=1, source_target_pairs={{0,32},{32,64},{64,96},{96,128},{128,160},{160,192},{192,224},{224... | collective-permute-start | bytes 1572872 | tf_op jit(solution)/shard_map/while/body/eval_jaxpr/ppermute | solution.py:10
  62.5 12.9 %collective-permute-start = (f32[1,256,512]{2,1,0:T(8,128)S(1)}, f32[1,256,512]{2,1,0:T(8,128)S(1)}, u32[]{:S(2)}, u32[]{:S(2)}) collective-permute-start(f32[1,256,512]{2,1,0:T(8,128)S(1)} %get-tuple-element.352), channel_id=1, source_target_pairs={{0,32},{32,64},{64,96},{96,128},{128,160},{160,192},{192,224},{224... | collective-permute-start | bytes 1572872 | tf_op jit(solution)/shard_map/while/body/eval_jaxpr/ppermute | solution.py:10
  75.4 11.3 %collective-permute-start = (f32[1,256,512]{2,1,0:T(8,128)S(1)}, f32[1,256,512]{2,1,0:T(8,128)S(1)}, u32[]{:S(2)}, u32[]{:S(2)}) collective-permute-start(f32[1,256,512]{2,1,0:T(8,128)S(1)} %get-tuple-element.352), channel_id=1, source_target_pairs={{0,32},{32,64},{64,96},{96,128},{128,160},{160,192},{192,224},{224... | collective-permute-start | bytes 1572872 | tf_op jit(solution)/shard_map/while/body/eval_jaxpr/ppermute | solution.py:10
  86.7 10.3 %collective-permute-start = (f32[1,256,512]{2,1,0:T(8,128)S(1)}, f32[1,256,512]{2,1,0:T(8,128)S(1)}, u32[]{:S(2)}, u32[]{:S(2)}) collective-permute-start(f32[1,256,512]{2,1,0:T(8,128)S(1)} %get-tuple-element.352), channel_id=1, source_target_pairs={{0,32},{32,64},{64,96},{96,128},{128,160},{160,192},{192,224},{224... | collective-permute-start | bytes 1572872 | tf_op jit(solution)/shard_map/while/body/eval_jaxpr/ppermute | solution.py:10
  97.0 11.4 %collective-permute-start = (f32[1,256,512]{2,1,0:T(8,128)S(1)}, f32[1,256,512]{2,1,0:T(8,128)S(1)}, u32[]{:S(2)}, u32[]{:S(2)}) collective-permute-start(f32[1,256,512]{2,1,0:T(8,128)S(1)} %get-tuple-element.352), channel_id=1, source_target_pairs={{0,32},{32,64},{64,96},{96,128},{128,160},{160,192},{192,224},{224... | collective-permute-start | bytes 1572872 | tf_op jit(solution)/shard_map/while/body/eval_jaxpr/ppermute | solution.py:10
  108.4 12.6 %collective-permute-start = (f32[1,256,512]{2,1,0:T(8,128)S(1)}, f32[1,256,512]{2,1,0:T(8,128)S(1)}, u32[]{:S(2)}, u32[]{:S(2)}) collective-permute-start(f32[1,256,512]{2,1,0:T(8,128)S(1)} %get-tuple-element.352), channel_id=1, source_target_pairs={{0,32},{32,64},{64,96},{96,128},{128,160},{160,192},{192,224},{224... | collective-permute-start | bytes 1572872 | tf_op jit(solution)/shard_map/while/body/eval_jaxpr/ppermute | solution.py:10
  121.0 13.9 %collective-permute-start = (f32[1,256,512]{2,1,0:T(8,128)S(1)}, f32[1,256,512]{2,1,0:T(8,128)S(1)}, u32[]{:S(2)}, u32[]{:S(2)}) collective-permute-start(f32[1,256,512]{2,1,0:T(8,128)S(1)} %get-tuple-element.352), channel_id=1, source_target_pairs={{0,32},{32,64},{64,96},{96,128},{128,160},{160,192},{192,224},{224... | collective-permute-start | bytes 1572872 | tf_op jit(solution)/shard_map/while/body/eval_jaxpr/ppermute | solution.py:10
  134.9 15.6 %collective-permute-start = (f32[1,256,512]{2,1,0:T(8,128)S(1)}, f32[1,256,512]{2,1,0:T(8,128)S(1)}, u32[]{:S(2)}, u32[]{:S(2)}) collective-permute-start(f32[1,256,512]{2,1,0:T(8,128)S(1)} %get-tuple-element.352), channel_id=1, source_target_pairs={{0,32},{32,64},{64,96},{96,128},{128,160},{160,192},{192,224},{224... | collective-permute-start | bytes 1572872 | tf_op jit(solution)/shard_map/while/body/eval_jaxpr/ppermute | solution.py:10
  150.5 16.7 %collective-permute-start = (f32[1,256,512]{2,1,0:T(8,128)S(1)}, f32[1,256,512]{2,1,0:T(8,128)S(1)}, u32[]{:S(2)}, u32[]{:S(2)}) collective-permute-start(f32[1,256,512]{2,1,0:T(8,128)S(1)} %get-tuple-element.352), channel_id=1, source_target_pairs={{0,32},{32,64},{64,96},{96,128},{128,160},{160,192},{192,224},{224... | collective-permute-start | bytes 1572872 | tf_op jit(solution)/shard_map/while/body/eval_jaxpr/ppermute | solution.py:10
  167.3 17.6 %collective-permute-start = (f32[1,256,512]{2,1,0:T(8,128)S(1)}, f32[1,256,512]{2,1,0:T(8,128)S(1)}, u32[]{:S(2)}, u32[]{:S(2)}) collective-permute-start(f32[1,256,512]{2,1,0:T(8,128)S(1)} %get-tuple-element.352), channel_id=1, source_target_pairs={{0,32},{32,64},{64,96},{96,128},{128,160},{160,192},{192,224},{224... | collective-permute-start | bytes 1572872 | tf_op jit(solution)/shard_map/while/body/eval_jaxpr/ppermute | solution.py:10
  184.9 16.3 %collective-permute-start = (f32[1,256,512]{2,1,0:T(8,128)S(1)}, f32[1,256,512]{2,1,0:T(8,128)S(1)}, u32[]{:S(2)}, u32[]{:S(2)}) collective-permute-start(f32[1,256,512]{2,1,0:T(8,128)S(1)} %get-tuple-element.352), channel_id=1, source_target_pairs={{0,32},{32,64},{64,96},{96,128},{128,160},{160,192},{192,224},{224... | collective-permute-start | bytes 1572872 | tf_op jit(solution)/shard_map/while/body/eval_jaxpr/ppermute | solution.py:10
  201.2 15.7 %collective-permute-start = (f32[1,256,512]{2,1,0:T(8,128)S(1)}, f32[1,256,512]{2,1,0:T(8,128)S(1)}, u32[]{:S(2)}, u32[]{:S(2)}) collective-permute-start(f32[1,256,512]{2,1,0:T(8,128)S(1)} %get-tuple-element.352), channel_id=1, source_target_pairs={{0,32},{32,64},{64,96},{96,128},{128,160},{160,192},{192,224},{224... | collective-permute-start | bytes 1572872 | tf_op jit(solution)/shard_map/while/body/eval_jaxpr/ppermute | solution.py:10
  216.9 140.6 %collective-permute-start = (f32[1,256,512]{2,1,0:T(8,128)S(1)}, f32[1,256,512]{2,1,0:T(8,128)S(1)}, u32[]{:S(2)}, u32[]{:S(2)}) collective-permute-start(f32[1,256,512]{2,1,0:T(8,128)S(1)} %get-tuple-element.352), channel_id=1, source_target_pairs={{0,32},{32,64},{64,96},{96,128},{128,160},{160,192},{192,224},{224... | collective-permute-start | bytes 1572872 | tf_op jit(solution)/shard_map/while/body/eval_jaxpr/ppermute | solution.py:10
  426.5 1.1 copy-start.3
where the time goes:
time: 430 us; the launch traced here: 429 us
  waiting for transfers between devices  327 us (76%)
  blocking collectives  53.2 us (12%)
  starting transfers between devices  20.5 us (5%)
  matrix products  13.2 us (3%)
  local copies, waits for them, and re-layouts  10.2 us (2%)
    ppermute x16, waiting for transfers between devices, shifted(): lax.ppermute(value, axis, [(source, source + steps) for source in range(i...  327 us
    all_to_all x1, blocking collectives, per_device(): lax.all_to_all(lesser_local, 'energy', split_axis=2, concat_axis=0, tiled...  53.2 us
    ppermute x16, starting transfers between devices, shifted(): lax.ppermute(value, axis, [(source, source + steps) for source in range(i...  20.5 us
  transfers between devices with their start and end apart: 16, of which 16 were waited for; matrix products, arithmetic and copies ran while one was open for 0% of the time, Pallas kernels for 0%

commit v1 on v0

v1 whole, which is shorter than its diff:
```python
import functools

import jax
import jax.numpy as jnp
from jax import lax
from jax.experimental import pallas as pl
from jax.experimental.pallas import tpu as pltpu
from jax.sharding import PartitionSpec as P

F32, BF16 = jnp.float32, jnp.bfloat16
GROUPS = (2, 3, 4, 3, 2, 2)
VMEM_BYTES = 40 * 1024 * 1024


def split(value):
    high = value.astype(BF16)
    return high, (value - high.astype(F32)).astype(BF16)


def dot(first, second):
    return jnp.dot(first, second, preferred_element_type=F32)


def expanded(matrix):
    half = matrix.shape[0]
    turned = jnp.concatenate([-matrix[:, half:], matrix[:, :half]], axis=1)
    return jnp.concatenate([matrix, turned], axis=0)


def dagger_form(matrix):
    half = matrix.shape[0]
    real, imag = matrix[:, :half].T, matrix[:, half:].T
    return jnp.concatenate(
        [jnp.concatenate([real, -imag], axis=1), jnp.concatenate([imag, real], axis=1)], axis=0
    )


def product_narrow(green, value):
    high, low = split(value)
    return dot(green, expanded(high)) + dot(green, expanded(low))


def product_wide(first_high, first_low, value):
    high, low = split(value)
    wide = expanded(high)
    return dot(first_high, wide) + dot(first_low, wide) + dot(first_high, expanded(low))


def right_narrow(value, form):
    high, low = split(value)
    return dot(high, form) + dot(low, form)


def right_wide(value, form_high, form_low):
    high, low = split(value)
    return dot(high, form_high) + dot(low, form_high) + dot(high, form_low)


def setup_kernel(
    position, coupling, green, sigma, local, first, joint, high, low, form_high, form_low, form_first
):
    half = green.shape[1]
    lead, follow = coupling[0, 0], coupling[0, 1]
    green_first, green_second = green[0], green[1]
    form = dagger_form(green_first)
    form_first[...] = form
    contact = jnp.where(position[0] == 0, lead * lead, 0.0)
    turned = jnp.concatenate(
        [-green_first[:, half:].astype(F32), green_first[:, :half].astype(F32)], axis=1
    )
    partial = dot(green_first, expanded(sigma[0])) + contact * turned
    first_block = right_narrow(partial, form)
    first[...] = first_block
    middle = sigma[1].astype(F32) + (follow * follow) * first_block
    local[...] = right_narrow(product_narrow(green_second, middle), dagger_form(green_second))
    whole = (lead * follow) * dot(green_second, expanded(green_first))
    joint[...] = whole
    part_high, part_low = split(whole)
    high[...], low[...] = part_high, part_low
    form_high[...], form_low[...] = dagger_form(part_high), dagger_form(part_low)


def hop_kernel(local, high, low, form_high, form_low, state, out):
    partial = product_wide(high[...], low[...], state[...])
    out[...] = local[...] + right_wide(partial, form_high[...], form_low[...])


def skip_kernel(high, low, form_high, form_low, left, right, out, state):
    value = left[...] + right[...]
    state[...] = value
    out[...] = right_wide(
        product_wide(high[...], low[...], value), form_high[...], form_low[...]
    )


def join_kernel(received, joint, whole, high, low, form_high, form_low):
    first_high, first_low = split(received[...])
    product = product_wide(first_high, first_low, joint[...])
    whole[...] = product
    part_high, part_low = split(product)
    high[...], low[...] = part_high, part_low
    form_high[...], form_low[...] = dagger_form(part_high), dagger_form(part_low)


def last_kernel(
    coupling, green, form_first, first, local, high, low, form_high, form_low, state, out
):
    rows = out.shape[2]
    lead = coupling[0, 0]
    value = state[...]
    block = first[...] + (lead * lead) * right_narrow(
        product_narrow(green[0], value), form_first[...]
    )
    out[:, 0] = block.reshape(-1, rows, block.shape[-1])
    block = local[...] + right_wide(
        product_wide(high[...], low[...], value), form_high[...], form_low[...]
    )
    out[:, 1] = block.reshape(-1, rows, block.shape[-1])


def density_kernel(weights, blocks, out):
    total = weights[0] * blocks[0]
    for level in range(1, blocks.shape[0]):
        total = total + weights[level] * blocks[level]
    out[...] = total


VMEM, SMEM = pl.BlockSpec(memory_space=pltpu.VMEM), pl.BlockSpec(memory_space=pltpu.SMEM)


def call(kernel, in_specs, shapes, flops):
    return pl.pallas_call(
        kernel,
        in_specs=in_specs,
        out_specs=jax.tree.map(lambda _: VMEM, shapes),
        out_shape=shapes,
        compiler_params=pltpu.CompilerParams(vmem_limit_bytes=VMEM_BYTES),
        cost_estimate=pl.CostEstimate(flops=flops, bytes_accessed=4 << 20, transcendentals=0),
    )


def plan(sizes):
    groups = len(sizes)
    heads = [sum(sizes[:k]) for k in range(groups)]
    tails = [head + size - 1 for head, size in zip(heads, sizes)]
    arrive = [0] + [sizes[0] + k - 1 for k in range(1, groups)]
    steps = {}

    def move(step, kind, source, target, role):
        steps.setdefault(step, []).append((kind, source, target, role))

    for k in range(groups):
        head, tail, size = heads[k], tails[k], sizes[k]
        middle = 0 < k < groups - 1
        if k == 0:
            for i in range(1, size):
                move(i, "forward", head + i - 1, head + i, "enter")
            move(size, "forward", tail, heads[1], "skip" if groups > 2 else "enter")
        if middle:
            for i in range(1, size):
                move(i, "forward", head + i - 1, head + i, "chain")
                move(i, "backward", tail - i + 1, tail - i, "join")
            own = "forward" if size < arrive[k] + 1 else "extra"
            move(size, own, tail, heads[k + 1], "hold")
            last = k + 1 == groups - 1
            move(arrive[k] + 1, "forward", head, heads[k + 1], "end" if last else "skip")
        if k > 0:
            delay = 1 if middle else 0
            for i in range(1, size):
                role = "enter" if head + i < tail else "keep"
                move(arrive[k] + delay + i, "forward", head + i - 1, head + i, role)
    return [steps[s] for s in sorted(steps)], heads


def member(position, places):
    mask = sum(1 << place for place in set(places))
    return ((jnp.int32(mask) >> position) & 1) == 1


def per_device(green_left, sigma_lesser, coupling, energy_weights):
    green, sigma = green_left[0], sigma_lesser[0]
    half, width = green.shape[1:]
    slabs, levels = lax.axis_size("slab"), lax.axis_size("energy")
    position = lax.axis_index("slab").astype(jnp.int32)
    wide = jax.ShapeDtypeStruct((half, width), F32)
    narrow = jax.ShapeDtypeStruct((half, width), BF16)
    form = jax.ShapeDtypeStruct((width, width), BF16)
    cost = 2 * half * width * width
    assert sum(GROUPS) == slabs

    local, first, joint, high, low, form_high, form_low, form_first = call(
        setup_kernel,
        [SMEM, SMEM, VMEM, VMEM],
        [wide, wide, wide, narrow, narrow, form, form, form],
        9 * cost,
    )(position[None], coupling, green, sigma)
    joint_forms = (high, low, form_high, form_low)
    hop = call(hop_kernel, [VMEM] * 6, wide, 6 * cost)
    skip = call(skip_kernel, [VMEM] * 6, [wide, wide], 6 * cost)
    join = call(join_kernel, [VMEM] * 2, [wide, narrow, narrow, form, form], 3 * cost)

    steps, heads = plan(GROUPS)
    zero = jnp.zeros((half, width), F32)
    outgoing, held, state = local, zero, zero
    whole, whole_forms = joint, joint_forms
    pending = []
    for moves in steps:
        received = {}
        by_kind = {}
        for kind, source, target, role in moves:
            by_kind.setdefault(kind, []).append((source, target, role))
        for kind in ("forward", "extra", "backward"):
            if kind in by_kind:
                pairs = [(source, target) for source, target, _ in by_kind[kind]]
                payload = whole if kind == "backward" else outgoing
                received[kind] = lax.ppermute(payload, "slab", pairs)
        places = {}
        for kind in by_kind:
            for _, target, role in by_kind[kind]:
                places.setdefault(role, []).append(target)
        if pending:
            outgoing = lax.cond(
                member(position, pending),
                lambda _, value: hop(local, *joint_forms, value),
                lambda old, _: old,
                outgoing,
                state,
            )
            pending = []
        if "join" in places:
            whole, *whole_forms = lax.cond(
                member(position, places["join"]),
                lambda value, *_: tuple(join(value, joint)),
                lambda _, *old: old,
                received["backward"],
                whole,
                *whole_forms,
            )
        for kind in by_kind:
            holders = [target for _, target, role in by_kind[kind] if role == "hold"]
            if holders:
                held = jnp.where(member(position, holders), received[kind], held)
        front = received["forward"]
        if "skip" in places:
            outgoing, state = lax.cond(
                member(position, places["skip"]),
                lambda value, kept, *_: tuple(skip(*whole_forms, value, kept)),
                lambda _, __, *old: old,
                front,
                held,
                outgoing,
                state,
            )
            pending = places["skip"]
        if "end" in places:
            outgoing, state = lax.cond(
                member(position, places["end"]),
                lambda value, kept, *_: (hop(local, *joint_forms, value + kept), value + kept),
                lambda _, __, *old: old,
                front,
                held,
                outgoing,
                state,
            )
        chained = places.get("chain", []) + places.get("enter", [])
        if chained:
            outgoing = lax.cond(
                member(position, chained),
                lambda value, _: hop(local, *joint_forms, value),
                lambda _, old: old,
                front,
                outgoing,
            )
        entered = places.get("enter", []) + places.get("keep", [])
        if entered:
            state = jnp.where(member(position, entered), front, state)

    rows = half // levels
    blocks = call(
        last_kernel,
        [SMEM] + [VMEM] * 9,
        jax.ShapeDtypeStruct((levels, 2, rows, width), F32),
        10 * cost,
    )(coupling, green, form_first, first, local, *joint_forms, state)
    block_rows = lax.all_to_all(blocks, "energy", split_axis=0, concat_axis=0, tiled=True)
    density = call(
        density_kernel,
        [SMEM, VMEM],
        jax.ShapeDtypeStruct((2, rows, width), F32),
        2 * half * width,
    )(energy_weights, block_rows)
    return block_rows, density


def solution(mesh):
    in_specs = (
        P("energy", "slab", None, None),
        P("energy", "slab", None, None),
        P("energy", "slab"),
        P(),
    )
    out_specs = (P(None, "slab", "energy", None), P("slab", "energy", None))
    return jax.shard_map(
        per_device, mesh=mesh, in_specs=in_specs, out_specs=out_specs, check_vma=False
    )
```

time: 430 us -> 177 us (0.41)
  waiting for transfers between devices: 327 us -> 99.1 us
  blocking collectives: 53.2 us -> 26.7 us
  matrix products: 13.2 us -> 0 us
  other arithmetic: 3.9 us -> 11 us
  Pallas kernels: 0 us -> 6.48 us
  local copies, waits for them, and re-layouts: 10.2 us -> 14.9 us
    ppermute x16 -> x12, waiting for transfers between devices: 327 us -> 99.1 us  [per_device(): received[kind] = lax.ppermute(payload, 'slab', pairs)]
    all_to_all x1, blocking collectives: 53.2 us -> 26.7 us  [per_device(): lax.all_to_all(blocks, 'energy', split_axis=0, concat_axis=0, tiled=True)]
    dot_general x13 -> x0, matrix products: 13.2 us -> none  [the longest x6 6.46 us: complex_product(): jnp.einsum('...ij,...jk->...ik', first_factor[..., :orbitals], second_fac...]
    select_n x0 -> x7, other arithmetic: none -> 11 us  [the longest x4 7.27 us: per_device(): state = jnp.where(member(position, entered), front, state)]
    cond x0 -> x10, local copies, waits for them, and re-layouts: none -> 10.3 us
    pallas_call x0 -> x3, Pallas kernels: none -> 6.48 us  [the longest x1 2.96 us: per_device(): call(setup_kernel, [SMEM, SMEM, VMEM, VMEM], [wide, wide, wide, narrow, n...]
    ppermute x16 -> x12, starting transfers between devices: 20.5 us -> 17.2 us  [per_device(): received[kind] = lax.ppermute(payload, 'slab', pairs)]
  transfers between devices with their start and end apart: 16 -> 12, of which waited for: 16 -> 1; matrix products, arithmetic and copies ran while one was open for 0% -> 11% of each run, Pallas kernels for 0% -> 0%
where the time goes in v1:
time: 177 us; the launch traced here: 176 us
  waiting for transfers between devices  99.1 us (56%)
  blocking collectives  26.7 us (15%)
  starting transfers between devices  17.2 us (10%)
  local copies, waits for them, and re-layouts  14.9 us (8%)
  other arithmetic  11 us (6%)
  Pallas kernels  6.48 us (4%)
    ppermute x12, waiting for transfers between devices, per_device(): received[kind] = lax.ppermute(payload, 'slab', pairs)  99.1 us
    all_to_all x1, blocking collectives, per_device(): lax.all_to_all(blocks, 'energy', split_axis=0, concat_axis=0, tiled=True)  26.7 us
    ppermute x12, starting transfers between devices, per_device(): received[kind] = lax.ppermute(payload, 'slab', pairs)  17.2 us
    cond x10, local copies, waits for them, and re-layouts  10.3 us
    select_n x4, other arithmetic, per_device(): state = jnp.where(member(position, entered), front, state)  7.27 us
    select_n x3, other arithmetic, per_device(): held = jnp.where(member(position, holders), received[kind], held)  3.75 us
    unnamed x15, local copies, waits for them, and re-layouts  3.72 us
  transfers between devices with their start and end apart: 12, of which 1 were waited for; matrix products, arithmetic and copies ran while one was open for 11% of the time, Pallas kernels for 0%

profile of v1, /device:TPU:481, one launch (start us, length us, event | category | flops | bytes accessed | tf_op | source)
XLA Modules:
  0.0 176.2 jit_solution(14551530638778906900)
XLA Ops:
  1.3 1.0 copy-done
  2.3 1.0 copy-done.4
  3.4 3.0 %shard_map.59 = (f32[256,512]{1,0:T(8,128)S(1)}, f32[256,512]{1,0:T(8,128)S(1)}, f32[256,512]{1,0:T(8,128)}, bf16[256,512]{1,0:T(8,128)(2,1)S(1)}, bf16[256,512]...) custom-call(s32[1]{0:T(128)} %bitcast.1.position, ...), custom_call_target="tpu_custom_call" | custom-call | flops 1207959552 | bytes 4194304 | tf_op jit(solution)/shard_map/pallas_call | solution.py:191
  6.3 1.4 collective-permute-start.1
  7.8 1.5 collective-permute-start
  9.2 4.2 %conditional.19 = ((f32[256,512]{1,0:T(8,128)}, bf16[256,512]{1,0:T(8,128)(2,1)}, bf16[256,512]{1,0:T(8,128)(2,1)S(1)}, bf16[512,512]{1,0:T(8,128)(2,1)}, bf16[512,512]{1,0:T(8,128)(2,1)})) conditional(s32[]{:T(128)} %convert_element_type.52, (f32[256,512]{1,0:T(8,128)}, bf16[256,512]{1,0:T(8,128)(2,1)S(1)}, bf16[256,512]{1,0:T(8,128)(2,1)S(1)}, ...), branch_computations={%region_2.0_spmd, %region_3.0_spmd} | conditional | flops 402653184 | bytes 4194352 | solution.py:231
  10.8 1.9 %copy.8 = f32[256,512]{1,0:T(8,128)} copy(f32[256,512]{1,0:T(8,128)} %get-tuple-element.499) | data formatting | bytes 1048576 | tf_op jit(solution)/shard_map/cond
  13.4 1.4 collective-permute-start.2
  15.7 1.4 collective-permute-start.3
  18.0 1.4 collective-permute-start.4
  20.3 1.9 %conditional.21 = (f32[256,512]{1,0:T(8,128)}, f32[256,512]{1,0:T(8,128)}) conditional(s32[]{:T(128)} %convert_element_type.49, (s32[]{:T(128)}, f32[256,512]{1,0:T(8,128)}, f32[256,512]{1,0:T(8,128)}, f32[256,512]{1,0:T(8,128)}) %tuple.147, (bf16[256,512]{1,0:T(8,128)(2,1)}, bf16[256,512]{1,0:T(8,128)(2,1)S(1)}, bf16[512,512]{1,0:T(8,128)(2,1)}, ...), branch_computations={%region_6.7_spmd, %region_7.8_spmd} | conditional | flops 805306368 | bytes 4194320 | solution.py:245
  20.3 1.9 %broadcast_select_fusion = f32[256,512]{1,0:T(8,128)} fusion(f32[256,512]{1,0:T(8,128)} %get-tuple-element.339, f32[256,512]{1,0:T(8,128)} %get-tuple-element.340, pred[]{:T(512)S(6)} %eq.7), kind=kLoop, calls=%fused_computation | loop fusion | flops 131072 | bytes 1572865 | tf_op jit(solution)/shard_map/jit(_where)/select_n | solution.py:276
  22.2 1.5 collective-permute-start.5
  23.6 1.5 collective-permute-start.6
  25.1 1.9 %conditional.23 = (f32[256,512]{1,0:T(8,128)}) conditional(s32[]{:T(128)} %convert_element_type.49, f32[256,512]{1,0:T(8,128)} %get-tuple-element.554, (f32[256,512]{1,0:T(8,128)S(1)}, bf16[256,512]{1,0:T(8,128)(2,1)S(1)}, bf16[256,512]{1,0:T(8,128)(2,1)S(1)}, bf16[512,512]{1,0:T(8,128)(2,1)S(1)}, bf16[512,512]{1,0:T(8,128)(2,1)S(1)}, ...), branch_computations={%region_10.11_spmd, %region_11.12_spmd} | conditional | flops 805306368 | bytes 4194312 | solution.py:222
  25.1 1.9 %copy.34 = f32[256,512]{1,0:T(8,128)} copy(f32[256,512]{1,0:T(8,128)} %param.10) | data formatting | bytes 1048576 | tf_op jit(solution)/shard_map/cond
  27.0 1.0 select_select_fusion.1
  28.0 1.4 collective-permute-start.8
  29.4 1.4 collective-permute-start.7
  30.9 1.9 %conditional.27 = (f32[256,512]{1,0:T(8,128)}) conditional(s32[]{:T(128)} %convert_element_type.48, f32[256,512]{1,0:T(8,128)} %get-tuple-element.558, (f32[256,512]{1,0:T(8,128)S(1)}, bf16[256,512]{1,0:T(8,128)(2,1)S(1)}, bf16[256,512]{1,0:T(8,128)(2,1)S(1)}, bf16[512,512]{1,0:T(8,128)(2,1)S(1)}, bf16[512,512]{1,0:T(8,128)(2,1)S(1)}, ...), branch_computations={%region_18.19_spmd, %region_19.20_spmd} | conditional | flops 805306368 | bytes 4194312 | solution.py:222
  30.9 1.9 %copy.50 = f32[256,512]{1,0:T(8,128)} copy(f32[256,512]{1,0:T(8,128)} %param.18) | data formatting | bytes 1048576 | tf_op jit(solution)/shard_map/cond
  32.8 1.9 %broadcast_select_fusion.3 = f32[256,512]{1,0:T(8,128)} fusion(f32[256,512]{1,0:T(8,128)} %collective-permute-done.8, f32[256,512]{1,0:T(8,128)} %select_select_fusion.1, pred[]{:T(512)S(6)} %eq.66), kind=kLoop, calls=%fused_computation.5 | loop fusion | flops 131072 | bytes 1572865 | tf_op jit(solution)/shard_map/jit(_where)/select_n | solution.py:242
  34.7 1.4 collective-permute-start.9
  36.1 2.0 %broadcast_select_fusion.2 = f32[256,512]{1,0:T(8,128)} fusion(f32[256,512]{1,0:T(8,128)} %collective-permute-done.7, f32[256,512]{1,0:T(8,128)} %get-tuple-element.494, pred[]{:T(512)S(6)} %eq.65), kind=kLoop, calls=%fused_computation.4 | loop fusion | flops 131072 | bytes 1572865 | tf_op jit(solution)/shard_map/jit(_where)/select_n | solution.py:276
  38.9 1.5 collective-permute-start.10
  40.4 2.0 %broadcast_select_fusion.4 = f32[256,512]{1,0:T(8,128)} fusion(f32[256,512]{1,0:T(8,128)} %collective-permute-done.9, f32[256,512]{1,0:T(8,128)} %get-tuple-element.495, pred[]{:T(512)S(6)} %eq.64), kind=kLoop, calls=%fused_computation.6 | loop fusion | flops 131072 | bytes 1572865 | tf_op jit(solution)/shard_map/jit(_where)/select_n | solution.py:276
  43.2 1.3 collective-permute-start.11
  44.5 99.1 %collective-permute-done.11 = f32[256,512]{1,0:T(8,128)} collective-permute-done((f32[256,512]{1,0:T(8,128)}, f32[256,512]{1,0:T(8,128)}, u32[]{:S(2)}, u32[]{:S(2)}) %collective-permute-start.11) | collective-permute-done | bytes 524320 | tf_op jit(solution)/shard_map/ppermute | solution.py:216
  143.6 1.4 select_select_fusion.state
  145.0 2.3 %shard_map.60 = f32[32,2,8,512]{3,2,1,0:T(8,128)S(1)} custom-call(f32[1,2]{1,0:T(1,128)S(1)} %copy-done.3, bf16[2,256,512]{2,1,0:T(8,128)(2,1)S(1)} %bitcast.4, bf16[512,512]{1,0:T(8,128)(2,1)S(1)} %get-tuple-element.471.form_first, f32[256,512]{1,0:T(8,128)S(1)} %get-tuple-element.472.first, f32[256,512]{1,0:T(8,128)S(1)} %get-tuple-element.473.local, ...), custom_call_target="tpu_custom_call" | custom-call | flops 1342177280 | bytes 4194304 | tf_op jit(solution)/shard_map/pallas_call | solution.py:279
  147.3 26.7 %all_to_all.5.blocks = f32[32,2,8,512]{3,2,1,0:T(8,128)S(1)} all-to-all(f32[32,2,8,512]{3,2,1,0:T(8,128)S(1)} %shard_map.60), channel_id=1, replica_groups=mesh['slab'=16,'energy'=32] {'energy'}, dimensions={0} | all-to-all | bytes 2097152 | tf_op jit(solution)/shard_map/all_to_all | solution.py:285
  174.0 1.2 shard_map.61
  (47 shorter events, 10.4 us)
Async XLA Ops:
  0.6 0.7 copy-start.3
  1.3 1.0 copy-start
  2.3 1.0 copy-start.4
  6.3 2.9 %collective-permute-start.1 = (f32[256,512]{1,0:T(8,128)}, f32[256,512]{1,0:T(8,128)}, u32[]{:S(2)}, u32[]{:S(2)}) collective-permute-start(f32[256,512]{1,0:T(8,128)} %get-tuple-element.478), channel_id=1, source_target_pairs={{128,96},{256,224},{352,320},{416,384},{129,97},{257,225},{353,321... | collective-permute-start | bytes 1572872 | tf_op jit(solution)/shard_map/ppermute | solution.py:216
  7.8 7.1 %collective-permute-start = (f32[256,512]{1,0:T(8,128)S(1)}, f32[256,512]{1,0:T(8,128)}, u32[]{:S(2)}, u32[]{:S(2)}) collective-permute-start(f32[256,512]{1,0:T(8,128)S(1)} %get-tuple-element.473.local), channel_id=1, source_target_pairs={{0,32},{64,96},{160,192},{288,320},{384,416},{1,33},{65,97},{161,1... | collective-permute-start | bytes 1572872 | tf_op jit(solution)/shard_map/ppermute | solution.py:216
  13.4 4.5 %collective-permute-start.2 = (f32[256,512]{1,0:T(8,128)}, f32[256,512]{1,0:T(8,128)}, u32[]{:S(2)}, u32[]{:S(2)}) collective-permute-start(f32[256,512]{1,0:T(8,128)} %get-tuple-element.479), channel_id=1, source_target_pairs={{96,64},{224,192},{320,288},{97,65},{225,193},{321,289},{98,66},{2... | collective-permute-start | bytes 1572872 | tf_op jit(solution)/shard_map/ppermute | solution.py:216
  15.7 3.8 %collective-permute-start.3 = (f32[256,512]{1,0:T(8,128)}, f32[256,512]{1,0:T(8,128)}, u32[]{:S(2)}, u32[]{:S(2)}) collective-permute-start(f32[256,512]{1,0:T(8,128)} %get-tuple-element.551), channel_id=1, source_target_pairs={{32,64},{96,128},{192,224},{320,352},{416,448},{33,65},{97,129},{1... | collective-permute-start | bytes 1572872 | tf_op jit(solution)/shard_map/ppermute | solution.py:216
  18.0 9.0 %collective-permute-start.4 = (f32[256,512]{1,0:T(8,128)}, f32[256,512]{1,0:T(8,128)}, u32[]{:S(2)}, u32[]{:S(2)}) collective-permute-start(f32[256,512]{1,0:T(8,128)} %get-tuple-element.486), channel_id=1, source_target_pairs={{192,160},{193,161},{194,162},{195,163},{196,164},{197,165},{198,1... | collective-permute-start | bytes 1572872 | tf_op jit(solution)/shard_map/ppermute | solution.py:216
  22.2 4.8 %collective-permute-start.5 = (f32[256,512]{1,0:T(8,128)}, f32[256,512]{1,0:T(8,128)}, u32[]{:S(2)}, u32[]{:S(2)}) collective-permute-start(f32[256,512]{1,0:T(8,128)} %get-tuple-element.554), channel_id=1, source_target_pairs={{64,160},{224,256},{352,384},{65,161},{225,257},{353,385},{66,162}... | collective-permute-start | bytes 1572872 | tf_op jit(solution)/shard_map/ppermute | solution.py:216
  23.6 3.4 %collective-permute-start.6 = (f32[256,512]{1,0:T(8,128)}, f32[256,512]{1,0:T(8,128)}, u32[]{:S(2)}, u32[]{:S(2)}) collective-permute-start(f32[256,512]{1,0:T(8,128)} %get-tuple-element.554), channel_id=1, source_target_pairs={{128,160},{129,161},{130,162},{131,163},{132,164},{133,165},{134,1... | collective-permute-start | bytes 1572872 | tf_op jit(solution)/shard_map/ppermute | solution.py:216
  28.0 4.8 %collective-permute-start.8 = (f32[256,512]{1,0:T(8,128)}, f32[256,512]{1,0:T(8,128)}, u32[]{:S(2)}, u32[]{:S(2)}) collective-permute-start(f32[256,512]{1,0:T(8,128)} %get-tuple-element.558), channel_id=1, source_target_pairs={{256,288},{257,289},{258,290},{259,291},{260,292},{261,293},{262,2... | collective-permute-start | bytes 1572872 | tf_op jit(solution)/shard_map/ppermute | solution.py:216
  29.4 5.2 %collective-permute-start.7 = (f32[256,512]{1,0:T(8,128)}, f32[256,512]{1,0:T(8,128)}, u32[]{:S(2)}, u32[]{:S(2)}) collective-permute-start(f32[256,512]{1,0:T(8,128)} %get-tuple-element.558), channel_id=1, source_target_pairs={{64,96},{160,288},{65,97},{161,289},{66,98},{162,290},{67,99},{163... | collective-permute-start | bytes 1572872 | tf_op jit(solution)/shard_map/ppermute | solution.py:216
  34.7 4.2 %collective-permute-start.9 = (f32[256,512]{1,0:T(8,128)}, f32[256,512]{1,0:T(8,128)}, u32[]{:S(2)}, u32[]{:S(2)}) collective-permute-start(f32[256,512]{1,0:T(8,128)} %get-tuple-element.561), channel_id=1, source_target_pairs={{96,128},{160,192},{288,384},{97,129},{161,193},{289,385},{98,130}... | collective-permute-start | bytes 1572872 | tf_op jit(solution)/shard_map/ppermute | solution.py:216
  36.1 2.0 %copy-start.6 = (f32[256,512]{1,0:T(8,128)S(1)}, f32[256,512]{1,0:T(8,128)}, u32[]{:S(2)}) copy-start(f32[256,512]{1,0:T(8,128)} %get-tuple-element.561) | copy-start | bytes 1572868
  38.9 4.2 %collective-permute-start.10 = (f32[256,512]{1,0:T(8,128)}, f32[256,512]{1,0:T(8,128)}, u32[]{:S(2)}, u32[]{:S(2)}) collective-permute-start(f32[256,512]{1,0:T(8,128)} %get-tuple-element.564), channel_id=1, source_target_pairs={{192,224},{288,320},{384,448},{193,225},{289,321},{385,449},{194,2... | collective-permute-start | bytes 1572872 | tf_op jit(solution)/shard_map/ppermute | solution.py:216
  40.4 2.0 %copy-start.7 = (f32[256,512]{1,0:T(8,128)S(1)}, f32[256,512]{1,0:T(8,128)}, u32[]{:S(2)}) copy-start(f32[256,512]{1,0:T(8,128)} %get-tuple-element.564) | copy-start | bytes 1572868
  43.2 100.4 %collective-permute-start.11 = (f32[256,512]{1,0:T(8,128)}, f32[256,512]{1,0:T(8,128)}, u32[]{:S(2)}, u32[]{:S(2)}) collective-permute-start(f32[256,512]{1,0:T(8,128)} %get-tuple-element.567), channel_id=1, source_target_pairs={{224,256},{320,352},{384,416},{448,480},{225,257},{321,353},{385,4... | collective-permute-start | bytes 1572872 | tf_op jit(solution)/shard_map/ppermute | solution.py:216
  143.6 1.4 copy-start.1
  147.3 26.8 %copy-start.2 = (f32[32]{0:T(128)S(1)}, f32[32]{0:T(128)}, u32[]{:S(2)}) copy-start(f32[32]{0:T(128)} %weights.1) | copy-start | bytes 388

commit v2 on v1

--- a/solution.py
+++ b/solution.py
@@ -80,26 +80,87 @@
     form_high[...], form_low[...] = dagger_form(part_high), dagger_form(part_low)
 
 
-def hop_kernel(local, high, low, form_high, form_low, state, out):
-    partial = product_wide(high[...], low[...], state[...])
-    out[...] = local[...] + right_wide(partial, form_high[...], form_low[...])
-
-
-def skip_kernel(high, low, form_high, form_low, left, right, out, state):
-    value = left[...] + right[...]
-    state[...] = value
-    out[...] = right_wide(
-        product_wide(high[...], low[...], value), form_high[...], form_low[...]
-    )
-
-
-def join_kernel(received, joint, whole, high, low, form_high, form_low):
-    first_high, first_low = split(received[...])
-    product = product_wide(first_high, first_low, joint[...])
-    whole[...] = product
-    part_high, part_low = split(product)
-    high[...], low[...] = part_high, part_low
-    form_high[...], form_low[...] = dagger_form(part_high), dagger_form(part_low)
+def sandwich(high, low, form_high, form_low, value):
+    partial = product_wide(high[...], low[...], value)
+    return right_wide(partial, form_high[...], form_low[...])
+
+
+def takes_part(places):
+    mask = sum(1 << place for place in set(places))
+    position = lax.axis_index("slab").astype(jnp.int32)
+    return ((jnp.int32(mask) >> position) & 1) == 1
+
+
+def step_kernel(roles, names, *refs):
+    ref = dict(zip(names, refs))
+    forms = [ref.get(name) for name in ("high", "low", "form_high", "form_low")]
+    whole_forms = [ref.get("whole_" + name) for name in ("high", "low", "form_high", "form_low")]
+
+    def hold(source):
+        def body():
+            ref["held_out"][...] = ref[source][...]
+
+        return body
+
+    for source in ("front", "extra"):
+        if roles.get("hold_" + source):
+            pl.when(takes_part(roles["hold_" + source]))(hold(source))
+    arriving = roles["enter"] + roles["keep"] + roles["lead"]
+    if "state" not in ref:
+
+        @pl.when(jnp.logical_not(takes_part(arriving)))
+        def _():
+            ref["state_out"][...] = jnp.zeros_like(ref["state_out"])
+
+    if arriving:
+
+        @pl.when(takes_part(arriving))
+        def _():
+            ref["state_out"][...] = ref["front"][...]
+
+    joined = roles["skip"] + roles["end"]
+    if joined:
+
+        @pl.when(takes_part(joined))
+        def _():
+            ref["state_out"][...] = ref["front"][...] + ref["held_out"][...]
+
+    onward = roles["enter"] + roles["end"]
+    if onward:
+
+        @pl.when(takes_part(onward))
+        def _():
+            ref["out"][...] = ref["local"][...] + sandwich(*forms, ref["state_out"][...])
+
+    beyond = roles["skip"] + roles["lead"]
+    if beyond:
+
+        @pl.when(takes_part(beyond))
+        def _():
+            ref["out"][...] = sandwich(*whole_forms, ref["state_out"][...])
+
+
+def after_kernel(places, local, high, low, form_high, form_low, state, out):
+    @pl.when(takes_part(places))
+    def _():
+        out[...] = local[...] + sandwich(high, low, form_high, form_low, state[...])
+
+
+def join_kernel(places, heads, received, joint, *rest):
+    product, high, low, form_high, form_low = rest[-5:]
+
+    @pl.when(takes_part(places))
+    def _():
+        first_high, first_low = split(received[...])
+        product[...] = product_wide(first_high, first_low, joint[...])
+
+    if heads:
+
+        @pl.when(takes_part(heads))
+        def _():
+            part_high, part_low = split(product[...])
+            high[...], low[...] = part_high, part_low
+            form_high[...], form_low[...] = dagger_form(part_high), dagger_form(part_low)
 
 
 def last_kernel(
@@ -128,12 +189,13 @@
 VMEM, SMEM = pl.BlockSpec(memory_space=pltpu.VMEM), pl.BlockSpec(memory_space=pltpu.SMEM)
 
 
-def call(kernel, in_specs, shapes, flops):
+def call(kernel, in_specs, shapes, flops, aliases=None):
     return pl.pallas_call(
         kernel,
         in_specs=in_specs,
         out_specs=jax.tree.map(lambda _: VMEM, shapes),
         out_shape=shapes,
+        input_output_aliases=aliases or {},
         compiler_params=pltpu.CompilerParams(vmem_limit_bytes=VMEM_BYTES),
         cost_estimate=pl.CostEstimate(flops=flops, bytes_accessed=4 << 20, transcendentals=0),
     )
@@ -155,10 +217,10 @@
         if k == 0:
             for i in range(1, size):
                 move(i, "forward", head + i - 1, head + i, "enter")
-            move(size, "forward", tail, heads[1], "skip" if groups > 2 else "enter")
+            move(size, "forward", tail, heads[1], "lead" if groups > 2 else "enter")
         if middle:
             for i in range(1, size):
-                move(i, "forward", head + i - 1, head + i, "chain")
+                move(i, "forward", head + i - 1, head + i, "enter")
                 move(i, "backward", tail - i + 1, tail - i, "join")
             own = "forward" if size < arrive[k] + 1 else "extra"
             move(size, own, tail, heads[k + 1], "hold")
@@ -172,11 +234,6 @@
     return [steps[s] for s in sorted(steps)], heads
 
 
-def member(position, places):
-    mask = sum(1 << place for place in set(places))
-    return ((jnp.int32(mask) >> position) & 1) == 1
-
-
 def per_device(green_left, sigma_lesser, coupling, energy_weights):
     green, sigma = green_left[0], sigma_lesser[0]
     half, width = green.shape[1:]
@@ -195,85 +252,83 @@
         9 * cost,
     )(position[None], coupling, green, sigma)
     joint_forms = (high, low, form_high, form_low)
-    hop = call(hop_kernel, [VMEM] * 6, wide, 6 * cost)
-    skip = call(skip_kernel, [VMEM] * 6, [wide, wide], 6 * cost)
-    join = call(join_kernel, [VMEM] * 2, [wide, narrow, narrow, form, form], 3 * cost)
-
     steps, heads = plan(GROUPS)
-    zero = jnp.zeros((half, width), F32)
-    outgoing, held, state = local, zero, zero
-    whole, whole_forms = joint, joint_forms
-    pending = []
+    shared = {"local": local, "high": high, "low": low, "form_high": form_high, "form_low": form_low}
+    joint_forms = (high, low, form_high, form_low)
+    outgoing, product, held, state, whole_forms, posted = local, joint, None, None, None, ()
     for moves in steps:
-        received = {}
         by_kind = {}
         for kind, source, target, role in moves:
             by_kind.setdefault(kind, []).append((source, target, role))
-        for kind in ("forward", "extra", "backward"):
-            if kind in by_kind:
-                pairs = [(source, target) for source, target, _ in by_kind[kind]]
-                payload = whole if kind == "backward" else outgoing
-                received[kind] = lax.ppermute(payload, "slab", pairs)
-        places = {}
-        for kind in by_kind:
-            for _, target, role in by_kind[kind]:
-                places.setdefault(role, []).append(target)
-        if pending:
-            outgoing = lax.cond(
-                member(position, pending),
-                lambda _, value: hop(local, *joint_forms, value),
-                lambda old, _: old,
-                outgoing,
-                state,
+        received = {
+            kind: lax.ppermute(
+                product if kind == "backward" else outgoing,
+                "slab",
+                [(source, target) for source, target, _ in by_kind[kind]],
             )
-            pending = []
-        if "join" in places:
-            whole, *whole_forms = lax.cond(
-                member(position, places["join"]),
-                lambda value, *_: tuple(join(value, joint)),
-                lambda _, *old: old,
-                received["backward"],
-                whole,
-                *whole_forms,
-            )
-        for kind in by_kind:
-            holders = [target for _, target, role in by_kind[kind] if role == "hold"]
-            if holders:
-                held = jnp.where(member(position, holders), received[kind], held)
-        front = received["forward"]
-        if "skip" in places:
-            outgoing, state = lax.cond(
-                member(position, places["skip"]),
-                lambda value, kept, *_: tuple(skip(*whole_forms, value, kept)),
-                lambda _, __, *old: old,
-                front,
-                held,
-                outgoing,
-                state,
-            )
-            pending = places["skip"]
-        if "end" in places:
-            outgoing, state = lax.cond(
-                member(position, places["end"]),
-                lambda value, kept, *_: (hop(local, *joint_forms, value + kept), value + kept),
-                lambda _, __, *old: old,
-                front,
-                held,
-                outgoing,
-                state,
-            )
-        chained = places.get("chain", []) + places.get("enter", [])
-        if chained:
-            outgoing = lax.cond(
-                member(position, chained),
-                lambda value, _: hop(local, *joint_forms, value),
-                lambda _, old: old,
-                front,
-                outgoing,
-            )
-        entered = places.get("enter", []) + places.get("keep", [])
-        if entered:
-            state = jnp.where(member(position, entered), front, state)
+            for kind in ("forward", "extra", "backward")
+            if kind in by_kind
+        }
+        after = None
+        if posted:
+            after = call(
+                functools.partial(after_kernel, posted), [VMEM] * 6, wide, 6 * cost
+            )(local, *joint_forms, state)
+
+        if "backward" in received:
+            places = [target for _, target, _ in by_kind["backward"]]
+            ready = [place for place in places if place in heads]
+            kept = tuple(whole_forms) if whole_forms else ()
+            product, *whole_forms = call(
+                functools.partial(join_kernel, places, ready),
+                [VMEM] * (2 + len(kept)),
+                [wide, narrow, narrow, form, form],
+                3 * cost,
+                {2 + i: 1 + i for i in range(len(kept))},
+            )(received["backward"], joint, *kept)
+
+        roles = {}
+        for role in ("enter", "keep", "lead", "skip", "end"):
+            roles[role] = [target for _, target, name in by_kind["forward"] if name == role]
+        for source, kind in (("front", "forward"), ("extra", "extra")):
+            roles["hold_" + source] = [
+                target for _, target, name in by_kind.get(kind, []) if name == "hold"
+            ]
+        holding = bool(roles["hold_front"] or roles["hold_extra"])
+        joining = bool(roles["skip"] or roles["end"])
+        inputs = {"front": received["forward"]}
+        if "extra" in received:
+            inputs["extra"] = received["extra"]
+        if roles["enter"] or roles["end"]:
+            inputs.update(shared)
+        beyond = roles["skip"] + roles["lead"]
+        if beyond:
+            for name, value in zip(("high", "low", "form_high", "form_low"), whole_forms):
+                inputs["whole_" + name] = value
+        outputs = ["out", "state_out"]
+        aliases = {}
+        if state is not None:
+            aliases[len(inputs)] = 1
+            inputs["state"] = state
+        if holding or joining:
+            if held is not None:
+                aliases[len(inputs)] = 2
+                inputs["held"] = held
+            outputs.append("held_out")
+        if after is not None:
+            aliases[len(inputs)] = 0
+            inputs["after"] = after
+        results = call(
+            functools.partial(step_kernel, roles, tuple(inputs) + tuple(outputs)),
+            [VMEM] * len(inputs),
+            [wide] * len(outputs),
+            6 * cost,
+            aliases,
+        )(*inputs.values())
+        outgoing, state = results[:2]
+        if holding or joining:
+            held = results[2]
+        posted = [place for place in beyond if place + 1 not in heads]
 
     rows = half // levels
     blocks = call(

time: 177 us -> 152 us (0.86)
  other arithmetic: 11 us -> 0 us
  local copies, waits for them, and re-layouts: 14.9 us -> 4.11 us
  starting transfers between devices: 17.2 us -> 8.92 us
  waiting for transfers between devices: 99.1 us -> 102 us
    select_n x7 -> x0, other arithmetic: 11 us -> none  [the longest x4 7.27 us: per_device(): state = jnp.where(member(position, entered), front, state)]
    cond x10 -> x0, local copies, waits for them, and re-layouts: 10.3 us -> none
    ppermute x12, starting transfers between devices: 17.2 us -> 8.92 us  [per_device(): lax.ppermute(product if kind == 'backward' else outgoing, 'slab', [(sourc...]
    ppermute x12, waiting for transfers between devices: 99.1 us -> 102 us  [per_device(): lax.ppermute(product if kind == 'backward' else outgoing, 'slab', [(sourc...]
    pallas_call x0 -> x14, Pallas kernels: none -> 2.14 us  [the longest x7 1.21 us: per_device(): call(functools.partial(step_kernel, roles, tuple(inputs) + tuple(outputs)...]
    unnamed x15 -> x11, local copies, waits for them, and re-layouts: 3.72 us -> 4.11 us
  transfers between devices with their start and end apart: 12 -> 12, of which waited for: 1 -> 1; matrix products, arithmetic and copies ran while one was open for 11% -> 0% of each run, Pallas kernels for 0% -> 1%
where the time goes in v2:
time: 152 us
  waiting for transfers between devices  102 us (67%)
  blocking collectives  27.7 us (18%)
  starting transfers between devices  8.92 us (6%)
  Pallas kernels  7.94 us (5%)
  local copies, waits for them, and re-layouts  4.11 us (3%)
    ppermute x12, waiting for transfers between devices, per_device(): lax.ppermute(product if kind == 'backward' else outgoing, 'slab', [(sourc...  102 us
    all_to_all x1, blocking collectives, per_device(): lax.all_to_all(blocks, 'energy', split_axis=0, concat_axis=0, tiled=True)  27.7 us
    ppermute x12, starting transfers between devices, per_device(): lax.ppermute(product if kind == 'backward' else outgoing, 'slab', [(sourc...  8.92 us
    unnamed x11, local copies, waits for them, and re-layouts  4.11 us
  transfers between devices with their start and end apart: 12, of which 1 were waited for; matrix products, arithmetic and copies ran while one was open for 0% of the time, Pallas kernels for 1%

profile of v2, /device:TPU:481, one launch (start us, length us, event | category | flops | bytes accessed | tf_op | source)
XLA Modules:
  0.0 151.6 jit_solution(3380778496120771973)
XLA Ops:
  0.6 0.6 copy-done.3
  1.3 1.0 copy-done
  2.3 1.0 copy-done.4
  3.4 2.3 %shard_map.59 = (f32[256,512]{1,0:T(8,128)S(1)}, f32[256,512]{1,0:T(8,128)S(1)}, f32[256,512]{1,0:T(8,128)S(1)}, bf16[256,512]{1,0:T(8,128)(2,1)S(1)}, bf16[256,...) custom-call(s32[1]{0:T(128)} %bitcast.1.position, ...), custom_call_target="tpu_custom_call" | custom-call | flops 1207959552 | bytes 4194304 | tf_op jit(solution)/shard_map/pallas_call | solution.py:248
  5.7 0.7 collective-permute-start.2
  6.4 0.7 collective-permute-start
  7.1 0.7 collective-permute-start.3
  7.8 0.1 shard_map.60
  7.9 0.7 collective-permute-start.1
  8.6 0.0 collective-permute-done.3.received
  8.7 0.7 collective-permute-start.6
  9.4 0.7 collective-permute-start.4
  10.1 0.7 collective-permute-start.5
  10.9 0.8 shard_map.64
  11.7 0.0 collective-permute-done.5.refs_1_
  11.7 0.7 collective-permute-start.7
  12.4 0.7 collective-permute-start.8
  13.1 0.0 collective-permute-done.7.refs_0_
  13.2 0.7 collective-permute-start.9
  13.9 0.0 collective-permute-done.9.refs_0_
  13.9 0.2 shard_map.70
  14.1 0.7 collective-permute-start.10
  14.9 0.0 collective-permute-done.10.refs_0_
  14.9 1.3 collective-permute-start.11
  16.2 102.0 %collective-permute-done.11.refs_0_ = f32[256,512]{1,0:T(8,128)S(1)} collective-permute-done((f32[256,512]{1,0:T(8,128)S(1)}, f32[256,512]{1,0:T(8,128)S(1)}, u32[]{:S(2)}, u32[]{:S(2)}) %collective-permute-start.11) | collective-permute-done | bytes 524320 | tf_op jit(solution)/shard_map/ppermute | solution.py:264
  118.2 0.8 shard_map.73
  119.0 0.4 copy-done.1
  119.4 2.2 %shard_map.74 = f32[32,2,8,512]{3,2,1,0:T(8,128)S(1)} custom-call(f32[1,2]{1,0:T(1,128)S(1)} %copy-done.3, bf16[2,256,512]{2,1,0:T(8,128)(2,1)S(1)} %bitcast.4, bf16[512,512]{1,0:T(8,128)(2,1)S(1)} %get-tuple-element.41.form_first, f32[256,512]{1,0:T(8,128)S(1)} %get-tuple-element.42.first, f32[256,512]{1,0:T(8,128)S(1)} %get-tuple-element.43.refs_1_.local.refs_2_, ...), custom_call_target="tpu_custom_call" | custom-call | flops 1342177280 | bytes 4194304 | tf_op jit(solution)/shard_map/pallas_call | solution.py:334
  121.7 0.0 copy-start.2
  121.7 27.7 %all_to_all.5.blocks = f32[32,2,8,512]{3,2,1,0:T(8,128)S(1)} all-to-all(f32[32,2,8,512]{3,2,1,0:T(8,128)S(1)} %shard_map.74), channel_id=1, replica_groups=mesh['slab'=16,'energy'=32] {'energy'}, dimensions={0} | all-to-all | bytes 2097152 | tf_op jit(solution)/shard_map/all_to_all | solution.py:340
  149.4 1.3 shard_map.75
  150.6 1.0 copy.51
  (21 shorter events, 0.3 us)
Async XLA Ops:
  0.6 0.7 copy-start.3
  1.3 1.0 copy-start
  2.3 1.0 copy-start.4
  5.7 1.4 collective-permute-start.2
  6.4 1.4 collective-permute-start
  7.1 1.5 collective-permute-start.3
  7.9 1.5 collective-permute-start.1
  8.7 2.2 %collective-permute-start.6 = (f32[256,512]{1,0:T(8,128)S(1)}, f32[256,512]{1,0:T(8,128)S(1)}, u32[]{:S(2)}, u32[]{:S(2)}) collective-permute-start(f32[256,512]{1,0:T(8,128)S(1)} %get-tuple-element.61), channel_id=1, source_target_pairs={{192,160},{193,161},{194,162},{195,163},{196,164},{197,165},{198,1... | collective-permute-start | bytes 1572872 | tf_op jit(solution)/shard_map/ppermute | solution.py:264
  9.4 2.3 %collective-permute-start.4 = (f32[256,512]{1,0:T(8,128)S(1)}, f32[256,512]{1,0:T(8,128)S(1)}, u32[]{:S(2)}, u32[]{:S(2)}) collective-permute-start(f32[256,512]{1,0:T(8,128)S(1)} %get-tuple-element.60), channel_id=1, source_target_pairs={{64,160},{224,256},{352,384},{65,161},{225,257},{353,385},{66,162}... | collective-permute-start | bytes 1572872 | tf_op jit(solution)/shard_map/ppermute | solution.py:264
  10.1 1.6 %collective-permute-start.5 = (f32[256,512]{1,0:T(8,128)S(1)}, f32[256,512]{1,0:T(8,128)S(1)}, u32[]{:S(2)}, u32[]{:S(2)}) collective-permute-start(f32[256,512]{1,0:T(8,128)S(1)} %get-tuple-element.60), channel_id=1, source_target_pairs={{128,160},{129,161},{130,162},{131,163},{132,164},{133,165},{134,1... | collective-permute-start | bytes 1572872 | tf_op jit(solution)/shard_map/ppermute | solution.py:264
  11.7 1.4 collective-permute-start.7
  12.4 0.7 collective-permute-start.8
  13.2 0.7 collective-permute-start.9
  14.1 0.7 collective-permute-start.10
  14.9 103.3 %collective-permute-start.11 = (f32[256,512]{1,0:T(8,128)S(1)}, f32[256,512]{1,0:T(8,128)S(1)}, u32[]{:S(2)}, u32[]{:S(2)}) collective-permute-start(f32[256,512]{1,0:T(8,128)S(1)} %get-tuple-element.77), channel_id=1, source_target_pairs={{224,256},{320,352},{384,416},{448,480},{225,257},{321,353},{385,4... | collective-permute-start | bytes 1572872 | tf_op jit(solution)/shard_map/ppermute | solution.py:264
  118.2 1.2 copy-start.1
  121.7 27.7 %copy-start.2 = (f32[32]{0:T(128)S(1)}, f32[32]{0:T(128)}, u32[]{:S(2)}) copy-start(f32[32]{0:T(128)} %weights.1) | copy-start | bytes 388

commit v3 on v2

--- a/solution.py
+++ b/solution.py
@@ -8,7 +8,7 @@
 from jax.sharding import PartitionSpec as P
 
 F32, BF16 = jnp.float32, jnp.bfloat16
-GROUPS = (2, 3, 4, 3, 2, 2)
+GROUPS = (2, 2, 3, 4, 3, 2)
 VMEM_BYTES = 40 * 1024 * 1024
 
 
@@ -146,9 +146,7 @@
         out[...] = local[...] + sandwich(high, low, form_high, form_low, state[...])
 
 
-def join_kernel(places, heads, received, joint, *rest):
-    product, high, low, form_high, form_low = rest[-5:]
-
+def join_kernel(places, heads, received, joint, product, *forms):
     @pl.when(takes_part(places))
     def _():
         first_high, first_low = split(received[...])
@@ -158,14 +156,26 @@
 
         @pl.when(takes_part(heads))
         def _():
+            high, low, form_high, form_low = forms
             part_high, part_low = split(product[...])
             high[...], low[...] = part_high, part_low
             form_high[...], form_low[...] = dagger_form(part_high), dagger_form(part_low)
 
 
 def last_kernel(
-    coupling, green, form_first, first, local, high, low, form_high, form_low, state, out
+    places, coupling, green, form_first, first, local, high, low, form_high, form_low, front,
+    state_in, out, state
 ):
+    arriving = takes_part(places)
+
+    @pl.when(arriving)
+    def _():
+        state[...] = front[...]
+
+    @pl.when(jnp.logical_not(arriving))
+    def _():
+        state[...] = state_in[...]
+
     rows = out.shape[2]
     lead = coupling[0, 0]
     value = state[...]
@@ -179,23 +189,28 @@
     out[:, 1] = block.reshape(-1, rows, block.shape[-1])
 
 
-def density_kernel(weights, blocks, out):
+def density_kernel(weights, blocks, out, kept, done):
+    copy = pltpu.make_async_copy(blocks, kept, done)
+    copy.start()
     total = weights[0] * blocks[0]
     for level in range(1, blocks.shape[0]):
         total = total + weights[level] * blocks[level]
     out[...] = total
+    copy.wait()
 
 
 VMEM, SMEM = pl.BlockSpec(memory_space=pltpu.VMEM), pl.BlockSpec(memory_space=pltpu.SMEM)
-
-
-def call(kernel, in_specs, shapes, flops, aliases=None):
+ANY = pl.BlockSpec(memory_space=pl.ANY)
+
+
+def call(kernel, in_specs, shapes, flops, aliases=None, scratch=()):
     return pl.pallas_call(
         kernel,
         in_specs=in_specs,
         out_specs=jax.tree.map(lambda _: VMEM, shapes),
         out_shape=shapes,
         input_output_aliases=aliases or {},
+        scratch_shapes=scratch,
         compiler_params=pltpu.CompilerParams(vmem_limit_bytes=VMEM_BYTES),
         cost_estimate=pl.CostEstimate(flops=flops, bytes_accessed=4 << 20, transcendentals=0),
     )
@@ -255,7 +270,7 @@
     steps, heads = plan(GROUPS)
     shared = {"local": local, "high": high, "low": low, "form_high": form_high, "form_low": form_low}
     joint_forms = (high, low, form_high, form_low)
-    outgoing, product, held, state, whole_forms, posted = local, joint, None, None, None, ()
+    outgoing, product, held, state, whole_forms, posted = local, joint, None, None, {}, ()
     for moves in steps:
         by_kind = {}
         for kind, source, target, role in moves:
@@ -278,14 +293,13 @@
         if "backward" in received:
             places = [target for _, target, _ in by_kind["backward"]]
             ready = [place for place in places if place in heads]
-            kept = tuple(whole_forms) if whole_forms else ()
-            product, *whole_forms = call(
+            product, *forms = call(
                 functools.partial(join_kernel, places, ready),
-                [VMEM] * (2 + len(kept)),
-                [wide, narrow, narrow, form, form],
+                [VMEM] * 2,
+                [wide] + [narrow, narrow, form, form] * bool(ready),
                 3 * cost,
-                {2 + i: 1 + i for i in range(len(kept))},
-            )(received["backward"], joint, *kept)
+            )(received["backward"], joint)
+            whole_forms.update({place: forms for place in ready})
 
         roles = {}
         for role in ("enter", "keep", "lead", "skip", "end"):
@@ -294,6 +308,8 @@
             roles["hold_" + source] = [
                 target for _, target, name in by_kind.get(kind, []) if name == "hold"
             ]
+        if moves is steps[-1]:
+            break
         holding = bool(roles["hold_front"] or roles["hold_extra"])
         joining = bool(roles["skip"] or roles["end"])
         inputs = {"front": received["forward"]}
@@ -303,7 +319,8 @@
             inputs.update(shared)
         beyond = roles["skip"] + roles["lead"]
         if beyond:
-            for name, value in zip(("high", "low", "form_high", "form_low"), whole_forms):
+            (place,) = beyond
+            for name, value in zip(("high", "low", "form_high", "form_low"), whole_forms[place]):
                 inputs["whole_" + name] = value
         outputs = ["out", "state_out"]
         aliases = {}
@@ -332,19 +349,25 @@
 
     rows = half // levels
     blocks = call(
-        last_kernel,
-        [SMEM] + [VMEM] * 9,
+        functools.partial(last_kernel, roles["keep"]),
+        [SMEM] + [VMEM] * 10,
         jax.ShapeDtypeStruct((levels, 2, rows, width), F32),
         10 * cost,
-    )(coupling, green, form_first, first, local, *joint_forms, state)
+        scratch=[pltpu.VMEM((half, width), F32)],
+    )(coupling, green, form_first, first, local, *joint_forms, received["forward"], state)
     block_rows = lax.all_to_all(blocks, "energy", split_axis=0, concat_axis=0, tiled=True)
-    density = call(
+    density, lesser = pl.pallas_call(
         density_kernel,
-        [SMEM, VMEM],
-        jax.ShapeDtypeStruct((2, rows, width), F32),
-        2 * half * width,
+        in_specs=[SMEM, VMEM],
+        out_specs=[VMEM, ANY],
+        out_shape=[
+            jax.ShapeDtypeStruct((2, rows, width), F32),
+            jax.ShapeDtypeStruct(block_rows.shape, F32),
+        ],
+        scratch_shapes=[pltpu.SemaphoreType.DMA],
+        compiler_params=pltpu.CompilerParams(vmem_limit_bytes=VMEM_BYTES),
     )(energy_weights, block_rows)
-    return block_rows, density
+    return lesser, density
 
 
 def solution(mesh):

time: 152 us -> 148 us (0.974)
  the two profiles are of different devices: /device:TPU:481 before, /device:TPU:417 now
where the time goes in v3:
time: 148 us; the launch traced here: 147 us
  waiting for transfers between devices  89.5 us (60%)
  blocking collectives  32.7 us (22%)
  starting transfers between devices  12.1 us (8%)
  Pallas kernels  9.08 us (6%)
  local copies, waits for them, and re-layouts  2.74 us (2%)
    ppermute x11, waiting for transfers between devices, per_device(): lax.ppermute(product if kind == 'backward' else outgoing, 'slab', [(sourc...  89.5 us
    all_to_all x1, blocking collectives, per_device(): lax.all_to_all(blocks, 'energy', split_axis=0, concat_axis=0, tiled=True)  32.7 us
    ppermute x11, starting transfers between devices, per_device(): lax.ppermute(product if kind == 'backward' else outgoing, 'slab', [(sourc...  12.1 us
  transfers between devices with their start and end apart: 11, of which 4 were waited for; matrix products, arithmetic and copies ran while one was open for 0% of the time, Pallas kernels for 2%

profile of v3, /device:TPU:417, one launch (start us, length us, event | category | flops | bytes accessed | tf_op | source)
XLA Modules:
  0.0 147.2 jit_solution(8147844306432822421)
XLA Ops:
  0.6 0.6 copy-done.2
  1.3 1.0 copy-done
  2.3 1.0 copy-done.4
  3.4 2.3 %shard_map.59 = (f32[256,512]{1,0:T(8,128)S(1)}, f32[256,512]{1,0:T(8,128)S(1)}, f32[256,512]{1,0:T(8,128)S(1)}, bf16[256,512]{1,0:T(8,128)(2,1)S(1)}, bf16[256,...) custom-call(s32[1]{0:T(128)} %bitcast.1.position, ...), custom_call_target="tpu_custom_call" | custom-call | flops 1207959552 | bytes 4194304 | tf_op jit(solution)/shard_map/pallas_call | solution.py:263
  5.7 0.7 collective-permute-start
  6.4 3.3 %collective-permute-start.2 = (f32[256,512]{1,0:T(8,128)S(1)}, f32[256,512]{1,0:T(8,128)S(1)}, u32[]{:S(2)}, u32[]{:S(2)}) collective-permute-start(f32[256,512]{1,0:T(8,128)S(1)} %get-tuple-element.52.joint), channel_id=1, source_target_pairs={{96,64},{192,160},{320,288},{416,384},{97,65},{193,161},{321,289},... | collective-permute-start | bytes 1572872 | tf_op jit(solution)/shard_map/ppermute | solution.py:279
  9.7 0.0 collective-permute-done.refs_0_
  9.7 0.1 shard_map.60
  9.7 1.3 collective-permute-start.1
  11.0 9.2 %collective-permute-done.2.received = f32[256,512]{1,0:T(8,128)S(1)} collective-permute-done((f32[256,512]{1,0:T(8,128)S(1)}, f32[256,512]{1,0:T(8,128)S(1)}, u32[]{:S(2)}, u32[]{:S(2)}) %collective-permute-start.2) | collective-permute-done | bytes 524320 | tf_op jit(solution)/shard_map/ppermute | solution.py:279
  20.2 0.7 collective-permute-start.4
  20.9 14.5 %collective-permute-done.1.refs_0_ = f32[256,512]{1,0:T(8,128)S(1)} collective-permute-done((f32[256,512]{1,0:T(8,128)S(1)}, f32[256,512]{1,0:T(8,128)S(1)}, u32[]{:S(2)}, u32[]{:S(2)}) %collective-permute-start.1) | collective-permute-done | bytes 524320 | tf_op jit(solution)/shard_map/ppermute | solution.py:279
  35.4 1.1 shard_map.62
  36.5 1.3 collective-permute-start.3
  37.8 0.0 collective-permute-done.4.received
  37.9 0.7 collective-permute-start.6
  38.6 8.5 %collective-permute-done.3.refs_0_ = f32[256,512]{1,0:T(8,128)S(1)} collective-permute-done((f32[256,512]{1,0:T(8,128)S(1)}, f32[256,512]{1,0:T(8,128)S(1)}, u32[]{:S(2)}, u32[]{:S(2)}) %collective-permute-start.3) | collective-permute-done | bytes 524320 | tf_op jit(solution)/shard_map/ppermute | solution.py:279
  47.1 0.7 collective-permute-start.5
  47.8 0.0 collective-permute-done.6.received
  47.8 0.8 shard_map.66
  48.6 0.7 collective-permute-start.7
  49.4 0.7 collective-permute-start.8
  50.1 0.2 shard_map.71.refs_8_
  50.3 0.0 collective-permute-done.8.refs_0_
  50.3 0.7 collective-permute-start.9
  51.0 0.0 copy-start.1
  51.1 1.4 collective-permute-start.10
  52.5 57.3 %collective-permute-done.10.front = f32[256,512]{1,0:T(8,128)S(1)} collective-permute-done((f32[256,512]{1,0:T(8,128)S(1)}, f32[256,512]{1,0:T(8,128)S(1)}, u32[]{:S(2)}, u32[]{:S(2)}) %collective-permute-start.10) | collective-permute-done | bytes 524320 | tf_op jit(solution)/shard_map/ppermute | solution.py:279
  109.8 2.3 %shard_map.74 = f32[32,2,8,512]{3,2,1,0:T(8,128)S(1)} custom-call(f32[1,2]{1,0:T(1,128)S(1)} %copy-done.2, bf16[2,256,512]{2,1,0:T(8,128)(2,1)S(1)} %bitcast.4, bf16[512,512]{1,0:T(8,128)(2,1)S(1)} %get-tuple-element.44.form_first, f32[256,512]{1,0:T(8,128)S(1)} %get-tuple-element.45.first, f32[256,512]{1,0:T(8,128)S(1)} %get-tuple-element.46.refs_1_.local, ...), custom_call_target="tpu_custom_call" | custom-call | flops 1342177280 | bytes 4194304 | tf_op jit(solution)/shard_map/pallas_call | solution.py:351
  112.1 0.0 copy-start.3
  112.2 32.7 %all_to_all.5.blocks = f32[32,2,8,512]{3,2,1,0:T(8,128)S(1)} all-to-all(f32[32,2,8,512]{3,2,1,0:T(8,128)S(1)} %shard_map.74), channel_id=1, replica_groups=mesh['slab'=16,'energy'=32] {'energy'}, dimensions={0} | all-to-all | bytes 2097152 | tf_op jit(solution)/shard_map/all_to_all | solution.py:358
  144.9 2.1 %shard_map.75 = (f32[2,8,512]{2,1,0:T(8,128)}, f32[32,2,8,512]{3,2,1,0:T(8,128)}) custom-call(f32[32]{0:T(128)S(1)} %copy-done.3, f32[32,2,8,512]{3,2,1,0:T(8,128)S(1)} %all_to_all.5.blocks), custom_call_target="tpu_custom_call" | custom-call | tf_op jit(solution)/shard_map/pallas_call | solution.py:359
  (18 shorter events, 0.2 us)
Async XLA Ops:
  0.6 0.7 copy-start.2
  1.3 1.0 copy-start
  2.3 1.0 copy-start.4
  5.7 4.0 %collective-permute-start = (f32[256,512]{1,0:T(8,128)S(1)}, f32[256,512]{1,0:T(8,128)S(1)}, u32[]{:S(2)}, u32[]{:S(2)}) collective-permute-start(f32[256,512]{1,0:T(8,128)S(1)} %get-tuple-element.46.refs_1_.local), channel_id=1, source_target_pairs={{0,32},{64,96},{128,160},{224,256},{352,384},{1,33},{65,97},{129,1... | collective-permute-start | bytes 1572872 | tf_op jit(solution)/shard_map/ppermute | solution.py:279
  6.4 13.8 %collective-permute-start.2 = (f32[256,512]{1,0:T(8,128)S(1)}, f32[256,512]{1,0:T(8,128)S(1)}, u32[]{:S(2)}, u32[]{:S(2)}) collective-permute-start(f32[256,512]{1,0:T(8,128)S(1)} %get-tuple-element.52.joint), channel_id=1, source_target_pairs={{96,64},{192,160},{320,288},{416,384},{97,65},{193,161},{321,289},... | collective-permute-start | bytes 1572872 | tf_op jit(solution)/shard_map/ppermute | solution.py:279
  9.7 25.6 %collective-permute-start.1 = (f32[256,512]{1,0:T(8,128)S(1)}, f32[256,512]{1,0:T(8,128)S(1)}, u32[]{:S(2)}, u32[]{:S(2)}) collective-permute-start(f32[256,512]{1,0:T(8,128)S(1)} %get-tuple-element.51), channel_id=1, source_target_pairs={{32,64},{96,128},{160,192},{256,288},{384,416},{33,65},{97,129},{1... | collective-permute-start | bytes 1572872 | tf_op jit(solution)/shard_map/ppermute | solution.py:279
  20.2 17.6 %collective-permute-start.4 = (f32[256,512]{1,0:T(8,128)S(1)}, f32[256,512]{1,0:T(8,128)S(1)}, u32[]{:S(2)}, u32[]{:S(2)}) collective-permute-start(f32[256,512]{1,0:T(8,128)S(1)} %get-tuple-element.59), channel_id=1, source_target_pairs={{160,128},{288,256},{384,352},{161,129},{289,257},{385,353},{162,1... | collective-permute-start | bytes 1572872 | tf_op jit(solution)/shard_map/ppermute | solution.py:279
  36.5 10.6 %collective-permute-start.3 = (f32[256,512]{1,0:T(8,128)S(1)}, f32[256,512]{1,0:T(8,128)S(1)}, u32[]{:S(2)}, u32[]{:S(2)}) collective-permute-start(f32[256,512]{1,0:T(8,128)S(1)} %get-tuple-element.58), channel_id=1, source_target_pairs={{64,128},{192,224},{288,320},{416,448},{65,129},{193,225},{289,321... | collective-permute-start | bytes 1572872 | tf_op jit(solution)/shard_map/ppermute | solution.py:279
  37.9 9.9 %collective-permute-start.6 = (f32[256,512]{1,0:T(8,128)S(1)}, f32[256,512]{1,0:T(8,128)S(1)}, u32[]{:S(2)}, u32[]{:S(2)}) collective-permute-start(f32[256,512]{1,0:T(8,128)S(1)} %get-tuple-element.67), channel_id=1, source_target_pairs={{256,224},{257,225},{258,226},{259,227},{260,228},{261,229},{262,2... | collective-permute-start | bytes 1572872 | tf_op jit(solution)/shard_map/ppermute | solution.py:279
  47.1 1.5 %collective-permute-start.5 = (f32[256,512]{1,0:T(8,128)S(1)}, f32[256,512]{1,0:T(8,128)S(1)}, u32[]{:S(2)}, u32[]{:S(2)}) collective-permute-start(f32[256,512]{1,0:T(8,128)S(1)} %get-tuple-element.66), channel_id=1, source_target_pairs={{64,96},{128,224},{320,352},{65,97},{129,225},{321,353},{66,98},{1... | collective-permute-start | bytes 1572872 | tf_op jit(solution)/shard_map/ppermute | solution.py:279
  48.6 0.7 collective-permute-start.7
  49.4 0.9 collective-permute-start.8
  50.3 0.7 collective-permute-start.9
  51.0 58.8 %copy-start.1 = (bf16[1,2,256,512]{3,2,1,0:T(8,128)(2,1)S(1)}, bf16[1,2,256,512]{3,2,1,0:T(8,128)(2,1)}, u32[]{:S(2)}) copy-start(bf16[1,2,256,512]{3,2,1,0:T(8,128)(2,1)} %param.4) | copy-start | bytes 1572868
  51.1 58.7 %collective-permute-start.10 = (f32[256,512]{1,0:T(8,128)S(1)}, f32[256,512]{1,0:T(8,128)S(1)}, u32[]{:S(2)}, u32[]{:S(2)}) collective-permute-start(f32[256,512]{1,0:T(8,128)S(1)} %get-tuple-element.82), channel_id=1, source_target_pairs={{288,320},{384,416},{289,321},{385,417},{290,322},{386,418},{291,3... | collective-permute-start | bytes 1572872 | tf_op jit(solution)/shard_map/ppermute | solution.py:279
  112.1 32.7 %copy-start.3 = (f32[32]{0:T(128)S(1)}, f32[32]{0:T(128)}, u32[]{:S(2)}) copy-start(f32[32]{0:T(128)} %weights.1) | copy-start | bytes 388

commit v4 on v3

--- a/solution.py
+++ b/solution.py
@@ -91,53 +91,46 @@
     return ((jnp.int32(mask) >> position) & 1) == 1
 
 
+def chain_kernel(places, local, high, low, form_high, form_low, front, out):
+    @pl.when(takes_part(places))
+    def _():
+        out[...] = local[...] + sandwich(high, low, form_high, form_low, front[...])
+
+
 def step_kernel(roles, names, *refs):
     ref = dict(zip(names, refs))
     forms = [ref.get(name) for name in ("high", "low", "form_high", "form_low")]
     whole_forms = [ref.get("whole_" + name) for name in ("high", "low", "form_high", "form_low")]
-
-    def hold(source):
-        def body():
-            ref["held_out"][...] = ref[source][...]
-
-        return body
-
-    for source in ("front", "extra"):
-        if roles.get("hold_" + source):
-            pl.when(takes_part(roles["hold_" + source]))(hold(source))
+    front, state = ref["front"], ref["state_out"]
+    if "state" not in ref:
+        state[...] = jnp.zeros_like(state)
     arriving = roles["enter"] + roles["keep"] + roles["lead"]
-    if "state" not in ref:
-
-        @pl.when(jnp.logical_not(takes_part(arriving)))
-        def _():
-            ref["state_out"][...] = jnp.zeros_like(ref["state_out"])
-
     if arriving:
 
         @pl.when(takes_part(arriving))
         def _():
-            ref["state_out"][...] = ref["front"][...]
+            state[...] = front[...]
 
     joined = roles["skip"] + roles["end"]
     if joined:
 
         @pl.when(takes_part(joined))
         def _():
-            ref["state_out"][...] = ref["front"][...] + ref["held_out"][...]
+            state[...] = front[...] + ref["held"][...]
 
     onward = roles["enter"] + roles["end"]
     if onward:
 
         @pl.when(takes_part(onward))
         def _():
-            ref["out"][...] = ref["local"][...] + sandwich(*forms, ref["state_out"][...])
+            ref["out"][...] = ref["local"][...] + sandwich(*forms, state[...])
 
     beyond = roles["skip"] + roles["lead"]
     if beyond:
 
         @pl.when(takes_part(beyond))
         def _():
-            ref["out"][...] = sandwich(*whole_forms, ref["state_out"][...])
+            ref["out"][...] = sandwich(*whole_forms, state[...])
 
 
 def after_kernel(places, local, high, low, form_high, form_low, state, out):
@@ -216,37 +209,45 @@
     )
 
 
+ROLES = ("enter", "lead", "skip", "end", "keep", "after")
+
+
 def plan(sizes):
     groups = len(sizes)
     heads = [sum(sizes[:k]) for k in range(groups)]
     tails = [head + size - 1 for head, size in zip(heads, sizes)]
     arrive = [0] + [sizes[0] + k - 1 for k in range(1, groups)]
-    steps = {}
-
-    def move(step, kind, source, target, role):
-        steps.setdefault(step, []).append((kind, source, target, role))
+    longest = max(sizes[1:-1])
+    chains = [[] for _ in range(longest + 1)]
+    products = [[] for _ in range(longest)]
+    count = max(arrive[k] + (0 < k < groups - 1) + sizes[k] - 1 for k in range(groups))
+    sweep = [[] for _ in range(count + 1)]
+    roles = [{role: [] for role in ROLES} for _ in range(count + 2)]
+
+    def move(step, source, target, role):
+        sweep[step].append((source, target))
+        roles[step][role].append(target)
 
     for k in range(groups):
         head, tail, size = heads[k], tails[k], sizes[k]
-        middle = 0 < k < groups - 1
         if k == 0:
             for i in range(1, size):
-                move(i, "forward", head + i - 1, head + i, "enter")
-            move(size, "forward", tail, heads[1], "lead" if groups > 2 else "enter")
+                move(i, i - 1, i, "enter")
+            move(size, tail, heads[1], "lead")
+            continue
+        middle = k < groups - 1
         if middle:
+            assert 1 < size <= arrive[k]
+            for i in range(1, size + 1):
+                chains[i].append((head + i - 1, head + i))
             for i in range(1, size):
-                move(i, "forward", head + i - 1, head + i, "enter")
-                move(i, "backward", tail - i + 1, tail - i, "join")
-            own = "forward" if size < arrive[k] + 1 else "extra"
-            move(size, own, tail, heads[k + 1], "hold")
-            last = k + 1 == groups - 1
-            move(arrive[k] + 1, "forward", head, heads[k + 1], "end" if last else "skip")
-        if k > 0:
-            delay = 1 if middle else 0
-            for i in range(1, size):
-                role = "enter" if head + i < tail else "keep"
-                move(arrive[k] + delay + i, "forward", head + i - 1, head + i, role)
-    return [steps[s] for s in sorted(steps)], heads
+                products[i].append((tail - i + 1, tail - i))
+            move(arrive[k] + 1, head, heads[k + 1], "skip" if k + 1 < groups - 1 else "end")
+            roles[arrive[k] + 1]["after"].append(head)
+        for i in range(1, size):
+            role = "enter" if head + i < tail else "keep"
+            move(arrive[k] + middle + i, head + i - 1, head + i, role)
+    return heads, tails, chains, products, sweep, roles
 
 
 def per_device(green_left, sigma_lesser, coupling, energy_weights):
@@ -267,94 +268,73 @@
         9 * cost,
     )(position[None], coupling, green, sigma)
     joint_forms = (high, low, form_high, form_low)
-    steps, heads = plan(GROUPS)
+    heads, tails, chains, products, sweep, roles = plan(GROUPS)
+    group_of = {head: k for k, head in enumerate(heads)}
     shared = {"local": local, "high": high, "low": low, "form_high": form_high, "form_low": form_low}
     joint_forms = (high, low, form_high, form_low)
-    outgoing, product, held, state, whole_forms, posted = local, joint, None, None, {}, ()
-    for moves in steps:
-        by_kind = {}
-        for kind, source, target, role in moves:
-            by_kind.setdefault(kind, []).append((source, target, role))
-        received = {
-            kind: lax.ppermute(
-                product if kind == "backward" else outgoing,
-                "slab",
-                [(source, target) for source, target, _ in by_kind[kind]],
+
+    composites, part = {}, local
+    whole_forms, product = {}, joint
+    state, outgoing = None, local
+    for step in range(1, len(sweep)):
+        role = roles[step]
+        front = lax.ppermute(outgoing, "slab", sweep[step])
+        if step < len(chains):
+            composites[step] = lax.ppermute(part, "slab", chains[step])
+        if step < len(products):
+            earlier = lax.ppermute(product, "slab", products[step])
+        if role["after"]:
+            after = call(functools.partial(after_kernel, role["after"]), [VMEM] * 6, wide, 6 * cost)(
+                local, *joint_forms, state
             )
-            for kind in ("forward", "extra", "backward")
-            if kind in by_kind
-        }
-        after = None
-        if posted:
-            after = call(
-                functools.partial(after_kernel, posted), [VMEM] * 6, wide, 6 * cost
-            )(local, *joint_forms, state)
-
-        if "backward" in received:
-            places = [target for _, target, _ in by_kind["backward"]]
+        if step == len(sweep) - 1:
+            break
+        if step < len(chains) - 1:
+            places = [target for _, target in chains[step] if target not in heads]
+            part = call(functools.partial(chain_kernel, places), [VMEM] * 6, wide, 6 * cost)(
+                local, *joint_forms, composites[step]
+            )
+        if step < len(products):
+            places = [target for _, target in products[step]]
             ready = [place for place in places if place in heads]
             product, *forms = call(
                 functools.partial(join_kernel, places, ready),
                 [VMEM] * 2,
                 [wide] + [narrow, narrow, form, form] * bool(ready),
                 3 * cost,
-            )(received["backward"], joint)
+            )(earlier, joint)
             whole_forms.update({place: forms for place in ready})
-
-        roles = {}
-        for role in ("enter", "keep", "lead", "skip", "end"):
-            roles[role] = [target for _, target, name in by_kind["forward"] if name == role]
-        for source, kind in (("front", "forward"), ("extra", "extra")):
-            roles["hold_" + source] = [
-                target for _, target, name in by_kind.get(kind, []) if name == "hold"
-            ]
-        if moves is steps[-1]:
-            break
-        holding = bool(roles["hold_front"] or roles["hold_extra"])
-        joining = bool(roles["skip"] or roles["end"])
-        inputs = {"front": received["forward"]}
-        if "extra" in received:
-            inputs["extra"] = received["extra"]
-        if roles["enter"] or roles["end"]:
+        inputs = {"front": front}
+        if role["enter"] or role["end"]:
             inputs.update(shared)
-        beyond = roles["skip"] + roles["lead"]
-        if beyond:
-            (place,) = beyond
+        for place in role["skip"] + role["lead"]:
             for name, value in zip(("high", "low", "form_high", "form_low"), whole_forms[place]):
                 inputs["whole_" + name] = value
-        outputs = ["out", "state_out"]
+        for place in role["skip"] + role["end"]:
+            inputs["held"] = composites[GROUPS[group_of[place] - 1]]
         aliases = {}
         if state is not None:
             aliases[len(inputs)] = 1
             inputs["state"] = state
-        if holding or joining:
-            if held is not None:
-                aliases[len(inputs)] = 2
-                inputs["held"] = held
-            outputs.append("held_out")
-        if after is not None:
+        if role["after"]:
             aliases[len(inputs)] = 0
             inputs["after"] = after
-        results = call(
-            functools.partial(step_kernel, roles, tuple(inputs) + tuple(outputs)),
+        outgoing, state = call(
+            functools.partial(step_kernel, role, tuple(inputs) + ("out", "state_out")),
             [VMEM] * len(inputs),
-            [wide] * len(outputs),
+            [wide, wide],
             6 * cost,
             aliases,
         )(*inputs.values())
-        outgoing, state = results[:2]
-        if holding or joining:
-            held = results[2]
-        posted = [place for place in beyond if place + 1 not in heads]
 
     rows = half // levels
     blocks = call(
-        functools.partial(last_kernel, roles["keep"]),
+        functools.partial(last_kernel, role["keep"]),
         [SMEM] + [VMEM] * 10,
         jax.ShapeDtypeStruct((levels, 2, rows, width), F32),
         10 * cost,
         scratch=[pltpu.VMEM((half, width), F32)],
-    )(coupling, green, form_first, first, local, *joint_forms, received["forward"], state)
+    )(coupling, green, form_first, first, local, *joint_forms, front, state)
     block_rows = lax.all_to_all(blocks, "energy", split_axis=0, concat_axis=0, tiled=True)
     density, lesser = pl.pallas_call(
         density_kernel,

time: 148 us -> 139 us (0.939)
  waiting for transfers between devices: 89.5 us -> 82.2 us
  blocking collectives: 32.7 us -> 29 us
  starting transfers between devices: 12.1 us -> 14.9 us
    ppermute x11 -> x15, waiting for transfers between devices: 89.5 us -> 82.2 us  [the longest x8 52.3 us: per_device(): front = lax.ppermute(outgoing, 'slab', sweep[step])]
    all_to_all x1, blocking collectives: 32.7 us -> 29 us  [per_device(): lax.all_to_all(blocks, 'energy', split_axis=0, concat_axis=0, tiled=True)]
    ppermute x11 -> x15, starting transfers between devices: 12.1 us -> 14.9 us  [the longest x8 6.27 us: per_device(): front = lax.ppermute(outgoing, 'slab', sweep[step])]
    pallas_call x12 -> x15, Pallas kernels: 3.81 us -> 3.81 us  [the longest x1 2.32 us: per_device(): call(functools.partial(last_kernel, role['keep']), [SMEM] + [VMEM] * 10,...]
  transfers between devices with their start and end apart: 11 -> 15, of which waited for: 4 -> 4; matrix products, arithmetic and copies ran while one was open for 0% -> 0% of each run, Pallas kernels for 2% -> 1%
where the time goes in v4:
time: 139 us
  waiting for transfers between devices  82.2 us (59%)
  blocking collectives  29 us (21%)
  starting transfers between devices  14.9 us (11%)
  Pallas kernels  9.09 us (7%)
  local copies, waits for them, and re-layouts  2.74 us (2%)
    ppermute x8, waiting for transfers between devices, per_device(): front = lax.ppermute(outgoing, 'slab', sweep[step])  52.3 us
    all_to_all x1, blocking collectives, per_device(): lax.all_to_all(blocks, 'energy', split_axis=0, concat_axis=0, tiled=True)  29 us
    ppermute x4, waiting for transfers between devices, per_device(): composites[step] = lax.ppermute(part, 'slab', chains[step])  21.5 us
    ppermute x3, waiting for transfers between devices, per_device(): earlier = lax.ppermute(product, 'slab', products[step])  8.45 us
    ppermute x8, starting transfers between devices, per_device(): front = lax.ppermute(outgoing, 'slab', sweep[step])  6.27 us
    ppermute x3, starting transfers between devices, per_device(): earlier = lax.ppermute(product, 'slab', products[step])  4.63 us
    ppermute x4, starting transfers between devices, per_device(): composites[step] = lax.ppermute(part, 'slab', chains[step])  3.99 us
  transfers between devices with their start and end apart: 15, of which 4 were waited for; matrix products, arithmetic and copies ran while one was open for 0% of the time, Pallas kernels for 1%

profile of v4, /device:TPU:417, one launch (start us, length us, event | category | flops | bytes accessed | tf_op | source)
XLA Modules:
  0.0 139.1 jit_solution(3140144623954628454)
XLA Ops:
  0.6 0.6 copy-done.2
  1.3 1.0 copy-done
  2.3 1.0 copy-done.4
  3.4 2.3 %shard_map.59 = (f32[256,512]{1,0:T(8,128)S(1)}, f32[256,512]{1,0:T(8,128)S(1)}, f32[256,512]{1,0:T(8,128)S(1)}, bf16[256,512]{1,0:T(8,128)(2,1)S(1)}, bf16[256,...) custom-call(s32[1]{0:T(128)} %bitcast.1.position, ...), custom_call_target="tpu_custom_call" | custom-call | flops 1207959552 | bytes 4194304 | tf_op jit(solution)/shard_map/pallas_call | solution.py:264
  5.7 0.7 collective-permute-start
  6.4 0.7 collective-permute-start.5
  7.1 3.3 %collective-permute-start.2 = (f32[256,512]{1,0:T(8,128)S(1)}, f32[256,512]{1,0:T(8,128)S(1)}, u32[]{:S(2)}, u32[]{:S(2)}) collective-permute-start(f32[256,512]{1,0:T(8,128)S(1)} %get-tuple-element.48.joint), channel_id=1, source_target_pairs={{96,64},{192,160},{320,288},{416,384},{97,65},{193,161},{321,289},... | collective-permute-start | bytes 1572872 | tf_op jit(solution)/shard_map/ppermute | solution.py:285
  10.4 0.7 collective-permute-start.1
  11.2 1.3 collective-permute-start.6
  12.5 8.4 %collective-permute-done.2.received = f32[256,512]{1,0:T(8,128)S(1)} collective-permute-done((f32[256,512]{1,0:T(8,128)S(1)}, f32[256,512]{1,0:T(8,128)S(1)}, u32[]{:S(2)}, u32[]{:S(2)}) %collective-permute-start.2) | collective-permute-done | bytes 524320 | tf_op jit(solution)/shard_map/ppermute | solution.py:285
  20.9 0.7 collective-permute-start.4
  21.6 0.7 collective-permute-start.3
  22.3 13.7 %collective-permute-done.6.refs_5_.front = f32[256,512]{1,0:T(8,128)S(1)} collective-permute-done((f32[256,512]{1,0:T(8,128)S(1)}, f32[256,512]{1,0:T(8,128)S(1)}, u32[]{:S(2)}, u32[]{:S(2)}) %collective-permute-start.6) | collective-permute-done | bytes 524320 | tf_op jit(solution)/shard_map/ppermute | solution.py:283
  36.0 1.1 shard_map.68
  37.1 1.3 collective-permute-start.9
  38.4 0.0 collective-permute-done.4.received
  38.5 0.7 collective-permute-start.8
  39.3 0.7 collective-permute-start.7
  40.0 7.7 %collective-permute-done.9.refs_5_.front.refs_6_ = f32[256,512]{1,0:T(8,128)S(1)} collective-permute-done((f32[256,512]{1,0:T(8,128)S(1)}, f32[256,512]{1,0:T(8,128)S(1)}, u32[]{:S(2)}, u32[]{:S(2)}) %collective-permute-start.9) | collective-permute-done | bytes 524320 | tf_op jit(solution)/shard_map/ppermute | solution.py:283
  47.7 0.7 collective-permute-start.11
  48.4 0.8 shard_map.67
  49.2 0.7 collective-permute-start.10
  49.9 0.2 shard_map.73
  50.2 0.7 collective-permute-start.12
  50.9 0.7 collective-permute-start.13
  51.7 0.0 copy-start.1
  51.7 1.4 %collective-permute-start.14 = (f32[256,512]{1,0:T(8,128)S(1)}, f32[256,512]{1,0:T(8,128)S(1)}, u32[]{:S(2)}, u32[]{:S(2)}) collective-permute-start(f32[256,512]{1,0:T(8,128)S(1)} %get-tuple-element.74), channel_id=1, source_target_pairs={{288,320},{384,416},{289,321},{385,417},{290,322},{386,418},{291,3... | collective-permute-start | bytes 1572872 | tf_op jit(solution)/shard_map/ppermute | solution.py:281
  53.1 52.3 %collective-permute-done.14.front = f32[256,512]{1,0:T(8,128)S(1)} collective-permute-done((f32[256,512]{1,0:T(8,128)S(1)}, f32[256,512]{1,0:T(8,128)S(1)}, u32[]{:S(2)}, u32[]{:S(2)}) %collective-permute-start.14) | collective-permute-done | bytes 524320 | tf_op jit(solution)/shard_map/ppermute | solution.py:281
  105.5 2.3 %shard_map.77 = f32[32,2,8,512]{3,2,1,0:T(8,128)S(1)} custom-call(f32[1,2]{1,0:T(1,128)S(1)} %copy-done.2, bf16[2,256,512]{2,1,0:T(8,128)(2,1)S(1)} %bitcast.4, bf16[512,512]{1,0:T(8,128)(2,1)S(1)} %get-tuple-element.40.form_first, f32[256,512]{1,0:T(8,128)S(1)} %get-tuple-element.41.first, f32[256,512]{1,0:T(8,128)S(1)} %get-tuple-element.42.refs_1_.local, ...), custom_call_target="tpu_custom_call" | custom-call | flops 1342177280 | bytes 4194304 | tf_op jit(solution)/shard_map/pallas_call | solution.py:331
  107.8 0.0 copy-start.3
  107.8 29.0 %all_to_all.5.blocks = f32[32,2,8,512]{3,2,1,0:T(8,128)S(1)} all-to-all(f32[32,2,8,512]{3,2,1,0:T(8,128)S(1)} %shard_map.77), channel_id=1, replica_groups=mesh['slab'=16,'energy'=32] {'energy'}, dimensions={0} | all-to-all | bytes 2097152 | tf_op jit(solution)/shard_map/all_to_all | solution.py:338
  136.8 2.1 %shard_map.78 = (f32[2,8,512]{2,1,0:T(8,128)}, f32[32,2,8,512]{3,2,1,0:T(8,128)}) custom-call(f32[32]{0:T(128)S(1)} %copy-done.3, f32[32,2,8,512]{3,2,1,0:T(8,128)S(1)} %all_to_all.5.blocks), custom_call_target="tpu_custom_call" | custom-call | tf_op jit(solution)/shard_map/pallas_call | solution.py:339
  (29 shorter events, 0.3 us)
Async XLA Ops:
  0.6 0.7 copy-start.2
  1.3 1.0 copy-start
  2.3 1.0 copy-start.4
  5.7 4.7 %collective-permute-start = (f32[256,512]{1,0:T(8,128)S(1)}, f32[256,512]{1,0:T(8,128)S(1)}, u32[]{:S(2)}, u32[]{:S(2)}) collective-permute-start(f32[256,512]{1,0:T(8,128)S(1)} %get-tuple-element.42.refs_1_.local), channel_id=1, source_target_pairs={{0,32},{1,33},{2,34},{3,35},{4,36},{5,37},{6,38},{7,39},{8,40},{9,... | collective-permute-start | bytes 1572872 | tf_op jit(solution)/shard_map/ppermute | solution.py:281
  6.4 4.7 %collective-permute-start.5 = (f32[256,512]{1,0:T(8,128)S(1)}, f32[256,512]{1,0:T(8,128)S(1)}, u32[]{:S(2)}, u32[]{:S(2)}) collective-permute-start(f32[256,512]{1,0:T(8,128)S(1)} %get-tuple-element.42.refs_1_.local), channel_id=1, source_target_pairs={{64,96},{128,160},{224,256},{352,384},{65,97},{129,161},{225,257},... | collective-permute-start | bytes 1572872 | tf_op jit(solution)/shard_map/ppermute | solution.py:283
  7.1 13.8 %collective-permute-start.2 = (f32[256,512]{1,0:T(8,128)S(1)}, f32[256,512]{1,0:T(8,128)S(1)}, u32[]{:S(2)}, u32[]{:S(2)}) collective-permute-start(f32[256,512]{1,0:T(8,128)S(1)} %get-tuple-element.48.joint), channel_id=1, source_target_pairs={{96,64},{192,160},{320,288},{416,384},{97,65},{193,161},{321,289},... | collective-permute-start | bytes 1572872 | tf_op jit(solution)/shard_map/ppermute | solution.py:285
  10.4 11.2 %collective-permute-start.1 = (f32[256,512]{1,0:T(8,128)S(1)}, f32[256,512]{1,0:T(8,128)S(1)}, u32[]{:S(2)}, u32[]{:S(2)}) collective-permute-start(f32[256,512]{1,0:T(8,128)S(1)} %get-tuple-element.47), channel_id=1, source_target_pairs={{32,64},{33,65},{34,66},{35,67},{36,68},{37,69},{38,70},{39,71},{4... | collective-permute-start | bytes 1572872 | tf_op jit(solution)/shard_map/ppermute | solution.py:281
  11.2 24.9 %collective-permute-start.6 = (f32[256,512]{1,0:T(8,128)S(1)}, f32[256,512]{1,0:T(8,128)S(1)}, u32[]{:S(2)}, u32[]{:S(2)}) collective-permute-start(f32[256,512]{1,0:T(8,128)S(1)} %shard_map.64), channel_id=1, source_target_pairs={{96,128},{160,192},{256,288},{384,416},{97,129},{161,193},{257,289... | collective-permute-start | bytes 1572872 | tf_op jit(solution)/shard_map/ppermute | solution.py:283
  20.9 17.6 %collective-permute-start.4 = (f32[256,512]{1,0:T(8,128)S(1)}, f32[256,512]{1,0:T(8,128)S(1)}, u32[]{:S(2)}, u32[]{:S(2)}) collective-permute-start(f32[256,512]{1,0:T(8,128)S(1)} %get-tuple-element.55), channel_id=1, source_target_pairs={{160,128},{288,256},{384,352},{161,129},{289,257},{385,353},{162,1... | collective-permute-start | bytes 1572872 | tf_op jit(solution)/shard_map/ppermute | solution.py:285
  21.6 17.6 %collective-permute-start.3 = (f32[256,512]{1,0:T(8,128)S(1)}, f32[256,512]{1,0:T(8,128)S(1)}, u32[]{:S(2)}, u32[]{:S(2)}) collective-permute-start(f32[256,512]{1,0:T(8,128)S(1)} %get-tuple-element.54), channel_id=1, source_target_pairs={{64,128},{65,129},{66,130},{67,131},{68,132},{69,133},{70,134},{71... | collective-permute-start | bytes 1572872 | tf_op jit(solution)/shard_map/ppermute | solution.py:281
  37.1 10.6 %collective-permute-start.9 = (f32[256,512]{1,0:T(8,128)S(1)}, f32[256,512]{1,0:T(8,128)S(1)}, u32[]{:S(2)}, u32[]{:S(2)}) collective-permute-start(f32[256,512]{1,0:T(8,128)S(1)} %shard_map.68), channel_id=1, source_target_pairs={{192,224},{288,320},{416,448},{193,225},{289,321},{417,449},{194,2... | collective-permute-start | bytes 1572872 | tf_op jit(solution)/shard_map/ppermute | solution.py:283
  38.5 9.9 %collective-permute-start.8 = (f32[256,512]{1,0:T(8,128)S(1)}, f32[256,512]{1,0:T(8,128)S(1)}, u32[]{:S(2)}, u32[]{:S(2)}) collective-permute-start(f32[256,512]{1,0:T(8,128)S(1)} %get-tuple-element.62), channel_id=1, source_target_pairs={{256,224},{257,225},{258,226},{259,227},{260,228},{261,229},{262,2... | collective-permute-start | bytes 1572872 | tf_op jit(solution)/shard_map/ppermute | solution.py:285
  39.3 10.0 %collective-permute-start.7 = (f32[256,512]{1,0:T(8,128)S(1)}, f32[256,512]{1,0:T(8,128)S(1)}, u32[]{:S(2)}, u32[]{:S(2)}) collective-permute-start(f32[256,512]{1,0:T(8,128)S(1)} %get-tuple-element.61), channel_id=1, source_target_pairs={{64,96},{128,224},{65,97},{129,225},{66,98},{130,226},{67,99},{131... | collective-permute-start | bytes 1572872 | tf_op jit(solution)/shard_map/ppermute | solution.py:281
  47.7 2.2 %collective-permute-start.11 = (f32[256,512]{1,0:T(8,128)S(1)}, f32[256,512]{1,0:T(8,128)S(1)}, u32[]{:S(2)}, u32[]{:S(2)}) collective-permute-start(f32[256,512]{1,0:T(8,128)S(1)} %shard_map.71), channel_id=1, source_target_pairs={{320,352},{321,353},{322,354},{323,355},{324,356},{325,357},{326,3... | collective-permute-start | bytes 1572872 | tf_op jit(solution)/shard_map/ppermute | solution.py:283
  49.2 0.7 collective-permute-start.10
  50.2 0.7 collective-permute-start.12
  50.9 0.7 collective-permute-start.13
  51.7 53.8 %copy-start.1 = (bf16[1,2,256,512]{3,2,1,0:T(8,128)(2,1)S(1)}, bf16[1,2,256,512]{3,2,1,0:T(8,128)(2,1)}, u32[]{:S(2)}) copy-start(bf16[1,2,256,512]{3,2,1,0:T(8,128)(2,1)} %param.4) | copy-start | bytes 1572868
  51.7 53.7 %collective-permute-start.14 = (f32[256,512]{1,0:T(8,128)S(1)}, f32[256,512]{1,0:T(8,128)S(1)}, u32[]{:S(2)}, u32[]{:S(2)}) collective-permute-start(f32[256,512]{1,0:T(8,128)S(1)} %get-tuple-element.74), channel_id=1, source_target_pairs={{288,320},{384,416},{289,321},{385,417},{290,322},{386,418},{291,3... | collective-permute-start | bytes 1572872 | tf_op jit(solution)/shard_map/ppermute | solution.py:281
  107.8 29.0 %copy-start.3 = (f32[32]{0:T(128)S(1)}, f32[32]{0:T(128)}, u32[]{:S(2)}) copy-start(f32[32]{0:T(128)} %weights.1) | copy-start | bytes 388

commit v5 on v4

--- a/solution.py
+++ b/solution.py
@@ -56,15 +56,13 @@
     return dot(high, form_high) + dot(low, form_high) + dot(high, form_low)
 
 
-def setup_kernel(
-    position, coupling, green, sigma, local, first, joint, high, low, form_high, form_low, form_first
-):
+def source_kernel(coupling, green, sigma, local, first, form_first):
     half = green.shape[1]
     lead, follow = coupling[0, 0], coupling[0, 1]
     green_first, green_second = green[0], green[1]
     form = dagger_form(green_first)
     form_first[...] = form
-    contact = jnp.where(position[0] == 0, lead * lead, 0.0)
+    contact = jnp.where(lax.axis_index("slab") == 0, lead * lead, 0.0)
     turned = jnp.concatenate(
         [-green_first[:, half:].astype(F32), green_first[:, :half].astype(F32)], axis=1
     )
@@ -73,13 +71,24 @@
     first[...] = first_block
     middle = sigma[1].astype(F32) + (follow * follow) * first_block
     local[...] = right_narrow(product_narrow(green_second, middle), dagger_form(green_second))
-    whole = (lead * follow) * dot(green_second, expanded(green_first))
+
+
+def joint_kernel(coupling, green, joint, high, low, form_high, form_low):
+    whole = (coupling[0, 0] * coupling[0, 1]) * dot(green[1], expanded(green[0]))
     joint[...] = whole
     part_high, part_low = split(whole)
     high[...], low[...] = part_high, part_low
     form_high[...], form_low[...] = dagger_form(part_high), dagger_form(part_low)
 
 
+def turn_kernel(token, value, out):
+    del token
+
+    @pl.when(lax.axis_index("energy") % 2 == 0)
+    def _():
+        out[...] = value[...]
+
+
 def sandwich(high, low, form_high, form_low, value):
     partial = product_wide(high[...], low[...], value)
     return right_wide(partial, form_high[...], form_low[...])
@@ -91,10 +100,16 @@
     return ((jnp.int32(mask) >> position) & 1) == 1
 
 
-def chain_kernel(places, local, high, low, form_high, form_low, front, out):
-    @pl.when(takes_part(places))
-    def _():
-        out[...] = local[...] + sandwich(high, low, form_high, form_low, front[...])
+def chain_kernel(places, local, high, low, form_high, form_low, *rest):
+    *arrived, out = rest
+    for core, front in enumerate(arrived):
+        mine = takes_part(places)
+        if len(arrived) > 1:
+            mine = mine & (lax.axis_index("energy") % 2 != core)
+
+        @pl.when(mine)
+        def _(front=front):
+            out[...] = local[...] + sandwich(high, low, form_high, form_low, front[...])
 
 
 def step_kernel(roles, names, *refs):
@@ -106,8 +121,15 @@
         state[...] = jnp.zeros_like(state)
     arriving = roles["enter"] + roles["keep"] + roles["lead"]
     if arriving:
-
-        @pl.when(takes_part(arriving))
+        late = False
+        if "late" in ref:
+            late = takes_part(arriving) & (lax.axis_index("energy") % 2 == 0)
+
+            @pl.when(late)
+            def _():
+                state[...] = ref["late"][...]
+
+        @pl.when(takes_part(arriving) & jnp.logical_not(late))
         def _():
             state[...] = front[...]
 
@@ -183,13 +205,22 @@
 
 
 def density_kernel(weights, blocks, out, kept, done):
-    copy = pltpu.make_async_copy(blocks, kept, done)
-    copy.start()
+    parts = done.shape[0]
+    size = blocks.shape[0] // parts
+    copies = [
+        pltpu.make_async_copy(
+            blocks.at[pl.ds(part * size, size)], kept.at[pl.ds(part * size, size)], done.at[part]
+        )
+        for part in range(parts)
+    ]
+    for copy in copies:
+        copy.start()
     total = weights[0] * blocks[0]
     for level in range(1, blocks.shape[0]):
         total = total + weights[level] * blocks[level]
     out[...] = total
-    copy.wait()
+    for copy in copies:
+        copy.wait()
 
 
 VMEM, SMEM = pl.BlockSpec(memory_space=pltpu.VMEM), pl.BlockSpec(memory_space=pltpu.SMEM)
@@ -207,6 +238,14 @@
         compiler_params=pltpu.CompilerParams(vmem_limit_bytes=VMEM_BYTES),
         cost_estimate=pl.CostEstimate(flops=flops, bytes_accessed=4 << 20, transcendentals=0),
     )
+
+
+def of_cores(pairs, levels, core):
+    return [
+        (source * levels + level, target * levels + level)
+        for source, target in pairs
+        for level in range(core, levels, 2)
+    ]
 
 
 ROLES = ("enter", "lead", "skip", "end", "keep", "after")
@@ -254,20 +293,18 @@
     green, sigma = green_left[0], sigma_lesser[0]
     half, width = green.shape[1:]
     slabs, levels = lax.axis_size("slab"), lax.axis_size("energy")
-    position = lax.axis_index("slab").astype(jnp.int32)
     wide = jax.ShapeDtypeStruct((half, width), F32)
     narrow = jax.ShapeDtypeStruct((half, width), BF16)
     form = jax.ShapeDtypeStruct((width, width), BF16)
     cost = 2 * half * width * width
     assert sum(GROUPS) == slabs
 
-    local, first, joint, high, low, form_high, form_low, form_first = call(
-        setup_kernel,
-        [SMEM, SMEM, VMEM, VMEM],
-        [wide, wide, wide, narrow, narrow, form, form, form],
-        9 * cost,
-    )(position[None], coupling, green, sigma)
-    joint_forms = (high, low, form_high, form_low)
+    local, first, form_first = call(
+        source_kernel, [SMEM, VMEM, VMEM], [wide, wide, form], 8 * cost
+    )(coupling, green, sigma)
+    joint, high, low, form_high, form_low = call(
+        joint_kernel, [SMEM, VMEM], [wide, narrow, narrow, form, form], cost
+    )(coupling, green)
     heads, tails, chains, products, sweep, roles = plan(GROUPS)
     group_of = {head: k for k, head in enumerate(heads)}
     shared = {"local": local, "high": high, "low": low, "form_high": form_high, "form_low": form_low}
@@ -278,8 +315,16 @@
     state, outgoing = None, local
     for step in range(1, len(sweep)):
         role = roles[step]
-        front = lax.ppermute(outgoing, "slab", sweep[step])
-        if step < len(chains):
+        if step == 1:
+            pairs = sweep[1] + chains[1]
+            front = lax.ppermute(local, ("slab", "energy"), of_cores(pairs, levels, 1))
+            partner = [(slab, slab ^ 1) for slab in range(slabs)]
+            token = lax.ppermute(coupling, ("slab", "energy"), of_cores(partner, levels, 0))
+            turned = call(turn_kernel, [VMEM] * 2, wide, 0)(token, local)
+            late = lax.ppermute(turned, ("slab", "energy"), of_cores(pairs, levels, 0))
+        else:
+            front = lax.ppermute(outgoing, "slab", sweep[step])
+        if 1 < step < len(chains):
             composites[step] = lax.ppermute(part, "slab", chains[step])
         if step < len(products):
             earlier = lax.ppermute(product, "slab", products[step])
@@ -291,9 +336,10 @@
             break
         if step < len(chains) - 1:
             places = [target for _, target in chains[step] if target not in heads]
-            part = call(functools.partial(chain_kernel, places), [VMEM] * 6, wide, 6 * cost)(
-                local, *joint_forms, composites[step]
-            )
+            arrived = [front, late] if step == 1 else [composites[step]]
+            part = call(
+                functools.partial(chain_kernel, places), [VMEM] * (5 + len(arrived)), wide, 6 * cost
+            )(local, *joint_forms, *arrived)
         if step < len(products):
             places = [target for _, target in products[step]]
             ready = [place for place in places if place in heads]
@@ -305,6 +351,8 @@
             )(earlier, joint)
             whole_forms.update({place: forms for place in ready})
         inputs = {"front": front}
+        if step == 1:
+            inputs["late"] = late
         if role["enter"] or role["end"]:
             inputs.update(shared)
         for place in role["skip"] + role["lead"]:
@@ -344,7 +392,7 @@
             jax.ShapeDtypeStruct((2, rows, width), F32),
             jax.ShapeDtypeStruct(block_rows.shape, F32),
         ],
-        scratch_shapes=[pltpu.SemaphoreType.DMA],
+        scratch_shapes=[pltpu.SemaphoreType.DMA((min(8, levels),))],
         compiler_params=pltpu.CompilerParams(vmem_limit_bytes=VMEM_BYTES),
     )(energy_weights, block_rows)
     return lesser, density

time: 139 us -> 138 us (level)
  waiting for transfers between devices: 82.2 us -> 70.8 us
  blocking collectives: 29 us -> 36.9 us
    all_to_all x1, blocking collectives: 29 us -> 36.9 us  [per_device(): lax.all_to_all(blocks, 'energy', split_axis=0, concat_axis=0, tiled=True)]
    ppermute x8 -> x7, waiting for transfers between devices: 52.3 us -> 46.7 us  [per_device(): front = lax.ppermute(outgoing, 'slab', sweep[step])]
    ppermute x4 -> x3, waiting for transfers between devices: 21.5 us -> 16.7 us  [per_device(): composites[step] = lax.ppermute(part, 'slab', chains[step])]
    ppermute x0 -> x3, starting transfers between devices: none -> 2.18 us  [the longest x1 0.83 us: per_device(): front = lax.ppermute(local, ('slab', 'energy'), of_cores(pairs, levels, 1))]
    ppermute x8 -> x7, starting transfers between devices: 6.27 us -> 5.46 us  [per_device(): front = lax.ppermute(outgoing, 'slab', sweep[step])]
    pallas_call x4 -> x6, Pallas kernels: 3.4 us -> 4.14 us  [the longest x1 2.01 us: per_device(): call(source_kernel, [SMEM, VMEM, VMEM], [wide, wide, form], 8 * cost)]
    ppermute x4 -> x3, starting transfers between devices: 3.99 us -> 3.3 us  [per_device(): composites[step] = lax.ppermute(part, 'slab', chains[step])]
  transfers between devices with their start and end apart: 15 -> 16, of which waited for: 4 -> 4; matrix products, arithmetic and copies ran while one was open for 0% -> 0% of each run, Pallas kernels for 1% -> 4%
where the time goes in v5:
time: 138 us; the launch traced here: 137 us
  waiting for transfers between devices  70.8 us (51%)
  blocking collectives  36.9 us (27%)
  starting transfers between devices  15.6 us (11%)
  Pallas kernels  9.93 us (7%)
  local copies, waits for them, and re-layouts  2.74 us (2%)
    ppermute x7, waiting for transfers between devices, per_device(): front = lax.ppermute(outgoing, 'slab', sweep[step])  46.7 us
    all_to_all x1, blocking collectives, per_device(): lax.all_to_all(blocks, 'energy', split_axis=0, concat_axis=0, tiled=True)  36.9 us
    ppermute x3, waiting for transfers between devices, per_device(): composites[step] = lax.ppermute(part, 'slab', chains[step])  16.7 us
    ppermute x3, waiting for transfers between devices, per_device(): earlier = lax.ppermute(product, 'slab', products[step])  7.42 us
    ppermute x7, starting transfers between devices, per_device(): front = lax.ppermute(outgoing, 'slab', sweep[step])  5.46 us
    ppermute x3, starting transfers between devices, per_device(): earlier = lax.ppermute(product, 'slab', products[step])  4.64 us
    ppermute x3, starting transfers between devices, per_device(): composites[step] = lax.ppermute(part, 'slab', chains[step])  3.3 us
  transfers between devices with their start and end apart: 16, of which 4 were waited for; matrix products, arithmetic and copies ran while one was open for 0% of the time, Pallas kernels for 4%

profile of v5, /device:TPU:417, one launch (start us, length us, event | category | flops | bytes accessed | tf_op | source)
XLA Modules:
  0.0 137.2 jit_solution(4866276081152816138)
XLA Ops:
  0.6 0.7 collective-permute-start.1
  1.3 0.6 copy-done.2
  2.0 1.0 copy-done
  3.0 1.0 copy-done.4
  4.0 2.0 %shard_map.59 = (f32[256,512]{1,0:T(8,128)S(1)}, f32[256,512]{1,0:T(8,128)S(1)}, bf16[512,512]{1,0:T(8,128)(2,1)S(1)}) custom-call(f32[1,2]{1,0:T(1,128)S(1)} %copy-done.2, bf16[2,256,512]{2,1,0:T(8,128)(2,1)S(1)} %bitcast.2, bf16[2,256,512]{2,1,0:T(8,128)(2,1)S(1)} %bitcast.5), custom_call_target="tpu_custom_call" | custom-call | flops 1073741824 | bytes 4194304 | tf_op jit(solution)/shard_map/pallas_call | solution.py:302
  6.1 0.0 copy-start.1
  6.1 0.8 collective-permute-start
  6.9 0.7 collective-permute-start.2
  7.7 1.0 shard_map.60
  8.7 3.3 %collective-permute-start.4 = (f32[256,512]{1,0:T(8,128)S(1)}, f32[256,512]{1,0:T(8,128)S(1)}, u32[]{:S(2)}, u32[]{:S(2)}) collective-permute-start(f32[256,512]{1,0:T(8,128)S(1)} %get-tuple-element.48.joint), channel_id=1, source_target_pairs={{96,64},{192,160},{320,288},{416,384},{97,65},{193,161},{321,289},... | collective-permute-start | bytes 1572872 | tf_op jit(solution)/shard_map/ppermute | solution.py:330
  12.0 0.7 collective-permute-start.3
  12.7 7.4 %collective-permute-done.4.received = f32[256,512]{1,0:T(8,128)S(1)} collective-permute-done((f32[256,512]{1,0:T(8,128)S(1)}, f32[256,512]{1,0:T(8,128)S(1)}, u32[]{:S(2)}, u32[]{:S(2)}) %collective-permute-start.4) | collective-permute-done | bytes 524320 | tf_op jit(solution)/shard_map/ppermute | solution.py:330
  20.1 0.7 collective-permute-start.6
  20.9 1.3 collective-permute-start.7
  22.2 0.7 collective-permute-start.5
  23.0 0.7 collective-permute-start.9
  23.7 11.3 %collective-permute-done.7.refs_5_.rest_0_ = f32[256,512]{1,0:T(8,128)S(1)} collective-permute-done((f32[256,512]{1,0:T(8,128)S(1)}, f32[256,512]{1,0:T(8,128)S(1)}, u32[]{:S(2)}, u32[]{:S(2)}) %collective-permute-start.7) | collective-permute-done | bytes 524320 | tf_op jit(solution)/shard_map/ppermute | solution.py:328
  35.0 1.1 shard_map.70
  36.1 1.3 collective-permute-start.10
  37.5 0.7 collective-permute-start.8
  38.2 0.8 shard_map.69
  39.0 5.3 %collective-permute-done.10.refs_5_.rest_0_.refs_6_ = f32[256,512]{1,0:T(8,128)S(1)} collective-permute-done((f32[256,512]{1,0:T(8,128)S(1)}, f32[256,512]{1,0:T(8,128)S(1)}, u32[]{:S(2)}, u32[]{:S(2)}) %collective-permute-start.10) | collective-permute-done | bytes 524320 | tf_op jit(solution)/shard_map/ppermute | solution.py:328
  44.3 0.7 collective-permute-start.12
  45.1 0.7 collective-permute-start.11
  45.8 0.2 shard_map.74.refs_12_
  46.1 0.7 collective-permute-start.13
  46.8 0.7 collective-permute-start.14
  47.6 1.3 collective-permute-start.15
  48.9 46.7 %collective-permute-done.15.front = f32[256,512]{1,0:T(8,128)S(1)} collective-permute-done((f32[256,512]{1,0:T(8,128)S(1)}, f32[256,512]{1,0:T(8,128)S(1)}, u32[]{:S(2)}, u32[]{:S(2)}) %collective-permute-start.15) | collective-permute-done | bytes 524320 | tf_op jit(solution)/shard_map/ppermute | solution.py:326
  95.6 2.3 %shard_map.79 = f32[32,2,8,512]{3,2,1,0:T(8,128)S(1)} custom-call(f32[1,2]{1,0:T(1,128)S(1)} %copy-done.2, bf16[2,256,512]{2,1,0:T(8,128)(2,1)S(1)} %bitcast.4, bf16[512,512]{1,0:T(8,128)(2,1)S(1)} %get-tuple-element.40.form_first, f32[256,512]{1,0:T(8,128)S(1)} %get-tuple-element.41.first, f32[256,512]{1,0:T(8,128)S(1)} %get-tuple-element.42.value.refs_2_.local.refs_1_, ...), custom_call_target="tpu_custom_call" | custom-call | flops 1342177280 | bytes 4194304 | tf_op jit(solution)/shard_map/pallas_call | solution.py:379
  97.9 36.9 %all_to_all.5.blocks = f32[32,2,8,512]{3,2,1,0:T(8,128)S(1)} all-to-all(f32[32,2,8,512]{3,2,1,0:T(8,128)S(1)} %shard_map.79), channel_id=1, replica_groups=mesh['slab'=16,'energy'=32] {'energy'}, dimensions={0} | all-to-all | bytes 2097152 | tf_op jit(solution)/shard_map/all_to_all | solution.py:386
  134.8 2.2 %shard_map.80 = (f32[2,8,512]{2,1,0:T(8,128)}, f32[32,2,8,512]{3,2,1,0:T(8,128)}) custom-call(f32[32]{0:T(128)S(1)} %copy-done.3, f32[32,2,8,512]{3,2,1,0:T(8,128)S(1)} %all_to_all.5.blocks), custom_call_target="tpu_custom_call" | custom-call | tf_op jit(solution)/shard_map/pallas_call | solution.py:387
  (33 shorter events, 0.4 us)
Async XLA Ops:
  0.6 6.3 %collective-permute-start.1 = (f32[1,2]{1,0:T(1,128)}, f32[1,2]{1,0:T(1,128)S(1)}, u32[]{:S(2)}, u32[]{:S(2)}) collective-permute-start(f32[1,2]{1,0:T(1,128)} %coupling.5), channel_id=1, source_target_pairs={{0,32},{2,34},{4,36},{6,38},{8,40},{10,42},{12,44},{14,46},{16,48}... | collective-permute-start | bytes 32 | tf_op jit(solution)/shard_map/ppermute | solution.py:322
  1.3 0.7 copy-start.2
  2.0 1.0 copy-start
  3.0 1.0 copy-start.4
  6.1 1.6 %copy-start.1 = (bf16[1,2,256,512]{3,2,1,0:T(8,128)(2,1)S(1)}, bf16[1,2,256,512]{3,2,1,0:T(8,128)(2,1)}, u32[]{:S(2)}) copy-start(bf16[1,2,256,512]{3,2,1,0:T(8,128)(2,1)} %param.4) | copy-start | bytes 1572868
  6.1 5.9 %collective-permute-start = (f32[256,512]{1,0:T(8,128)S(1)}, f32[256,512]{1,0:T(8,128)S(1)}, u32[]{:S(2)}, u32[]{:S(2)}) collective-permute-start(f32[256,512]{1,0:T(8,128)S(1)} %get-tuple-element.42.value.refs_2_.local.refs_1_), channel_id=1, source_target_pairs={{1,33},{3,35},{5,37},{7,39},{9,41},{11,43},{13,45},{15,47},{17,49}... | collective-permute-start | bytes 1572872 | tf_op jit(solution)/shard_map/ppermute | solution.py:320
  6.9 5.0 %collective-permute-start.2 = (f32[256,512]{1,0:T(8,128)S(1)}, f32[256,512]{1,0:T(8,128)S(1)}, u32[]{:S(2)}, u32[]{:S(2)}) collective-permute-start(f32[256,512]{1,0:T(8,128)S(1)} %shard_map.61), channel_id=1, source_target_pairs={{0,32},{2,34},{4,36},{6,38},{8,40},{10,42},{12,44},{14,46},{16,48}... | collective-permute-start | bytes 1572872 | tf_op jit(solution)/shard_map/ppermute | solution.py:324
  8.7 11.5 %collective-permute-start.4 = (f32[256,512]{1,0:T(8,128)S(1)}, f32[256,512]{1,0:T(8,128)S(1)}, u32[]{:S(2)}, u32[]{:S(2)}) collective-permute-start(f32[256,512]{1,0:T(8,128)S(1)} %get-tuple-element.48.joint), channel_id=1, source_target_pairs={{96,64},{192,160},{320,288},{416,384},{97,65},{193,161},{321,289},... | collective-permute-start | bytes 1572872 | tf_op jit(solution)/shard_map/ppermute | solution.py:330
  12.0 10.1 %collective-permute-start.3 = (f32[256,512]{1,0:T(8,128)S(1)}, f32[256,512]{1,0:T(8,128)S(1)}, u32[]{:S(2)}, u32[]{:S(2)}) collective-permute-start(f32[256,512]{1,0:T(8,128)S(1)} %get-tuple-element.47), channel_id=1, source_target_pairs={{32,64},{33,65},{34,66},{35,67},{36,68},{37,69},{38,70},{39,71},{4... | collective-permute-start | bytes 1572872 | tf_op jit(solution)/shard_map/ppermute | solution.py:326
  20.1 2.8 %collective-permute-start.6 = (f32[256,512]{1,0:T(8,128)S(1)}, f32[256,512]{1,0:T(8,128)S(1)}, u32[]{:S(2)}, u32[]{:S(2)}) collective-permute-start(f32[256,512]{1,0:T(8,128)S(1)} %get-tuple-element.55), channel_id=1, source_target_pairs={{160,128},{288,256},{384,352},{161,129},{289,257},{385,353},{162,1... | collective-permute-start | bytes 1572872 | tf_op jit(solution)/shard_map/ppermute | solution.py:330
  20.9 14.1 %collective-permute-start.7 = (f32[256,512]{1,0:T(8,128)S(1)}, f32[256,512]{1,0:T(8,128)S(1)}, u32[]{:S(2)}, u32[]{:S(2)}) collective-permute-start(f32[256,512]{1,0:T(8,128)S(1)} %shard_map.66), channel_id=1, source_target_pairs={{96,128},{160,192},{256,288},{384,416},{97,129},{161,193},{257,289... | collective-permute-start | bytes 1572872 | tf_op jit(solution)/shard_map/ppermute | solution.py:328
  22.2 15.2 %collective-permute-start.5 = (f32[256,512]{1,0:T(8,128)S(1)}, f32[256,512]{1,0:T(8,128)S(1)}, u32[]{:S(2)}, u32[]{:S(2)}) collective-permute-start(f32[256,512]{1,0:T(8,128)S(1)} %get-tuple-element.54), channel_id=1, source_target_pairs={{64,128},{65,129},{66,130},{67,131},{68,132},{69,133},{70,134},{71... | collective-permute-start | bytes 1572872 | tf_op jit(solution)/shard_map/ppermute | solution.py:326
  23.0 15.2 %collective-permute-start.9 = (f32[256,512]{1,0:T(8,128)S(1)}, f32[256,512]{1,0:T(8,128)S(1)}, u32[]{:S(2)}, u32[]{:S(2)}) collective-permute-start(f32[256,512]{1,0:T(8,128)S(1)} %get-tuple-element.62), channel_id=1, source_target_pairs={{256,224},{257,225},{258,226},{259,227},{260,228},{261,229},{262,2... | collective-permute-start | bytes 1572872 | tf_op jit(solution)/shard_map/ppermute | solution.py:330
  36.1 8.2 %collective-permute-start.10 = (f32[256,512]{1,0:T(8,128)S(1)}, f32[256,512]{1,0:T(8,128)S(1)}, u32[]{:S(2)}, u32[]{:S(2)}) collective-permute-start(f32[256,512]{1,0:T(8,128)S(1)} %shard_map.70), channel_id=1, source_target_pairs={{192,224},{288,320},{416,448},{193,225},{289,321},{417,449},{194,2... | collective-permute-start | bytes 1572872 | tf_op jit(solution)/shard_map/ppermute | solution.py:328
  37.5 7.6 %collective-permute-start.8 = (f32[256,512]{1,0:T(8,128)S(1)}, f32[256,512]{1,0:T(8,128)S(1)}, u32[]{:S(2)}, u32[]{:S(2)}) collective-permute-start(f32[256,512]{1,0:T(8,128)S(1)} %get-tuple-element.61), channel_id=1, source_target_pairs={{64,96},{128,224},{65,97},{129,225},{66,98},{130,226},{67,99},{131... | collective-permute-start | bytes 1572872 | tf_op jit(solution)/shard_map/ppermute | solution.py:326
  44.3 1.7 %collective-permute-start.12 = (f32[256,512]{1,0:T(8,128)S(1)}, f32[256,512]{1,0:T(8,128)S(1)}, u32[]{:S(2)}, u32[]{:S(2)}) collective-permute-start(f32[256,512]{1,0:T(8,128)S(1)} %shard_map.73), channel_id=1, source_target_pairs={{320,352},{321,353},{322,354},{323,355},{324,356},{325,357},{326,3... | collective-permute-start | bytes 1572872 | tf_op jit(solution)/shard_map/ppermute | solution.py:328
  45.1 0.9 collective-permute-start.11
  46.1 0.7 collective-permute-start.13
  46.8 0.7 collective-permute-start.14
  47.6 48.0 %collective-permute-start.15 = (f32[256,512]{1,0:T(8,128)S(1)}, f32[256,512]{1,0:T(8,128)S(1)}, u32[]{:S(2)}, u32[]{:S(2)}) collective-permute-start(f32[256,512]{1,0:T(8,128)S(1)} %get-tuple-element.74), channel_id=1, source_target_pairs={{288,320},{384,416},{289,321},{385,417},{290,322},{386,418},{291,3... | collective-permute-start | bytes 1572872 | tf_op jit(solution)/shard_map/ppermute | solution.py:326
  97.9 36.9 %copy-start.3 = (f32[32]{0:T(128)S(1)}, f32[32]{0:T(128)}, u32[]{:S(2)}) copy-start(f32[32]{0:T(128)} %weights.1) | copy-start | bytes 388

commit v6 on v5

--- a/solution.py
+++ b/solution.py
@@ -58,11 +58,11 @@
 
 def source_kernel(coupling, green, sigma, local, first, form_first):
     half = green.shape[1]
-    lead, follow = coupling[0, 0], coupling[0, 1]
+    lead, follow = coupling[:, 0:1], coupling[:, 1:2]
     green_first, green_second = green[0], green[1]
     form = dagger_form(green_first)
     form_first[...] = form
-    contact = jnp.where(lax.axis_index("slab") == 0, lead * lead, 0.0)
+    contact = (lead * lead) * (lax.axis_index("slab") == 0).astype(F32)
     turned = jnp.concatenate(
         [-green_first[:, half:].astype(F32), green_first[:, :half].astype(F32)], axis=1
     )
@@ -74,7 +74,7 @@
 
 
 def joint_kernel(coupling, green, joint, high, low, form_high, form_low):
-    whole = (coupling[0, 0] * coupling[0, 1]) * dot(green[1], expanded(green[0]))
+    whole = (coupling[:, 0:1] * coupling[:, 1:2]) * dot(green[1], expanded(green[0]))
     joint[...] = whole
     part_high, part_low = split(whole)
     high[...], low[...] = part_high, part_low
@@ -161,11 +161,17 @@
         out[...] = local[...] + sandwich(high, low, form_high, form_low, state[...])
 
 
-def join_kernel(places, heads, received, joint, product, *forms):
-    @pl.when(takes_part(places))
-    def _():
-        first_high, first_low = split(received[...])
-        product[...] = product_wide(first_high, first_low, joint[...])
+def join_kernel(places, heads, count, *refs):
+    arrived, (joint, product, *forms) = refs[:count], refs[count:]
+    for core, received in enumerate(arrived):
+        mine = takes_part(places)
+        if count > 1:
+            mine = mine & (lax.axis_index("energy") % 2 != core)
+
+        @pl.when(mine)
+        def _(received=received):
+            first_high, first_low = split(received[...])
+            product[...] = product_wide(first_high, first_low, joint[...])
 
     if heads:
 
@@ -192,7 +198,7 @@
         state[...] = state_in[...]
 
     rows = out.shape[2]
-    lead = coupling[0, 0]
+    lead = coupling[:, 0:1]
     value = state[...]
     block = first[...] + (lead * lead) * right_narrow(
         product_narrow(green[0], value), form_first[...]
@@ -215,15 +221,15 @@
     ]
     for copy in copies:
         copy.start()
-    total = weights[0] * blocks[0]
+    total = weights[0:1, 0:1] * blocks[0]
     for level in range(1, blocks.shape[0]):
-        total = total + weights[level] * blocks[level]
+        total = total + weights[level : level + 1, 0:1] * blocks[level]
     out[...] = total
     for copy in copies:
         copy.wait()
 
 
-VMEM, SMEM = pl.BlockSpec(memory_space=pltpu.VMEM), pl.BlockSpec(memory_space=pltpu.SMEM)
+VMEM = pl.BlockSpec(memory_space=pltpu.VMEM)
 ANY = pl.BlockSpec(memory_space=pl.ANY)
 
 
@@ -300,10 +306,10 @@
     assert sum(GROUPS) == slabs
 
     local, first, form_first = call(
-        source_kernel, [SMEM, VMEM, VMEM], [wide, wide, form], 8 * cost
+        source_kernel, [VMEM, VMEM, VMEM], [wide, wide, form], 8 * cost
     )(coupling, green, sigma)
     joint, high, low, form_high, form_low = call(
-        joint_kernel, [SMEM, VMEM], [wide, narrow, narrow, form, form], cost
+        joint_kernel, [VMEM, VMEM], [wide, narrow, narrow, form, form], cost
     )(coupling, green)
     heads, tails, chains, products, sweep, roles = plan(GROUPS)
     group_of = {head: k for k, head in enumerate(heads)}
@@ -320,13 +326,19 @@
             front = lax.ppermute(local, ("slab", "energy"), of_cores(pairs, levels, 1))
             partner = [(slab, slab ^ 1) for slab in range(slabs)]
             token = lax.ppermute(coupling, ("slab", "energy"), of_cores(partner, levels, 0))
+            token = lax.ppermute(token, ("slab", "energy"), of_cores(partner, levels, 0))
             turned = call(turn_kernel, [VMEM] * 2, wide, 0)(token, local)
             late = lax.ppermute(turned, ("slab", "energy"), of_cores(pairs, levels, 0))
         else:
             front = lax.ppermute(outgoing, "slab", sweep[step])
         if 1 < step < len(chains):
             composites[step] = lax.ppermute(part, "slab", chains[step])
-        if step < len(products):
+        if step == 1:
+            pairs = products[1]
+            earlier = lax.ppermute(product, ("slab", "energy"), of_cores(pairs, levels, 1))
+            turned = call(turn_kernel, [VMEM] * 2, wide, 0)(token, product)
+            later = lax.ppermute(turned, ("slab", "energy"), of_cores(pairs, levels, 0))
+        elif step < len(products):
             earlier = lax.ppermute(product, "slab", products[step])
         if role["after"]:
             after = call(functools.partial(after_kernel, role["after"]), [VMEM] * 6, wide, 6 * cost)(
@@ -344,11 +356,11 @@
             places = [target for _, target in products[step]]
             ready = [place for place in places if place in heads]
             product, *forms = call(
-                functools.partial(join_kernel, places, ready),
-                [VMEM] * 2,
+                functools.partial(join_kernel, places, ready, 2 if step == 1 else 1),
+                [VMEM] * (3 if step == 1 else 2),
                 [wide] + [narrow, narrow, form, form] * bool(ready),
                 3 * cost,
-            )(earlier, joint)
+            )(*([earlier, later] if step == 1 else [earlier]), joint)
             whole_forms.update({place: forms for place in ready})
         inputs = {"front": front}
         if step == 1:
@@ -375,10 +387,11 @@
             aliases,
         )(*inputs.values())
 
+    weights = jnp.broadcast_to(energy_weights[:, None], (levels, 128))
     rows = half // levels
     blocks = call(
         functools.partial(last_kernel, role["keep"]),
-        [SMEM] + [VMEM] * 10,
+        [VMEM] * 11,
         jax.ShapeDtypeStruct((levels, 2, rows, width), F32),
         10 * cost,
         scratch=[pltpu.VMEM((half, width), F32)],
@@ -386,7 +399,7 @@
     block_rows = lax.all_to_all(blocks, "energy", split_axis=0, concat_axis=0, tiled=True)
     density, lesser = pl.pallas_call(
         density_kernel,
-        in_specs=[SMEM, VMEM],
+        in_specs=[VMEM, VMEM],
         out_specs=[VMEM, ANY],
         out_shape=[
             jax.ShapeDtypeStruct((2, rows, width), F32),
@@ -394,7 +407,7 @@
         ],
         scratch_shapes=[pltpu.SemaphoreType.DMA((min(8, levels),))],
         compiler_params=pltpu.CompilerParams(vmem_limit_bytes=VMEM_BYTES),
-    )(energy_weights, block_rows)
+    )(weights, block_rows)
     return lesser, density
 
 

time: 138 us -> 129 us (0.935)
  waiting for transfers between devices: 70.8 us -> 61.8 us
  Pallas kernels: 9.93 us -> 7.57 us
    ppermute x3 -> x2, waiting for transfers between devices: 7.42 us -> 0.01 us  [per_device(): earlier = lax.ppermute(product, 'slab', products[step])]
    ppermute x0 -> x3, starting transfers between devices: none -> 4.62 us  [the longest x1 3.27 us: per_device(): lax.ppermute(product, ('slab', 'energy'), of_cores(pairs, levels, 1))]
    ppermute x3, waiting for transfers between devices: 16.7 us -> 12.7 us  [per_device(): composites[step] = lax.ppermute(part, 'slab', chains[step])]
    ppermute x3 -> x2, starting transfers between devices: 4.64 us -> 1.38 us  [per_device(): earlier = lax.ppermute(product, 'slab', products[step])]
    ppermute x0 -> x3, waiting for transfers between devices: none -> 3.25 us  [the longest x1 3.24 us: per_device(): lax.ppermute(product, ('slab', 'energy'), of_cores(pairs, levels, 1))]
    pallas_call x7 -> x8, Pallas kernels: 8.36 us -> 6.22 us  [the longest x1 1.76 us: per_device(): call(functools.partial(last_kernel, role['keep']), [VMEM] * 11, jax.Shape...]
  transfers between devices with their start and end apart: 16 -> 18, of which waited for: 4 -> 4; matrix products, arithmetic and copies ran while one was open for 0% -> 0% of each run, Pallas kernels for 4% -> 3%
where the time goes in v6:
time: 129 us; the launch traced here: 128 us
  waiting for transfers between devices  61.8 us (48%)
  blocking collectives  38.1 us (30%)
  starting transfers between devices  16.9 us (13%)
  Pallas kernels  7.57 us (6%)
  local copies, waits for them, and re-layouts  2.81 us (2%)
    ppermute x7, waiting for transfers between devices, per_device(): front = lax.ppermute(outgoing, 'slab', sweep[step])  45.9 us
    all_to_all x1, blocking collectives, per_device(): lax.all_to_all(blocks, 'energy', split_axis=0, concat_axis=0, tiled=True)  38.1 us
    ppermute x3, waiting for transfers between devices, per_device(): composites[step] = lax.ppermute(part, 'slab', chains[step])  12.7 us
    ppermute x7, starting transfers between devices, per_device(): front = lax.ppermute(outgoing, 'slab', sweep[step])  5.45 us
    ppermute x3, starting transfers between devices, per_device(): composites[step] = lax.ppermute(part, 'slab', chains[step])  3.3 us
    ppermute x1, starting transfers between devices, per_device(): lax.ppermute(product, ('slab', 'energy'), of_cores(pairs, levels, 1))  3.27 us
    ppermute x1, waiting for transfers between devices, per_device(): lax.ppermute(product, ('slab', 'energy'), of_cores(pairs, levels, 1))  3.24 us
    unnamed x10, local copies, waits for them, and re-layouts  2.74 us
  transfers between devices with their start and end apart: 18, of which 4 were waited for; matrix products, arithmetic and copies ran while one was open for 0% of the time, Pallas kernels for 3%

profile of v6, /device:TPU:417, one launch (start us, length us, event | category | flops | bytes accessed | tf_op | source)
XLA Modules:
  0.0 128.5 jit_solution(12724030176994777035)
XLA Ops:
  0.6 0.7 collective-permute-start.1
  1.3 0.6 copy-done.2
  2.0 1.0 copy-done
  3.0 1.0 copy-done.3
  4.0 1.5 %shard_map.59 = (f32[256,512]{1,0:T(8,128)S(1)}, f32[256,512]{1,0:T(8,128)S(1)}, bf16[512,512]{1,0:T(8,128)(2,1)S(1)}) custom-call(f32[1,2]{1,0:T(1,128)S(1)} %copy-done.2, bf16[2,256,512]{2,1,0:T(8,128)(2,1)S(1)} %bitcast.2, bf16[2,256,512]{2,1,0:T(8,128)(2,1)S(1)} %bitcast.5), custom_call_target="tpu_custom_call" | custom-call | flops 1073741824 | bytes 4194304 | tf_op jit(solution)/shard_map/pallas_call | solution.py:308
  5.5 0.8 collective-permute-start
  6.4 0.7 collective-permute-start.2
  7.1 0.7 collective-permute-start.3
  7.8 0.5 shard_map.60
  8.3 3.3 %collective-permute-start.5 = (f32[256,512]{1,0:T(8,128)S(1)}, f32[256,512]{1,0:T(8,128)S(1)}, u32[]{:S(2)}, u32[]{:S(2)}) collective-permute-start(f32[256,512]{1,0:T(8,128)S(1)} %get-tuple-element.48.value.refs_2_.refs_1_), channel_id=1, source_target_pairs={{97,65},{99,67},{101,69},{103,71},{105,73},{107,75},{109,77},{111,... | collective-permute-start | bytes 1572872 | tf_op jit(solution)/shard_map/ppermute | solution.py:338
  11.6 0.7 collective-permute-start.6
  12.4 0.7 collective-permute-start.4
  13.1 1.3 %collective-permute-start.9 = (f32[256,512]{1,0:T(8,128)S(1)}, f32[256,512]{1,0:T(8,128)S(1)}, u32[]{:S(2)}, u32[]{:S(2)}) collective-permute-start(f32[256,512]{1,0:T(8,128)S(1)} %shard_map.67), channel_id=1, source_target_pairs={{96,128},{160,192},{256,288},{384,416},{97,129},{161,193},{257,289... | collective-permute-start | bytes 1572872 | tf_op jit(solution)/shard_map/ppermute | solution.py:335
  14.4 3.2 %collective-permute-done.5.refs_0_ = f32[256,512]{1,0:T(8,128)S(1)} collective-permute-done((f32[256,512]{1,0:T(8,128)S(1)}, f32[256,512]{1,0:T(8,128)S(1)}, u32[]{:S(2)}, u32[]{:S(2)}) %collective-permute-start.5) | collective-permute-done | bytes 524320 | tf_op jit(solution)/shard_map/ppermute | solution.py:338
  17.6 0.7 collective-permute-start.8
  18.4 0.7 collective-permute-start.7
  19.1 8.1 %collective-permute-done.9.refs_5_.rest_0_ = f32[256,512]{1,0:T(8,128)S(1)} collective-permute-done((f32[256,512]{1,0:T(8,128)S(1)}, f32[256,512]{1,0:T(8,128)S(1)}, u32[]{:S(2)}, u32[]{:S(2)}) %collective-permute-start.9) | collective-permute-done | bytes 524320 | tf_op jit(solution)/shard_map/ppermute | solution.py:335
  27.2 1.1 shard_map.71
  28.3 1.3 %collective-permute-start.12 = (f32[256,512]{1,0:T(8,128)S(1)}, f32[256,512]{1,0:T(8,128)S(1)}, u32[]{:S(2)}, u32[]{:S(2)}) collective-permute-start(f32[256,512]{1,0:T(8,128)S(1)} %shard_map.71), channel_id=1, source_target_pairs={{192,224},{288,320},{416,448},{193,225},{289,321},{417,449},{194,2... | collective-permute-start | bytes 1572872 | tf_op jit(solution)/shard_map/ppermute | solution.py:335
  29.7 0.7 collective-permute-start.11
  30.4 0.7 collective-permute-start.10
  31.1 4.6 %collective-permute-done.12.refs_5_.rest_0_.refs_6_ = f32[256,512]{1,0:T(8,128)S(1)} collective-permute-done((f32[256,512]{1,0:T(8,128)S(1)}, f32[256,512]{1,0:T(8,128)S(1)}, u32[]{:S(2)}, u32[]{:S(2)}) %collective-permute-start.12) | collective-permute-done | bytes 524320 | tf_op jit(solution)/shard_map/ppermute | solution.py:335
  35.7 0.7 collective-permute-start.14
  36.4 0.8 shard_map.70
  37.2 0.7 collective-permute-start.13
  38.0 0.7 collective-permute-start.15
  38.8 0.7 collective-permute-start.16
  39.5 1.3 %collective-permute-start.17 = (f32[256,512]{1,0:T(8,128)S(1)}, f32[256,512]{1,0:T(8,128)S(1)}, u32[]{:S(2)}, u32[]{:S(2)}) collective-permute-start(f32[256,512]{1,0:T(8,128)S(1)} %get-tuple-element.74), channel_id=1, source_target_pairs={{288,320},{384,416},{289,321},{385,417},{290,322},{386,418},{291,3... | collective-permute-start | bytes 1572872 | tf_op jit(solution)/shard_map/ppermute | solution.py:333
  40.8 45.9 %collective-permute-done.17.front = f32[256,512]{1,0:T(8,128)S(1)} collective-permute-done((f32[256,512]{1,0:T(8,128)S(1)}, f32[256,512]{1,0:T(8,128)S(1)}, u32[]{:S(2)}, u32[]{:S(2)}) %collective-permute-start.17) | collective-permute-done | bytes 524320 | tf_op jit(solution)/shard_map/ppermute | solution.py:333
  86.7 1.8 %shard_map.80 = f32[32,2,8,512]{3,2,1,0:T(8,128)S(1)} custom-call(f32[1,2]{1,0:T(1,128)S(1)} %copy-done.2, bf16[2,256,512]{2,1,0:T(8,128)(2,1)S(1)} %bitcast.4, bf16[512,512]{1,0:T(8,128)(2,1)S(1)} %get-tuple-element.40.form_first, f32[256,512]{1,0:T(8,128)S(1)} %get-tuple-element.41.first, f32[256,512]{1,0:T(8,128)S(1)} %get-tuple-element.42.value.refs_2_.local.refs_1_, ...), custom_call_target="tpu_custom_call" | custom-call | flops 1342177280 | bytes 4194304 | tf_op jit(solution)/shard_map/pallas_call | solution.py:392
  88.5 38.1 %all_to_all.5.blocks = f32[32,2,8,512]{3,2,1,0:T(8,128)S(1)} all-to-all(f32[32,2,8,512]{3,2,1,0:T(8,128)S(1)} %shard_map.80), channel_id=1, replica_groups=mesh['slab'=16,'energy'=32] {'energy'}, dimensions={0} | all-to-all | bytes 2097152 | tf_op jit(solution)/shard_map/all_to_all | solution.py:399
  126.7 1.7 %shard_map.81 = (f32[2,8,512]{2,1,0:T(8,128)}, f32[32,2,8,512]{3,2,1,0:T(8,128)}) custom-call(f32[32,128]{1,0:T(8,128)S(1)} %broadcast_in_dim.2.weights, f32[32,2,8,512]{3,2,1,0:T(8,128)S(1)} %all_to_all.5.blocks), custom_call_target="tpu_custom_call" | custom-call | tf_op jit(solution)/shard_map/pallas_call | solution.py:400
  (39 shorter events, 0.4 us)
Async XLA Ops:
  0.6 5.7 %collective-permute-start.1 = (f32[1,2]{1,0:T(1,128)}, f32[1,2]{1,0:T(1,128)S(1)}, u32[]{:S(2)}, u32[]{:S(2)}) collective-permute-start(f32[1,2]{1,0:T(1,128)} %coupling.5), channel_id=1, source_target_pairs={{0,32},{2,34},{4,36},{6,38},{8,40},{10,42},{12,44},{14,46},{16,48}... | collective-permute-start | bytes 32 | tf_op jit(solution)/shard_map/ppermute | solution.py:328
  1.3 0.7 copy-start.2
  2.0 1.0 copy-start
  3.0 1.0 copy-start.3
  5.5 2.3 %copy-start.1 = (bf16[1,2,256,512]{3,2,1,0:T(8,128)(2,1)S(1)}, bf16[1,2,256,512]{3,2,1,0:T(8,128)(2,1)}, u32[]{:S(2)}) copy-start(bf16[1,2,256,512]{3,2,1,0:T(8,128)(2,1)} %param.4) | copy-start | bytes 1572868
  5.5 6.8 %collective-permute-start = (f32[256,512]{1,0:T(8,128)S(1)}, f32[256,512]{1,0:T(8,128)S(1)}, u32[]{:S(2)}, u32[]{:S(2)}) collective-permute-start(f32[256,512]{1,0:T(8,128)S(1)} %get-tuple-element.42.value.refs_2_.local.refs_1_), channel_id=1, source_target_pairs={{1,33},{3,35},{5,37},{7,39},{9,41},{11,43},{13,45},{15,47},{17,49}... | collective-permute-start | bytes 1572872 | tf_op jit(solution)/shard_map/ppermute | solution.py:326
  6.4 0.7 collective-permute-start.2
  7.1 5.2 %collective-permute-start.3 = (f32[256,512]{1,0:T(8,128)S(1)}, f32[256,512]{1,0:T(8,128)S(1)}, u32[]{:S(2)}, u32[]{:S(2)}) collective-permute-start(f32[256,512]{1,0:T(8,128)S(1)} %shard_map.61), channel_id=1, source_target_pairs={{0,32},{2,34},{4,36},{6,38},{8,40},{10,42},{12,44},{14,46},{16,48}... | collective-permute-start | bytes 1572872 | tf_op jit(solution)/shard_map/ppermute | solution.py:331
  8.3 9.4 %collective-permute-start.5 = (f32[256,512]{1,0:T(8,128)S(1)}, f32[256,512]{1,0:T(8,128)S(1)}, u32[]{:S(2)}, u32[]{:S(2)}) collective-permute-start(f32[256,512]{1,0:T(8,128)S(1)} %get-tuple-element.48.value.refs_2_.refs_1_), channel_id=1, source_target_pairs={{97,65},{99,67},{101,69},{103,71},{105,73},{107,75},{109,77},{111,... | collective-permute-start | bytes 1572872 | tf_op jit(solution)/shard_map/ppermute | solution.py:338
  11.6 6.1 %collective-permute-start.6 = (f32[256,512]{1,0:T(8,128)S(1)}, f32[256,512]{1,0:T(8,128)S(1)}, u32[]{:S(2)}, u32[]{:S(2)}) collective-permute-start(f32[256,512]{1,0:T(8,128)S(1)} %shard_map.63), channel_id=1, source_target_pairs={{96,64},{98,66},{100,68},{102,70},{104,72},{106,74},{108,76},{110,... | collective-permute-start | bytes 1572872 | tf_op jit(solution)/shard_map/ppermute | solution.py:340
  12.4 6.0 %collective-permute-start.4 = (f32[256,512]{1,0:T(8,128)S(1)}, f32[256,512]{1,0:T(8,128)S(1)}, u32[]{:S(2)}, u32[]{:S(2)}) collective-permute-start(f32[256,512]{1,0:T(8,128)S(1)} %get-tuple-element.47), channel_id=1, source_target_pairs={{32,64},{33,65},{34,66},{35,67},{36,68},{37,69},{38,70},{39,71},{4... | collective-permute-start | bytes 1572872 | tf_op jit(solution)/shard_map/ppermute | solution.py:333
  13.1 14.1 %collective-permute-start.9 = (f32[256,512]{1,0:T(8,128)S(1)}, f32[256,512]{1,0:T(8,128)S(1)}, u32[]{:S(2)}, u32[]{:S(2)}) collective-permute-start(f32[256,512]{1,0:T(8,128)S(1)} %shard_map.67), channel_id=1, source_target_pairs={{96,128},{160,192},{256,288},{384,416},{97,129},{161,193},{257,289... | collective-permute-start | bytes 1572872 | tf_op jit(solution)/shard_map/ppermute | solution.py:335
  17.6 12.0 %collective-permute-start.8 = (f32[256,512]{1,0:T(8,128)S(1)}, f32[256,512]{1,0:T(8,128)S(1)}, u32[]{:S(2)}, u32[]{:S(2)}) collective-permute-start(f32[256,512]{1,0:T(8,128)S(1)} %get-tuple-element.55), channel_id=1, source_target_pairs={{160,128},{288,256},{384,352},{161,129},{289,257},{385,353},{162,1... | collective-permute-start | bytes 1572872 | tf_op jit(solution)/shard_map/ppermute | solution.py:342
  18.4 12.0 %collective-permute-start.7 = (f32[256,512]{1,0:T(8,128)S(1)}, f32[256,512]{1,0:T(8,128)S(1)}, u32[]{:S(2)}, u32[]{:S(2)}) collective-permute-start(f32[256,512]{1,0:T(8,128)S(1)} %get-tuple-element.54), channel_id=1, source_target_pairs={{64,128},{65,129},{66,130},{67,131},{68,132},{69,133},{70,134},{71... | collective-permute-start | bytes 1572872 | tf_op jit(solution)/shard_map/ppermute | solution.py:333
  28.3 7.4 %collective-permute-start.12 = (f32[256,512]{1,0:T(8,128)S(1)}, f32[256,512]{1,0:T(8,128)S(1)}, u32[]{:S(2)}, u32[]{:S(2)}) collective-permute-start(f32[256,512]{1,0:T(8,128)S(1)} %shard_map.71), channel_id=1, source_target_pairs={{192,224},{288,320},{416,448},{193,225},{289,321},{417,449},{194,2... | collective-permute-start | bytes 1572872 | tf_op jit(solution)/shard_map/ppermute | solution.py:335
  29.7 6.7 %collective-permute-start.11 = (f32[256,512]{1,0:T(8,128)S(1)}, f32[256,512]{1,0:T(8,128)S(1)}, u32[]{:S(2)}, u32[]{:S(2)}) collective-permute-start(f32[256,512]{1,0:T(8,128)S(1)} %get-tuple-element.62), channel_id=1, source_target_pairs={{256,224},{257,225},{258,226},{259,227},{260,228},{261,229},{262,2... | collective-permute-start | bytes 1572872 | tf_op jit(solution)/shard_map/ppermute | solution.py:342
  30.4 6.8 %collective-permute-start.10 = (f32[256,512]{1,0:T(8,128)S(1)}, f32[256,512]{1,0:T(8,128)S(1)}, u32[]{:S(2)}, u32[]{:S(2)}) collective-permute-start(f32[256,512]{1,0:T(8,128)S(1)} %get-tuple-element.61), channel_id=1, source_target_pairs={{64,96},{128,224},{65,97},{129,225},{66,98},{130,226},{67,99},{131... | collective-permute-start | bytes 1572872 | tf_op jit(solution)/shard_map/ppermute | solution.py:333
  35.7 2.2 %collective-permute-start.14 = (f32[256,512]{1,0:T(8,128)S(1)}, f32[256,512]{1,0:T(8,128)S(1)}, u32[]{:S(2)}, u32[]{:S(2)}) collective-permute-start(f32[256,512]{1,0:T(8,128)S(1)} %shard_map.74), channel_id=1, source_target_pairs={{320,352},{321,353},{322,354},{323,355},{324,356},{325,357},{326,3... | collective-permute-start | bytes 1572872 | tf_op jit(solution)/shard_map/ppermute | solution.py:335
  37.2 0.7 collective-permute-start.13
  38.0 0.7 collective-permute-start.15
  38.8 0.7 collective-permute-start.16
  39.5 47.2 %collective-permute-start.17 = (f32[256,512]{1,0:T(8,128)S(1)}, f32[256,512]{1,0:T(8,128)S(1)}, u32[]{:S(2)}, u32[]{:S(2)}) collective-permute-start(f32[256,512]{1,0:T(8,128)S(1)} %get-tuple-element.74), channel_id=1, source_target_pairs={{288,320},{384,416},{289,321},{385,417},{290,322},{386,418},{291,3... | collective-permute-start | bytes 1572872 | tf_op jit(solution)/shard_map/ppermute | solution.py:333
  88.5 38.2 %copy-start.4 = (f32[32]{0:T(128)S(1)}, f32[32]{0:T(128)}, u32[]{:S(2)}) copy-start(f32[32]{0:T(128)} %param.7) | copy-start | bytes 388

commit v7 on v6

--- a/solution.py
+++ b/solution.py
@@ -140,7 +140,13 @@
         def _():
             state[...] = front[...] + ref["held"][...]
 
-    onward = roles["enter"] + roles["end"]
+    if roles["beside"]:
+
+        @pl.when(takes_part(roles["beside"]))
+        def _():
+            state[...] = ref["inner"][...]
+
+    onward = roles["enter"] + roles["end"] + roles["beside"]
     if onward:
 
         @pl.when(takes_part(onward))
@@ -153,6 +159,12 @@
         @pl.when(takes_part(beyond))
         def _():
             ref["out"][...] = sandwich(*whole_forms, state[...])
+
+    if roles["both"]:
+
+        @pl.when(takes_part(roles["both"]))
+        def _():
+            ref["inner_out"][...] = ref["local"][...] + sandwich(*forms, state[...])
 
 
 def after_kernel(places, local, high, low, form_high, form_low, state, out):
@@ -254,7 +266,7 @@
     ]
 
 
-ROLES = ("enter", "lead", "skip", "end", "keep", "after")
+ROLES = ("enter", "lead", "skip", "end", "keep", "after", "both", "beside")
 
 
 def plan(sizes):
@@ -288,10 +300,17 @@
             for i in range(1, size):
                 products[i].append((tail - i + 1, tail - i))
             move(arrive[k] + 1, head, heads[k + 1], "skip" if k + 1 < groups - 1 else "end")
-            roles[arrive[k] + 1]["after"].append(head)
+            if k == groups - 2 and size > 2:
+                roles[arrive[k]]["both"].append(head)
+            else:
+                roles[arrive[k] + 1]["after"].append(head)
+        together = k == groups - 2 and size > 2
         for i in range(1, size):
+            if together and i == 1:
+                roles[arrive[k] + 1]["beside"].append(head + 1)
+                continue
             role = "enter" if head + i < tail else "keep"
-            move(arrive[k] + middle + i, head + i - 1, head + i, role)
+            move(arrive[k] + (middle and not together) + i, head + i - 1, head + i, role)
     return heads, tails, chains, products, sweep, roles
 
 
@@ -365,7 +384,9 @@
         inputs = {"front": front}
         if step == 1:
             inputs["late"] = late
-        if role["enter"] or role["end"]:
+        if role["beside"]:
+            inputs["inner"] = inner
+        if role["enter"] or role["end"] or role["both"] or role["beside"]:
             inputs.update(shared)
         for place in role["skip"] + role["lead"]:
             for name, value in zip(("high", "low", "form_high", "form_low"), whole_forms[place]):
@@ -379,13 +400,17 @@
         if role["after"]:
             aliases[len(inputs)] = 0
             inputs["after"] = after
-        outgoing, state = call(
-            functools.partial(step_kernel, role, tuple(inputs) + ("out", "state_out")),
+        outputs = ("out", "state_out") + ("inner_out",) * bool(role["both"])
+        outgoing, state, *inside = call(
+            functools.partial(step_kernel, role, tuple(inputs) + outputs),
             [VMEM] * len(inputs),
-            [wide, wide],
+            [wide] * len(outputs),
             6 * cost,
             aliases,
         )(*inputs.values())
+        if role["both"]:
+            (place,) = role["both"]
+            inner = lax.ppermute(inside[0], "slab", [(place, place + 1)])
 
     weights = jnp.broadcast_to(energy_weights[:, None], (levels, 128))
     rows = half // levels

time: 129 us -> 128 us (level)
  transfers between devices with their start and end apart: 18 -> 19, of which waited for: 4 -> 4; matrix products, arithmetic and copies ran while one was open for 0% -> 0% of each run, Pallas kernels for 3% -> 3%
where the time goes in v7:
time: 128 us
  waiting for transfers between devices  60.9 us (48%)
  blocking collectives  37.6 us (29%)
  starting transfers between devices  17.6 us (14%)
  Pallas kernels  7.56 us (6%)
  local copies, waits for them, and re-layouts  2.81 us (2%)
    ppermute x7, waiting for transfers between devices, per_device(): front = lax.ppermute(outgoing, 'slab', sweep[step])  45 us
    all_to_all x1, blocking collectives, per_device(): lax.all_to_all(blocks, 'energy', split_axis=0, concat_axis=0, tiled=True)  37.6 us
    ppermute x3, waiting for transfers between devices, per_device(): composites[step] = lax.ppermute(part, 'slab', chains[step])  12.7 us
    ppermute x7, starting transfers between devices, per_device(): front = lax.ppermute(outgoing, 'slab', sweep[step])  5.45 us
    ppermute x3, starting transfers between devices, per_device(): composites[step] = lax.ppermute(part, 'slab', chains[step])  3.3 us
    ppermute x1, starting transfers between devices, per_device(): lax.ppermute(product, ('slab', 'energy'), of_cores(pairs, levels, 1))  3.26 us
    ppermute x1, waiting for transfers between devices, per_device(): lax.ppermute(product, ('slab', 'energy'), of_cores(pairs, levels, 1))  3.24 us
    unnamed x10, local copies, waits for them, and re-layouts  2.74 us
  transfers between devices with their start and end apart: 19, of which 4 were waited for; matrix products, arithmetic and copies ran while one was open for 0% of the time, Pallas kernels for 3%

profile of v7, /device:TPU:417, one launch (start us, length us, event | category | flops | bytes accessed | tf_op | source)
XLA Modules:
  0.0 127.7 jit_solution(1488924520286407242)
XLA Ops:
  0.6 0.7 collective-permute-start.1
  1.3 0.6 copy-done.2
  2.0 1.0 copy-done
  3.0 1.0 copy-done.3
  4.0 1.5 %shard_map.59 = (f32[256,512]{1,0:T(8,128)S(1)}, f32[256,512]{1,0:T(8,128)S(1)}, bf16[512,512]{1,0:T(8,128)(2,1)S(1)}) custom-call(f32[1,2]{1,0:T(1,128)S(1)} %copy-done.2, bf16[2,256,512]{2,1,0:T(8,128)(2,1)S(1)} %bitcast.2, bf16[2,256,512]{2,1,0:T(8,128)(2,1)S(1)} %bitcast.5), custom_call_target="tpu_custom_call" | custom-call | flops 1073741824 | bytes 4194304 | tf_op jit(solution)/shard_map/pallas_call | solution.py:327
  5.5 0.8 collective-permute-start
  6.4 0.7 collective-permute-start.2
  7.1 0.7 collective-permute-start.3
  8.3 3.3 %collective-permute-start.5 = (f32[256,512]{1,0:T(8,128)S(1)}, f32[256,512]{1,0:T(8,128)S(1)}, u32[]{:S(2)}, u32[]{:S(2)}) collective-permute-start(f32[256,512]{1,0:T(8,128)S(1)} %get-tuple-element.49.value.refs_2_.refs_1_), channel_id=1, source_target_pairs={{97,65},{99,67},{101,69},{103,71},{105,73},{107,75},{109,77},{111,... | collective-permute-start | bytes 1572872 | tf_op jit(solution)/shard_map/ppermute | solution.py:357
  11.6 0.7 collective-permute-start.6
  12.4 0.7 collective-permute-start.4
  13.1 1.3 %collective-permute-start.9 = (f32[256,512]{1,0:T(8,128)S(1)}, f32[256,512]{1,0:T(8,128)S(1)}, u32[]{:S(2)}, u32[]{:S(2)}) collective-permute-start(f32[256,512]{1,0:T(8,128)S(1)} %shard_map.67), channel_id=1, source_target_pairs={{96,128},{160,192},{256,288},{384,416},{97,129},{161,193},{257,289... | collective-permute-start | bytes 1572872 | tf_op jit(solution)/shard_map/ppermute | solution.py:354
  14.4 3.2 %collective-permute-done.5.refs_0_ = f32[256,512]{1,0:T(8,128)S(1)} collective-permute-done((f32[256,512]{1,0:T(8,128)S(1)}, f32[256,512]{1,0:T(8,128)S(1)}, u32[]{:S(2)}, u32[]{:S(2)}) %collective-permute-start.5) | collective-permute-done | bytes 524320 | tf_op jit(solution)/shard_map/ppermute | solution.py:357
  17.6 0.7 collective-permute-start.8
  18.4 0.7 collective-permute-start.7
  19.1 8.1 %collective-permute-done.9.refs_5_.rest_0_ = f32[256,512]{1,0:T(8,128)S(1)} collective-permute-done((f32[256,512]{1,0:T(8,128)S(1)}, f32[256,512]{1,0:T(8,128)S(1)}, u32[]{:S(2)}, u32[]{:S(2)}) %collective-permute-start.9) | collective-permute-done | bytes 524320 | tf_op jit(solution)/shard_map/ppermute | solution.py:354
  27.2 1.1 shard_map.71
  28.3 1.3 %collective-permute-start.12 = (f32[256,512]{1,0:T(8,128)S(1)}, f32[256,512]{1,0:T(8,128)S(1)}, u32[]{:S(2)}, u32[]{:S(2)}) collective-permute-start(f32[256,512]{1,0:T(8,128)S(1)} %shard_map.71), channel_id=1, source_target_pairs={{192,224},{288,320},{416,448},{193,225},{289,321},{417,449},{194,2... | collective-permute-start | bytes 1572872 | tf_op jit(solution)/shard_map/ppermute | solution.py:354
  29.7 0.7 collective-permute-start.11
  30.4 0.7 collective-permute-start.10
  31.1 4.6 %collective-permute-done.12.refs_5_.rest_0_.refs_7_ = f32[256,512]{1,0:T(8,128)S(1)} collective-permute-done((f32[256,512]{1,0:T(8,128)S(1)}, f32[256,512]{1,0:T(8,128)S(1)}, u32[]{:S(2)}, u32[]{:S(2)}) %collective-permute-start.12) | collective-permute-done | bytes 524320 | tf_op jit(solution)/shard_map/ppermute | solution.py:354
  35.7 0.7 collective-permute-start.14
  36.4 0.8 shard_map.70
  37.2 0.7 collective-permute-start.13
  38.0 0.7 collective-permute-start.15
  38.7 0.7 collective-permute-start.16
  39.5 1.3 %collective-permute-start.17 = (f32[256,512]{1,0:T(8,128)S(1)}, f32[256,512]{1,0:T(8,128)S(1)}, u32[]{:S(2)}, u32[]{:S(2)}) collective-permute-start(f32[256,512]{1,0:T(8,128)S(1)} %get-tuple-element.74), channel_id=1, source_target_pairs={{256,288},{384,416},{448,480},{257,289},{385,417},{449,481},{258,2... | collective-permute-start | bytes 1572872 | tf_op jit(solution)/shard_map/ppermute | solution.py:352
  40.8 45.0 %collective-permute-done.17.refs_0_ = f32[256,512]{1,0:T(8,128)S(1)} collective-permute-done((f32[256,512]{1,0:T(8,128)S(1)}, f32[256,512]{1,0:T(8,128)S(1)}, u32[]{:S(2)}, u32[]{:S(2)}) %collective-permute-start.17) | collective-permute-done | bytes 524320 | tf_op jit(solution)/shard_map/ppermute | solution.py:352
  85.8 0.7 collective-permute-start.18
  86.5 1.8 %shard_map.79 = f32[32,2,8,512]{3,2,1,0:T(8,128)S(1)} custom-call(f32[1,2]{1,0:T(1,128)S(1)} %copy-done.2, bf16[2,256,512]{2,1,0:T(8,128)(2,1)S(1)} %bitcast.4, bf16[512,512]{1,0:T(8,128)(2,1)S(1)} %get-tuple-element.41.form_first, f32[256,512]{1,0:T(8,128)S(1)} %get-tuple-element.42.first, f32[256,512]{1,0:T(8,128)S(1)} %get-tuple-element.43.value.refs_2_.local.refs_1_, ...), custom_call_target="tpu_custom_call" | custom-call | flops 1342177280 | bytes 4194304 | tf_op jit(solution)/shard_map/pallas_call | solution.py:417
  88.3 37.6 %all_to_all.5.blocks = f32[32,2,8,512]{3,2,1,0:T(8,128)S(1)} all-to-all(f32[32,2,8,512]{3,2,1,0:T(8,128)S(1)} %shard_map.79), channel_id=1, replica_groups=mesh['slab'=16,'energy'=32] {'energy'}, dimensions={0} | all-to-all | bytes 2097152 | tf_op jit(solution)/shard_map/all_to_all | solution.py:424
  125.9 1.7 %shard_map.80 = (f32[2,8,512]{2,1,0:T(8,128)}, f32[32,2,8,512]{3,2,1,0:T(8,128)}) custom-call(f32[32,128]{1,0:T(8,128)S(1)} %broadcast_in_dim.2.weights, f32[32,2,8,512]{3,2,1,0:T(8,128)S(1)} %all_to_all.5.blocks), custom_call_target="tpu_custom_call" | custom-call | tf_op jit(solution)/shard_map/pallas_call | solution.py:425
  (40 shorter events, 0.9 us)
Async XLA Ops:
  0.6 5.7 %collective-permute-start.1 = (f32[1,2]{1,0:T(1,128)}, f32[1,2]{1,0:T(1,128)S(1)}, u32[]{:S(2)}, u32[]{:S(2)}) collective-permute-start(f32[1,2]{1,0:T(1,128)} %coupling.5), channel_id=1, source_target_pairs={{0,32},{2,34},{4,36},{6,38},{8,40},{10,42},{12,44},{14,46},{16,48}... | collective-permute-start | bytes 32 | tf_op jit(solution)/shard_map/ppermute | solution.py:347
  1.3 0.7 copy-start.2
  2.0 1.0 copy-start
  3.0 1.0 copy-start.3
  5.5 2.3 %copy-start.1 = (bf16[1,2,256,512]{3,2,1,0:T(8,128)(2,1)S(1)}, bf16[1,2,256,512]{3,2,1,0:T(8,128)(2,1)}, u32[]{:S(2)}) copy-start(bf16[1,2,256,512]{3,2,1,0:T(8,128)(2,1)} %param.4) | copy-start | bytes 1572868
  5.5 6.8 %collective-permute-start = (f32[256,512]{1,0:T(8,128)S(1)}, f32[256,512]{1,0:T(8,128)S(1)}, u32[]{:S(2)}, u32[]{:S(2)}) collective-permute-start(f32[256,512]{1,0:T(8,128)S(1)} %get-tuple-element.43.value.refs_2_.local.refs_1_), channel_id=1, source_target_pairs={{1,33},{3,35},{5,37},{7,39},{9,41},{11,43},{13,45},{15,47},{17,49}... | collective-permute-start | bytes 1572872 | tf_op jit(solution)/shard_map/ppermute | solution.py:345
  6.4 0.7 collective-permute-start.2
  7.1 5.2 %collective-permute-start.3 = (f32[256,512]{1,0:T(8,128)S(1)}, f32[256,512]{1,0:T(8,128)S(1)}, u32[]{:S(2)}, u32[]{:S(2)}) collective-permute-start(f32[256,512]{1,0:T(8,128)S(1)} %shard_map.61), channel_id=1, source_target_pairs={{0,32},{2,34},{4,36},{6,38},{8,40},{10,42},{12,44},{14,46},{16,48}... | collective-permute-start | bytes 1572872 | tf_op jit(solution)/shard_map/ppermute | solution.py:350
  8.3 9.4 %collective-permute-start.5 = (f32[256,512]{1,0:T(8,128)S(1)}, f32[256,512]{1,0:T(8,128)S(1)}, u32[]{:S(2)}, u32[]{:S(2)}) collective-permute-start(f32[256,512]{1,0:T(8,128)S(1)} %get-tuple-element.49.value.refs_2_.refs_1_), channel_id=1, source_target_pairs={{97,65},{99,67},{101,69},{103,71},{105,73},{107,75},{109,77},{111,... | collective-permute-start | bytes 1572872 | tf_op jit(solution)/shard_map/ppermute | solution.py:357
  11.6 6.1 %collective-permute-start.6 = (f32[256,512]{1,0:T(8,128)S(1)}, f32[256,512]{1,0:T(8,128)S(1)}, u32[]{:S(2)}, u32[]{:S(2)}) collective-permute-start(f32[256,512]{1,0:T(8,128)S(1)} %shard_map.63), channel_id=1, source_target_pairs={{96,64},{98,66},{100,68},{102,70},{104,72},{106,74},{108,76},{110,... | collective-permute-start | bytes 1572872 | tf_op jit(solution)/shard_map/ppermute | solution.py:359
  12.4 6.0 %collective-permute-start.4 = (f32[256,512]{1,0:T(8,128)S(1)}, f32[256,512]{1,0:T(8,128)S(1)}, u32[]{:S(2)}, u32[]{:S(2)}) collective-permute-start(f32[256,512]{1,0:T(8,128)S(1)} %get-tuple-element.48), channel_id=1, source_target_pairs={{32,64},{33,65},{34,66},{35,67},{36,68},{37,69},{38,70},{39,71},{4... | collective-permute-start | bytes 1572872 | tf_op jit(solution)/shard_map/ppermute | solution.py:352
  13.1 14.1 %collective-permute-start.9 = (f32[256,512]{1,0:T(8,128)S(1)}, f32[256,512]{1,0:T(8,128)S(1)}, u32[]{:S(2)}, u32[]{:S(2)}) collective-permute-start(f32[256,512]{1,0:T(8,128)S(1)} %shard_map.67), channel_id=1, source_target_pairs={{96,128},{160,192},{256,288},{384,416},{97,129},{161,193},{257,289... | collective-permute-start | bytes 1572872 | tf_op jit(solution)/shard_map/ppermute | solution.py:354
  17.6 12.0 %collective-permute-start.8 = (f32[256,512]{1,0:T(8,128)S(1)}, f32[256,512]{1,0:T(8,128)S(1)}, u32[]{:S(2)}, u32[]{:S(2)}) collective-permute-start(f32[256,512]{1,0:T(8,128)S(1)} %get-tuple-element.56), channel_id=1, source_target_pairs={{160,128},{288,256},{384,352},{161,129},{289,257},{385,353},{162,1... | collective-permute-start | bytes 1572872 | tf_op jit(solution)/shard_map/ppermute | solution.py:361
  18.4 12.0 %collective-permute-start.7 = (f32[256,512]{1,0:T(8,128)S(1)}, f32[256,512]{1,0:T(8,128)S(1)}, u32[]{:S(2)}, u32[]{:S(2)}) collective-permute-start(f32[256,512]{1,0:T(8,128)S(1)} %get-tuple-element.55), channel_id=1, source_target_pairs={{64,128},{65,129},{66,130},{67,131},{68,132},{69,133},{70,134},{71... | collective-permute-start | bytes 1572872 | tf_op jit(solution)/shard_map/ppermute | solution.py:352
  28.3 7.4 %collective-permute-start.12 = (f32[256,512]{1,0:T(8,128)S(1)}, f32[256,512]{1,0:T(8,128)S(1)}, u32[]{:S(2)}, u32[]{:S(2)}) collective-permute-start(f32[256,512]{1,0:T(8,128)S(1)} %shard_map.71), channel_id=1, source_target_pairs={{192,224},{288,320},{416,448},{193,225},{289,321},{417,449},{194,2... | collective-permute-start | bytes 1572872 | tf_op jit(solution)/shard_map/ppermute | solution.py:354
  29.7 6.7 %collective-permute-start.11 = (f32[256,512]{1,0:T(8,128)S(1)}, f32[256,512]{1,0:T(8,128)S(1)}, u32[]{:S(2)}, u32[]{:S(2)}) collective-permute-start(f32[256,512]{1,0:T(8,128)S(1)} %get-tuple-element.63), channel_id=1, source_target_pairs={{256,224},{257,225},{258,226},{259,227},{260,228},{261,229},{262,2... | collective-permute-start | bytes 1572872 | tf_op jit(solution)/shard_map/ppermute | solution.py:361
  30.4 6.8 %collective-permute-start.10 = (f32[256,512]{1,0:T(8,128)S(1)}, f32[256,512]{1,0:T(8,128)S(1)}, u32[]{:S(2)}, u32[]{:S(2)}) collective-permute-start(f32[256,512]{1,0:T(8,128)S(1)} %get-tuple-element.62), channel_id=1, source_target_pairs={{64,96},{128,224},{65,97},{129,225},{66,98},{130,226},{67,99},{131... | collective-permute-start | bytes 1572872 | tf_op jit(solution)/shard_map/ppermute | solution.py:352
  35.7 2.2 %collective-permute-start.14 = (f32[256,512]{1,0:T(8,128)S(1)}, f32[256,512]{1,0:T(8,128)S(1)}, u32[]{:S(2)}, u32[]{:S(2)}) collective-permute-start(f32[256,512]{1,0:T(8,128)S(1)} %shard_map.74), channel_id=1, source_target_pairs={{320,352},{321,353},{322,354},{323,355},{324,356},{325,357},{326,3... | collective-permute-start | bytes 1572872 | tf_op jit(solution)/shard_map/ppermute | solution.py:354
  37.2 0.7 collective-permute-start.13
  38.0 1.4 %collective-permute-start.15 = (f32[256,512]{1,0:T(8,128)S(1)}, f32[256,512]{1,0:T(8,128)S(1)}, u32[]{:S(2)}, u32[]{:S(2)}) collective-permute-start(f32[256,512]{1,0:T(8,128)S(1)} %get-tuple-element.71), channel_id=1, source_target_pairs={{160,192},{224,256},{352,448},{161,193},{225,257},{353,449},{162,1... | collective-permute-start | bytes 1572872 | tf_op jit(solution)/shard_map/ppermute | solution.py:352
  38.7 0.7 collective-permute-start.16
  39.5 46.3 %collective-permute-start.17 = (f32[256,512]{1,0:T(8,128)S(1)}, f32[256,512]{1,0:T(8,128)S(1)}, u32[]{:S(2)}, u32[]{:S(2)}) collective-permute-start(f32[256,512]{1,0:T(8,128)S(1)} %get-tuple-element.74), channel_id=1, source_target_pairs={{256,288},{384,416},{448,480},{257,289},{385,417},{449,481},{258,2... | collective-permute-start | bytes 1572872 | tf_op jit(solution)/shard_map/ppermute | solution.py:352
  85.8 0.7 collective-permute-start.18
  88.2 37.6 %copy-start.4 = (f32[32]{0:T(128)S(1)}, f32[32]{0:T(128)}, u32[]{:S(2)}) copy-start(f32[32]{0:T(128)} %param.7) | copy-start | bytes 388

commit v8 on v7

--- a/solution.py
+++ b/solution.py
@@ -212,13 +212,15 @@
     rows = out.shape[2]
     lead = coupling[:, 0:1]
     value = state[...]
-    block = first[...] + (lead * lead) * right_narrow(
-        product_narrow(green[0], value), form_first[...]
-    )
+    half = value.shape[0]
+    part_high, part_low = split(value)
+    by_high = dot(jnp.concatenate([green[0], high[...], low[...]], axis=0), expanded(part_high))
+    by_low = dot(jnp.concatenate([green[0], high[...]], axis=0), expanded(part_low))
+    left_first = by_high[:half] + by_low[:half]
+    left_joint = by_high[half : 2 * half] + by_high[2 * half :] + by_low[half:]
+    block = first[...] + (lead * lead) * right_narrow(left_first, form_first[...])
     out[:, 0] = block.reshape(-1, rows, block.shape[-1])
-    block = local[...] + right_wide(
-        product_wide(high[...], low[...], value), form_high[...], form_low[...]
-    )
+    block = local[...] + right_wide(left_joint, form_high[...], form_low[...])
     out[:, 1] = block.reshape(-1, rows, block.shape[-1])
 
 

time: 128 us -> 128 us (level)
  no operation moved by 1% of the time
where the time goes in v8:
time: 128 us
  waiting for transfers between devices  60.9 us (48%)
  blocking collectives  37.6 us (29%)
  starting transfers between devices  17.6 us (14%)
  Pallas kernels  7.37 us (6%)
  local copies, waits for them, and re-layouts  2.81 us (2%)
    ppermute x7, waiting for transfers between devices, per_device(): front = lax.ppermute(outgoing, 'slab', sweep[step])  45 us
    all_to_all x1, blocking collectives, per_device(): lax.all_to_all(blocks, 'energy', split_axis=0, concat_axis=0, tiled=True)  37.6 us
    ppermute x3, waiting for transfers between devices, per_device(): composites[step] = lax.ppermute(part, 'slab', chains[step])  12.7 us
    ppermute x7, starting transfers between devices, per_device(): front = lax.ppermute(outgoing, 'slab', sweep[step])  5.45 us
    ppermute x3, starting transfers between devices, per_device(): composites[step] = lax.ppermute(part, 'slab', chains[step])  3.3 us
    ppermute x1, starting transfers between devices, per_device(): lax.ppermute(product, ('slab', 'energy'), of_cores(pairs, levels, 1))  3.26 us
    ppermute x1, waiting for transfers between devices, per_device(): lax.ppermute(product, ('slab', 'energy'), of_cores(pairs, levels, 1))  3.24 us
    unnamed x10, local copies, waits for them, and re-layouts  2.74 us
  transfers between devices with their start and end apart: 19, of which 4 were waited for; matrix products, arithmetic and copies ran while one was open for 0% of the time, Pallas kernels for 3%

profile of v8, /device:TPU:417, one launch (start us, length us, event | category | flops | bytes accessed | tf_op | source)
XLA Modules:
  0.0 127.5 jit_solution(15303395118223948892)
XLA Ops:
  0.6 0.7 collective-permute-start.1
  1.3 0.6 copy-done.2
  2.0 1.0 copy-done
  3.0 1.0 copy-done.3
  4.0 1.5 %shard_map.59 = (f32[256,512]{1,0:T(8,128)S(1)}, f32[256,512]{1,0:T(8,128)S(1)}, bf16[512,512]{1,0:T(8,128)(2,1)S(1)}) custom-call(f32[1,2]{1,0:T(1,128)S(1)} %copy-done.2, bf16[2,256,512]{2,1,0:T(8,128)(2,1)S(1)} %bitcast.2, bf16[2,256,512]{2,1,0:T(8,128)(2,1)S(1)} %bitcast.5), custom_call_target="tpu_custom_call" | custom-call | flops 1073741824 | bytes 4194304 | tf_op jit(solution)/shard_map/pallas_call | solution.py:329
  5.5 0.8 collective-permute-start
  6.4 0.7 collective-permute-start.2
  7.1 0.7 collective-permute-start.3
  8.3 3.3 %collective-permute-start.5 = (f32[256,512]{1,0:T(8,128)S(1)}, f32[256,512]{1,0:T(8,128)S(1)}, u32[]{:S(2)}, u32[]{:S(2)}) collective-permute-start(f32[256,512]{1,0:T(8,128)S(1)} %get-tuple-element.49.value.refs_2_.refs_1_), channel_id=1, source_target_pairs={{97,65},{99,67},{101,69},{103,71},{105,73},{107,75},{109,77},{111,... | collective-permute-start | bytes 1572872 | tf_op jit(solution)/shard_map/ppermute | solution.py:359
  11.6 0.7 collective-permute-start.6
  12.4 0.7 collective-permute-start.4
  13.1 1.3 %collective-permute-start.9 = (f32[256,512]{1,0:T(8,128)S(1)}, f32[256,512]{1,0:T(8,128)S(1)}, u32[]{:S(2)}, u32[]{:S(2)}) collective-permute-start(f32[256,512]{1,0:T(8,128)S(1)} %shard_map.67), channel_id=1, source_target_pairs={{96,128},{160,192},{256,288},{384,416},{97,129},{161,193},{257,289... | collective-permute-start | bytes 1572872 | tf_op jit(solution)/shard_map/ppermute | solution.py:356
  14.4 3.2 %collective-permute-done.5.refs_0_ = f32[256,512]{1,0:T(8,128)S(1)} collective-permute-done((f32[256,512]{1,0:T(8,128)S(1)}, f32[256,512]{1,0:T(8,128)S(1)}, u32[]{:S(2)}, u32[]{:S(2)}) %collective-permute-start.5) | collective-permute-done | bytes 524320 | tf_op jit(solution)/shard_map/ppermute | solution.py:359
  17.6 0.7 collective-permute-start.8
  18.4 0.7 collective-permute-start.7
  19.1 8.1 %collective-permute-done.9.refs_5_.rest_0_ = f32[256,512]{1,0:T(8,128)S(1)} collective-permute-done((f32[256,512]{1,0:T(8,128)S(1)}, f32[256,512]{1,0:T(8,128)S(1)}, u32[]{:S(2)}, u32[]{:S(2)}) %collective-permute-start.9) | collective-permute-done | bytes 524320 | tf_op jit(solution)/shard_map/ppermute | solution.py:356
  27.2 1.1 shard_map.71
  28.3 1.3 %collective-permute-start.12 = (f32[256,512]{1,0:T(8,128)S(1)}, f32[256,512]{1,0:T(8,128)S(1)}, u32[]{:S(2)}, u32[]{:S(2)}) collective-permute-start(f32[256,512]{1,0:T(8,128)S(1)} %shard_map.71), channel_id=1, source_target_pairs={{192,224},{288,320},{416,448},{193,225},{289,321},{417,449},{194,2... | collective-permute-start | bytes 1572872 | tf_op jit(solution)/shard_map/ppermute | solution.py:356
  29.7 0.7 collective-permute-start.11
  30.4 0.7 collective-permute-start.10
  31.1 4.6 %collective-permute-done.12.refs_5_.rest_0_.refs_7_ = f32[256,512]{1,0:T(8,128)S(1)} collective-permute-done((f32[256,512]{1,0:T(8,128)S(1)}, f32[256,512]{1,0:T(8,128)S(1)}, u32[]{:S(2)}, u32[]{:S(2)}) %collective-permute-start.12) | collective-permute-done | bytes 524320 | tf_op jit(solution)/shard_map/ppermute | solution.py:356
  35.7 0.7 collective-permute-start.14
  36.4 0.8 shard_map.70
  37.2 0.7 collective-permute-start.13
  38.0 0.7 collective-permute-start.15
  38.7 0.7 collective-permute-start.16
  39.5 1.3 %collective-permute-start.17 = (f32[256,512]{1,0:T(8,128)S(1)}, f32[256,512]{1,0:T(8,128)S(1)}, u32[]{:S(2)}, u32[]{:S(2)}) collective-permute-start(f32[256,512]{1,0:T(8,128)S(1)} %get-tuple-element.74), channel_id=1, source_target_pairs={{256,288},{384,416},{448,480},{257,289},{385,417},{449,481},{258,2... | collective-permute-start | bytes 1572872 | tf_op jit(solution)/shard_map/ppermute | solution.py:354
  40.8 45.0 %collective-permute-done.17.refs_0_ = f32[256,512]{1,0:T(8,128)S(1)} collective-permute-done((f32[256,512]{1,0:T(8,128)S(1)}, f32[256,512]{1,0:T(8,128)S(1)}, u32[]{:S(2)}, u32[]{:S(2)}) %collective-permute-start.17) | collective-permute-done | bytes 524320 | tf_op jit(solution)/shard_map/ppermute | solution.py:354
  85.8 0.7 collective-permute-start.18
  86.5 1.6 %shard_map.79 = f32[32,2,8,512]{3,2,1,0:T(8,128)S(1)} custom-call(f32[1,2]{1,0:T(1,128)S(1)} %copy-done.2, bf16[2,256,512]{2,1,0:T(8,128)(2,1)S(1)} %bitcast.4, bf16[512,512]{1,0:T(8,128)(2,1)S(1)} %get-tuple-element.41.form_first, f32[256,512]{1,0:T(8,128)S(1)} %get-tuple-element.42.first, f32[256,512]{1,0:T(8,128)S(1)} %get-tuple-element.43.value.refs_2_.local.refs_1_, ...), custom_call_target="tpu_custom_call" | custom-call | flops 1342177280 | bytes 4194304 | tf_op jit(solution)/shard_map/pallas_call | solution.py:419
  88.1 37.6 %all_to_all.5.blocks = f32[32,2,8,512]{3,2,1,0:T(8,128)S(1)} all-to-all(f32[32,2,8,512]{3,2,1,0:T(8,128)S(1)} %shard_map.79), channel_id=1, replica_groups=mesh['slab'=16,'energy'=32] {'energy'}, dimensions={0} | all-to-all | bytes 2097152 | tf_op jit(solution)/shard_map/all_to_all | solution.py:426
  125.7 1.7 %shard_map.80 = (f32[2,8,512]{2,1,0:T(8,128)}, f32[32,2,8,512]{3,2,1,0:T(8,128)}) custom-call(f32[32,128]{1,0:T(8,128)S(1)} %broadcast_in_dim.2.weights, f32[32,2,8,512]{3,2,1,0:T(8,128)S(1)} %all_to_all.5.blocks), custom_call_target="tpu_custom_call" | custom-call | tf_op jit(solution)/shard_map/pallas_call | solution.py:427
  (40 shorter events, 0.9 us)
Async XLA Ops:
  0.6 5.7 %collective-permute-start.1 = (f32[1,2]{1,0:T(1,128)}, f32[1,2]{1,0:T(1,128)S(1)}, u32[]{:S(2)}, u32[]{:S(2)}) collective-permute-start(f32[1,2]{1,0:T(1,128)} %coupling.5), channel_id=1, source_target_pairs={{0,32},{2,34},{4,36},{6,38},{8,40},{10,42},{12,44},{14,46},{16,48}... | collective-permute-start | bytes 32 | tf_op jit(solution)/shard_map/ppermute | solution.py:349
  1.3 0.7 copy-start.2
  2.0 1.0 copy-start
  3.0 1.0 copy-start.3
  5.5 2.3 %copy-start.1 = (bf16[1,2,256,512]{3,2,1,0:T(8,128)(2,1)S(1)}, bf16[1,2,256,512]{3,2,1,0:T(8,128)(2,1)}, u32[]{:S(2)}) copy-start(bf16[1,2,256,512]{3,2,1,0:T(8,128)(2,1)} %param.4) | copy-start | bytes 1572868
  5.5 6.8 %collective-permute-start = (f32[256,512]{1,0:T(8,128)S(1)}, f32[256,512]{1,0:T(8,128)S(1)}, u32[]{:S(2)}, u32[]{:S(2)}) collective-permute-start(f32[256,512]{1,0:T(8,128)S(1)} %get-tuple-element.43.value.refs_2_.local.refs_1_), channel_id=1, source_target_pairs={{1,33},{3,35},{5,37},{7,39},{9,41},{11,43},{13,45},{15,47},{17,49}... | collective-permute-start | bytes 1572872 | tf_op jit(solution)/shard_map/ppermute | solution.py:347
  6.4 0.7 collective-permute-start.2
  7.1 5.2 %collective-permute-start.3 = (f32[256,512]{1,0:T(8,128)S(1)}, f32[256,512]{1,0:T(8,128)S(1)}, u32[]{:S(2)}, u32[]{:S(2)}) collective-permute-start(f32[256,512]{1,0:T(8,128)S(1)} %shard_map.61), channel_id=1, source_target_pairs={{0,32},{2,34},{4,36},{6,38},{8,40},{10,42},{12,44},{14,46},{16,48}... | collective-permute-start | bytes 1572872 | tf_op jit(solution)/shard_map/ppermute | solution.py:352
  8.3 9.4 %collective-permute-start.5 = (f32[256,512]{1,0:T(8,128)S(1)}, f32[256,512]{1,0:T(8,128)S(1)}, u32[]{:S(2)}, u32[]{:S(2)}) collective-permute-start(f32[256,512]{1,0:T(8,128)S(1)} %get-tuple-element.49.value.refs_2_.refs_1_), channel_id=1, source_target_pairs={{97,65},{99,67},{101,69},{103,71},{105,73},{107,75},{109,77},{111,... | collective-permute-start | bytes 1572872 | tf_op jit(solution)/shard_map/ppermute | solution.py:359
  11.6 6.1 %collective-permute-start.6 = (f32[256,512]{1,0:T(8,128)S(1)}, f32[256,512]{1,0:T(8,128)S(1)}, u32[]{:S(2)}, u32[]{:S(2)}) collective-permute-start(f32[256,512]{1,0:T(8,128)S(1)} %shard_map.63), channel_id=1, source_target_pairs={{96,64},{98,66},{100,68},{102,70},{104,72},{106,74},{108,76},{110,... | collective-permute-start | bytes 1572872 | tf_op jit(solution)/shard_map/ppermute | solution.py:361
  12.4 6.0 %collective-permute-start.4 = (f32[256,512]{1,0:T(8,128)S(1)}, f32[256,512]{1,0:T(8,128)S(1)}, u32[]{:S(2)}, u32[]{:S(2)}) collective-permute-start(f32[256,512]{1,0:T(8,128)S(1)} %get-tuple-element.48), channel_id=1, source_target_pairs={{32,64},{33,65},{34,66},{35,67},{36,68},{37,69},{38,70},{39,71},{4... | collective-permute-start | bytes 1572872 | tf_op jit(solution)/shard_map/ppermute | solution.py:354
  13.1 14.1 %collective-permute-start.9 = (f32[256,512]{1,0:T(8,128)S(1)}, f32[256,512]{1,0:T(8,128)S(1)}, u32[]{:S(2)}, u32[]{:S(2)}) collective-permute-start(f32[256,512]{1,0:T(8,128)S(1)} %shard_map.67), channel_id=1, source_target_pairs={{96,128},{160,192},{256,288},{384,416},{97,129},{161,193},{257,289... | collective-permute-start | bytes 1572872 | tf_op jit(solution)/shard_map/ppermute | solution.py:356
  17.6 12.0 %collective-permute-start.8 = (f32[256,512]{1,0:T(8,128)S(1)}, f32[256,512]{1,0:T(8,128)S(1)}, u32[]{:S(2)}, u32[]{:S(2)}) collective-permute-start(f32[256,512]{1,0:T(8,128)S(1)} %get-tuple-element.56), channel_id=1, source_target_pairs={{160,128},{288,256},{384,352},{161,129},{289,257},{385,353},{162,1... | collective-permute-start | bytes 1572872 | tf_op jit(solution)/shard_map/ppermute | solution.py:363
  18.4 12.0 %collective-permute-start.7 = (f32[256,512]{1,0:T(8,128)S(1)}, f32[256,512]{1,0:T(8,128)S(1)}, u32[]{:S(2)}, u32[]{:S(2)}) collective-permute-start(f32[256,512]{1,0:T(8,128)S(1)} %get-tuple-element.55), channel_id=1, source_target_pairs={{64,128},{65,129},{66,130},{67,131},{68,132},{69,133},{70,134},{71... | collective-permute-start | bytes 1572872 | tf_op jit(solution)/shard_map/ppermute | solution.py:354
  28.3 7.4 %collective-permute-start.12 = (f32[256,512]{1,0:T(8,128)S(1)}, f32[256,512]{1,0:T(8,128)S(1)}, u32[]{:S(2)}, u32[]{:S(2)}) collective-permute-start(f32[256,512]{1,0:T(8,128)S(1)} %shard_map.71), channel_id=1, source_target_pairs={{192,224},{288,320},{416,448},{193,225},{289,321},{417,449},{194,2... | collective-permute-start | bytes 1572872 | tf_op jit(solution)/shard_map/ppermute | solution.py:356
  29.7 6.7 %collective-permute-start.11 = (f32[256,512]{1,0:T(8,128)S(1)}, f32[256,512]{1,0:T(8,128)S(1)}, u32[]{:S(2)}, u32[]{:S(2)}) collective-permute-start(f32[256,512]{1,0:T(8,128)S(1)} %get-tuple-element.63), channel_id=1, source_target_pairs={{256,224},{257,225},{258,226},{259,227},{260,228},{261,229},{262,2... | collective-permute-start | bytes 1572872 | tf_op jit(solution)/shard_map/ppermute | solution.py:363
  30.4 6.8 %collective-permute-start.10 = (f32[256,512]{1,0:T(8,128)S(1)}, f32[256,512]{1,0:T(8,128)S(1)}, u32[]{:S(2)}, u32[]{:S(2)}) collective-permute-start(f32[256,512]{1,0:T(8,128)S(1)} %get-tuple-element.62), channel_id=1, source_target_pairs={{64,96},{128,224},{65,97},{129,225},{66,98},{130,226},{67,99},{131... | collective-permute-start | bytes 1572872 | tf_op jit(solution)/shard_map/ppermute | solution.py:354
  35.7 2.2 %collective-permute-start.14 = (f32[256,512]{1,0:T(8,128)S(1)}, f32[256,512]{1,0:T(8,128)S(1)}, u32[]{:S(2)}, u32[]{:S(2)}) collective-permute-start(f32[256,512]{1,0:T(8,128)S(1)} %shard_map.74), channel_id=1, source_target_pairs={{320,352},{321,353},{322,354},{323,355},{324,356},{325,357},{326,3... | collective-permute-start | bytes 1572872 | tf_op jit(solution)/shard_map/ppermute | solution.py:356
  37.2 0.7 collective-permute-start.13
  38.0 1.4 %collective-permute-start.15 = (f32[256,512]{1,0:T(8,128)S(1)}, f32[256,512]{1,0:T(8,128)S(1)}, u32[]{:S(2)}, u32[]{:S(2)}) collective-permute-start(f32[256,512]{1,0:T(8,128)S(1)} %get-tuple-element.71), channel_id=1, source_target_pairs={{160,192},{224,256},{352,448},{161,193},{225,257},{353,449},{162,1... | collective-permute-start | bytes 1572872 | tf_op jit(solution)/shard_map/ppermute | solution.py:354
  38.7 0.7 collective-permute-start.16
  39.5 46.3 %collective-permute-start.17 = (f32[256,512]{1,0:T(8,128)S(1)}, f32[256,512]{1,0:T(8,128)S(1)}, u32[]{:S(2)}, u32[]{:S(2)}) collective-permute-start(f32[256,512]{1,0:T(8,128)S(1)} %get-tuple-element.74), channel_id=1, source_target_pairs={{256,288},{384,416},{448,480},{257,289},{385,417},{449,481},{258,2... | collective-permute-start | bytes 1572872 | tf_op jit(solution)/shard_map/ppermute | solution.py:354
  85.8 0.7 collective-permute-start.18
  88.1 37.6 %copy-start.4 = (f32[32]{0:T(128)S(1)}, f32[32]{0:T(128)}, u32[]{:S(2)}) copy-start(f32[32]{0:T(128)} %param.7) | copy-start | bytes 388
